TPU v7x, 32 devices: a whole 2x2x4 slice. The times are simulated.
32 devices in a mesh: dp: 4 (over x, core), chan: 8 (over z, y).
Axes of the slice: x: 2, y: 2, z: 4, core: 2. Of those that a mesh axis runs over, the one named last changes fastest.
Arguments:
- canvas: float32 [8, 3, 64, 64], P('dp'), may hold values from -6 to 6
- crop_boxes: int32 [8, 3], P('dp'), may hold values from 0 to 48, as said below
- time_steps: int32 [8], P('dp'), may hold values from 0 to 999
- noise_field: float32 [3, 8, 256], P(None, 'dp'), may hold values from -6 to 6
- step_count: int32 [1], replicated, may hold values from 1 to 20
- w_in: float32 [256, 27], P('chan'), may hold values from -1.25 to 1.25
- m_in: float32 [256, 27], P('chan'), may hold values from -0.03125 to 0.03125
- v_in: float32 [256, 27], P('chan'), may hold values from 2.4414062e-06 to 9.765625e-06
- conv_w: float32 [4, 256, 2304], P(None, 'chan'), may hold values from -0.125 to 0.125
- conv_m: float32 [4, 256, 2304], P(None, 'chan'), may hold values from -0.03125 to 0.03125
- conv_v: float32 [4, 256, 2304], P(None, 'chan'), may hold values from 2.4414062e-06 to 9.765625e-06
- temb_w: float32 [2, 256, 512], P(None, 'chan'), may hold values from -0.25 to 0.25
- temb_m: float32 [2, 256, 512], P(None, 'chan'), may hold values from -0.03125 to 0.03125
- temb_v: float32 [2, 256, 512], P(None, 'chan'), may hold values from 2.4414062e-06 to 9.765625e-06
- attn_w: float32 [4, 256, 256], P(None, 'chan'), may hold values from -0.5 to 0.5
- attn_m: float32 [4, 256, 256], P(None, 'chan'), may hold values from -0.03125 to 0.03125
- attn_v: float32 [4, 256, 256], P(None, 'chan'), may hold values from 2.4414062e-06 to 9.765625e-06
- out_w: float32 [3, 2304], replicated, may hold values from -0.125 to 0.125
- out_m: float32 [3, 2304], replicated, may hold values from -0.03125 to 0.03125
- out_v: float32 [3, 2304], replicated, may hold values from 2.4414062e-06 to 9.765625e-06
- vectors: float32 [22, 256], P(None, 'chan')
- vec_m: float32 [22, 256], P(None, 'chan'), may hold values from -0.03125 to 0.03125
- vec_v: float32 [22, 256], P(None, 'chan'), may hold values from 2.4414062e-06 to 9.765625e-06
Outputs:
- loss: float32 [], replicated
- matrix_norms: float32 [12, 2], replicated
- w_in_new: float32 [256, 27], P('chan')
- m_in_new: float32 [256, 27], P('chan')
- v_in_new: float32 [256, 27], P('chan')
- conv_new: float32 [4, 256, 2304], P(None, 'chan')
- conv_m_new: float32 [4, 256, 2304], P(None, 'chan')
- conv_v_new: float32 [4, 256, 2304], P(None, 'chan')
- conv_low: bfloat16 [4, 256, 2304], P(None, 'chan')
- temb_new: float32 [2, 256, 512], P(None, 'chan')
- temb_m_new: float32 [2, 256, 512], P(None, 'chan')
- temb_v_new: float32 [2, 256, 512], P(None, 'chan')
- temb_low: bfloat16 [2, 256, 512], P(None, 'chan')
- attn_new: float32 [4, 256, 256], P(None, 'chan')
- attn_m_new: float32 [4, 256, 256], P(None, 'chan')
- attn_v_new: float32 [4, 256, 256], P(None, 'chan')
- attn_low: bfloat16 [4, 256, 256], P(None, 'chan')
- out_new: float32 [3, 2304], replicated
- out_m_new: float32 [3, 2304], replicated
- out_v_new: float32 [3, 2304], replicated
- vec_new: float32 [22, 256], P(None, 'chan')
- vec_m_new: float32 [22, 256], P(None, 'chan')
- vec_v_new: float32 [22, 256], P(None, 'chan')
- attn_grad_sum: float32 [4, 256, 256], P(None, 'chan')
Inputs may be any that keep to these rules, and one draw needn't show every extreme that they name: `crop_boxes`: row b holds the window's top row and left column, each from 0 to 48, and the side of the counted square, 4 + 12 * b // max(7, 1) plus 0 or 1, at most 16; the last image's side is 16, the first image's window is at row 48, column 0.
All inputs are finite; a program needn't handle non-finite values.
Results may differ from a plain program's by a relative error of at most 0.0092.
Values may be sent and summed in bfloat16 or wider, within the bound.
A program may use at most 192 MiB of HBM per device.

v0:
```python
import math

import jax
import jax.numpy as jnp
from jax import lax
from jax.sharding import PartitionSpec as P

TEMB = 512
HW = 16
GSIZE = 8


NORM_EPS = 1e-05
BETA_ONE = 0.9
BETA_TWO = 0.95
ADAM_EPS = 1e-06
DECAY = 0.01
RATE = 0.3
CONTRACT_ROWS = (((1,), (1,)), ((), ()))
CONTRACT_COLS = (((0,), (0,)), ((), ()))


def to_columns(field, images):
    field_depth = field.shape[0]
    square = field.reshape(field_depth, images, HW, HW)
    padded = jnp.pad(square, ((0, 0), (0, 0), (1, 1), (1, 1)))
    shifted = [
        padded[:, :, row_off : row_off + HW, col_off : col_off + HW]
        for row_off in range(3)
        for col_off in range(3)
    ]
    return jnp.stack(shifted, axis=1).reshape(field_depth * 9, images * HW * HW)


def from_columns(columns, images):
    zero_field = jnp.zeros((columns.shape[0] // 9, columns.shape[1]), jnp.float32)
    unused, pull_back = jax.vjp(lambda field: to_columns(field, images), zero_field)
    return pull_back(columns)[0]


def group_act(field, gain, shift):
    field_depth, rows_all = field.shape
    images = rows_all // (HW * HW)
    grouped = field.reshape(field_depth // GSIZE, GSIZE, images, HW * HW)
    centre = jnp.mean(grouped, axis=(1, 3), keepdims=True)
    spread = jnp.mean((grouped - centre) ** 2, axis=(1, 3), keepdims=True)
    scaled = ((grouped - centre) * lax.rsqrt(spread + NORM_EPS)).reshape(field_depth, rows_all)
    return jax.nn.silu(scaled * gain[:, None] + shift[:, None])


def prepare(canvas, crop_boxes, time_steps):
    images = canvas.shape[0]

    def crop_one(picture, box_row):
        return lax.dynamic_slice(picture, (jnp.int32(0), box_row[0], box_row[1]), (3, HW, HW))

    windows = jax.vmap(crop_one)(canvas, crop_boxes)
    clean = jnp.transpose(windows, (1, 0, 2, 3)).reshape(3, images * HW * HW)
    ladder = jnp.arange(HW, dtype=jnp.int32)
    inside = ladder[None, :] < crop_boxes[:, 2:3]
    mask_rows = (
        (inside[:, :, None] & inside[:, None, :]).astype(jnp.float32).reshape(images * HW * HW)
    )
    phase = (time_steps.astype(jnp.float32) / 1000.0 + 0.008) / 1.008
    alpha_bar = jnp.cos(phase * (math.pi / 2)) ** 2
    abar_rows = jnp.repeat(alpha_bar, HW * HW)
    frequency = jnp.exp(-math.log(10000.0) * jnp.arange(TEMB // 2, dtype=jnp.float32) / (TEMB // 2))
    angles = time_steps.astype(jnp.float32)[None, :] * frequency[:, None]
    embedding = jnp.concatenate([jnp.sin(angles), jnp.cos(angles)], axis=0)
    return (clean, mask_rows, abar_rows, embedding)


def per_image_add(field, shift):
    field_depth, rows_all = field.shape
    images = shift.shape[1]
    return (field.reshape(field_depth, images, HW * HW) + shift[:, :, None]).reshape(
        field_depth, rows_all
    )


def gather_act(value_low):
    return lax.all_gather(value_low, "chan", axis=0, tiled=True)


def linear_fwd(weight_low, gathered, images, kernel):
    columns = to_columns(gathered, images) if kernel == 3 else gathered
    return jnp.dot(weight_low, columns, preferred_element_type=jnp.float32)


def linear_back(weight_low, gathered, grad_low, images, kernel):
    columns = to_columns(gathered, images) if kernel == 3 else gathered
    weight_grad = lax.dot_general(
        grad_low, columns, CONTRACT_ROWS, preferred_element_type=jnp.float32
    )
    part_columns = lax.dot_general(
        weight_low, grad_low, CONTRACT_COLS, preferred_element_type=jnp.float32
    )
    input_grad = lax.psum_scatter(
        from_columns(part_columns, images) if kernel == 3 else part_columns,
        "chan",
        scatter_dimension=0,
        tiled=True,
    )
    return (weight_grad, input_grad)


def res_forward(hidden, block, conv_low, temb_low, vectors, temb_act, images):
    first_gath = gather_act(
        group_act(hidden, vectors[3 * block], vectors[6 + 3 * block]).astype(jnp.bfloat16)
    )
    middle = (
        linear_fwd(conv_low[2 * block], first_gath, images, 3) + vectors[13 + 2 * block][:, None]
    )
    shift = (
        jnp.dot(temb_low[block], temb_act, preferred_element_type=jnp.float32)
        + vectors[17 + block][:, None]
    )
    middle = per_image_add(middle, shift)
    second_gath = gather_act(
        group_act(middle, vectors[1 + 3 * block], vectors[7 + 3 * block]).astype(jnp.bfloat16)
    )
    branch = (
        linear_fwd(conv_low[2 * block + 1], second_gath, images, 3)
        + vectors[14 + 2 * block][:, None]
    )
    return ((hidden, first_gath, middle, second_gath), hidden + branch)


def res_backward(kept, grad_out, block, conv_low, vectors, temb_act, images, vec_grad):
    hidden, first_gath, middle, second_gath = kept
    local_rows = hidden.shape[0]
    conv_two, grad_second = linear_back(
        conv_low[2 * block + 1], second_gath, grad_out.astype(jnp.bfloat16), images, 3
    )
    unused, pull_second = jax.vjp(group_act, middle, vectors[1 + 3 * block], vectors[7 + 3 * block])
    grad_middle, gain_two, shift_two = pull_second(grad_second)
    conv_one, grad_first = linear_back(
        conv_low[2 * block], first_gath, grad_middle.astype(jnp.bfloat16), images, 3
    )
    grad_shift = jnp.sum(grad_middle.reshape(local_rows, images, HW * HW), axis=2)
    temb_grad = lax.dot_general(
        grad_shift.astype(jnp.bfloat16), temb_act, CONTRACT_ROWS, preferred_element_type=jnp.float32
    )
    unused, pull_first = jax.vjp(group_act, hidden, vectors[3 * block], vectors[6 + 3 * block])
    grad_hidden, gain_one, shift_one = pull_first(grad_first)
    vec_grad = vec_grad.at[3 * block].add(gain_one).at[1 + 3 * block].add(gain_two)
    vec_grad = vec_grad.at[6 + 3 * block].add(shift_one).at[7 + 3 * block].add(shift_two)
    vec_grad = (
        vec_grad.at[13 + 2 * block]
        .add(jnp.sum(grad_middle, axis=1))
        .at[14 + 2 * block]
        .add(jnp.sum(grad_out, axis=1))
    )
    vec_grad = vec_grad.at[17 + block].add(jnp.sum(grad_shift, axis=1))
    return (grad_out + grad_hidden, conv_one, conv_two, temb_grad, vec_grad)


def partial_scores(query, key_part, images):
    local_rows = query.shape[0]
    return jnp.einsum(
        "cbi,cbj->bij",
        query.reshape(local_rows, images, HW * HW),
        key_part.reshape(local_rows, images, HW * HW),
        preferred_element_type=jnp.float32,
    )


def attn_forward(hidden, attn_low, vectors, images, scale):
    local_rows = hidden.shape[0]
    gathered = gather_act(group_act(hidden, vectors[2], vectors[8]).astype(jnp.bfloat16))
    triple = linear_fwd(attn_low[:3].reshape(3 * local_rows, -1), gathered, images, 1)
    query = (triple[:local_rows] + vectors[19][:, None]).astype(jnp.bfloat16)
    key_part = triple[local_rows : 2 * local_rows].astype(jnp.bfloat16)
    value = (triple[2 * local_rows :] + vectors[20][:, None]).astype(jnp.bfloat16)
    scores = lax.psum(partial_scores(query, key_part, images), "chan") * scale
    probs = jax.nn.softmax(scores, axis=-1)
    mixed = jnp.einsum(
        "bij,cbj->cbi",
        probs.astype(jnp.bfloat16),
        value.reshape(local_rows, images, HW * HW),
        preferred_element_type=jnp.float32,
    )
    mixed_gath = gather_act(mixed.reshape(local_rows, images * HW * HW).astype(jnp.bfloat16))
    output = hidden + (linear_fwd(attn_low[3], mixed_gath, images, 1) + vectors[21][:, None])
    return ((hidden, gathered, query, key_part, value, None, mixed_gath), output)


def attn_backward(kept, grad_out, attn_low, vectors, images, scale, vec_grad):
    hidden, gathered, query, key_part, value, kept_probs, mixed_gath = kept
    local_rows = hidden.shape[0]
    proj_grad, grad_mixed = linear_back(
        attn_low[3], mixed_gath, grad_out.astype(jnp.bfloat16), images, 1
    )
    mixed_low = grad_mixed.astype(jnp.bfloat16).reshape(local_rows, images, HW * HW)
    value_cube = value.reshape(local_rows, images, HW * HW)
    probs_part = jnp.einsum(
        "cbi,cbj->bij", mixed_low, value_cube, preferred_element_type=jnp.float32
    )
    scores, grad_probs = lax.psum((partial_scores(query, key_part, images), probs_part), "chan")
    probs = jax.nn.softmax(scores * scale, axis=-1)
    grad_value = jnp.einsum(
        "bij,cbi->cbj", probs.astype(jnp.bfloat16), mixed_low, preferred_element_type=jnp.float32
    )
    grad_scores = probs * (grad_probs - jnp.sum(probs * grad_probs, axis=-1, keepdims=True))
    scores_low = grad_scores.astype(jnp.bfloat16)
    grad_query = scale * jnp.einsum(
        "bij,cbj->cbi",
        scores_low,
        key_part.reshape(local_rows, images, HW * HW),
        preferred_element_type=jnp.float32,
    )
    grad_key = scale * jnp.einsum(
        "bij,cbi->cbj",
        scores_low,
        query.reshape(local_rows, images, HW * HW),
        preferred_element_type=jnp.float32,
    )
    grad_triple = jnp.concatenate([grad_query, grad_key, grad_value], axis=0).reshape(
        3 * local_rows, images * HW * HW
    )
    qkv_grad, grad_normed = linear_back(
        attn_low[:3].reshape(3 * local_rows, -1),
        gathered,
        grad_triple.astype(jnp.bfloat16),
        images,
        1,
    )
    unused, pull_norm = jax.vjp(group_act, hidden, vectors[2], vectors[8])
    grad_hidden, gain_grad, shift_grad = pull_norm(grad_normed)
    vec_grad = vec_grad.at[2].add(gain_grad).at[8].add(shift_grad)
    vec_grad = vec_grad.at[19].add(jnp.sum(grad_triple[:local_rows], axis=1))
    vec_grad = vec_grad.at[20].add(jnp.sum(grad_triple[2 * local_rows :], axis=1))
    vec_grad = vec_grad.at[21].add(jnp.sum(grad_out, axis=1))
    attn_grad = jnp.concatenate([qkv_grad.reshape(3, local_rows, -1), proj_grad[None]], axis=0)
    return (grad_out + grad_hidden, attn_grad, vec_grad)


def adapt(grad, first, second, count_step):
    first_new = BETA_ONE * first + (1.0 - BETA_ONE) * grad
    second_new = BETA_TWO * second + (1.0 - BETA_TWO) * grad * grad
    direction = (
        first_new
        / (1.0 - BETA_ONE**count_step)
        / (jnp.sqrt(second_new / (1.0 - BETA_TWO**count_step)) + ADAM_EPS)
    )
    return (first_new, second_new, direction)


def square_sums(matrix_set):
    stacked = matrix_set.reshape((-1,) + matrix_set.shape[-2:])
    return jnp.sum(stacked * stacked, axis=(1, 2))


def apply_ratio(weight, update, ratio):
    stacked_w = weight.reshape((-1,) + weight.shape[-2:])
    stacked_u = update.reshape(stacked_w.shape)
    return (stacked_w - RATE * ratio[:, None, None] * stacked_u).reshape(weight.shape)


def per_device(
    canvas,
    crop_boxes,
    time_steps,
    noise_field,
    step_count,
    w_in,
    m_in,
    v_in,
    conv_w,
    conv_m,
    conv_v,
    temb_w,
    temb_m,
    temb_v,
    attn_w,
    attn_m,
    attn_v,
    out_w,
    out_m,
    out_v,
    vectors,
    vec_m,
    vec_v,
):
    images = canvas.shape[0]
    rows_all = images * HW * HW
    local_rows = conv_w.shape[1]
    scale = (conv_w.shape[2] // 9) ** (-0.5)
    clean, mask_rows, abar_rows, embedding = prepare(canvas, crop_boxes, time_steps)
    total_count = lax.psum(3.0 * jnp.sum(mask_rows), "dp")
    weight_squares = jnp.concatenate(
        [square_sums(w_in), square_sums(conv_w), square_sums(temb_w), square_sums(attn_w)]
    )
    noise_rows = noise_field.reshape(3, rows_all)
    noisy_low = (jnp.sqrt(abar_rows) * clean + jnp.sqrt(1.0 - abar_rows) * noise_rows).astype(
        jnp.bfloat16
    )
    temb_act = jax.nn.silu(embedding).astype(jnp.bfloat16)
    in_low = w_in.astype(jnp.bfloat16)
    conv_low = conv_w.astype(jnp.bfloat16)
    temb_low = temb_w.astype(jnp.bfloat16)
    attn_low = attn_w.astype(jnp.bfloat16)
    out_low = out_w.astype(jnp.bfloat16)
    input_columns = to_columns(noisy_low, images)
    hidden = (
        jnp.dot(in_low, input_columns, preferred_element_type=jnp.float32) + vectors[12][:, None]
    )
    first_kept, hidden = res_forward(hidden, 0, conv_low, temb_low, vectors, temb_act, images)
    attn_kept, hidden = attn_forward(hidden, attn_low, vectors, images, scale)
    second_kept, hidden = res_forward(hidden, 1, conv_low, temb_low, vectors, temb_act, images)
    final_gath = gather_act(group_act(hidden, vectors[5], vectors[11]).astype(jnp.bfloat16))
    final_columns = to_columns(final_gath, images)
    pred = jnp.dot(out_low, final_columns, preferred_element_type=jnp.float32)
    error = pred - noise_rows
    local_loss = jnp.sum(mask_rows * error * error) / total_count
    grad_pred = (2.0 * mask_rows * error / total_count).astype(jnp.bfloat16)
    out_grad = lax.dot_general(
        grad_pred, final_columns, CONTRACT_ROWS, preferred_element_type=jnp.float32
    )
    own_weight = lax.dynamic_slice_in_dim(
        out_low, lax.axis_index("chan") * local_rows * 9, local_rows * 9, 1
    )
    own_columns = lax.dot_general(
        own_weight, grad_pred, CONTRACT_COLS, preferred_element_type=jnp.float32
    )
    unused, pull_final = jax.vjp(group_act, hidden, vectors[5], vectors[11])
    grad_hidden, gain_final, shift_final = pull_final(from_columns(own_columns, images))
    vec_grad = jnp.zeros(vectors.shape, jnp.float32).at[5].add(gain_final).at[11].add(shift_final)
    grad_hidden, conv_two_a, conv_two_b, temb_two, vec_grad = res_backward(
        second_kept, grad_hidden, 1, conv_low, vectors, temb_act, images, vec_grad
    )
    grad_hidden, attn_grad, vec_grad = attn_backward(
        attn_kept, grad_hidden, attn_low, vectors, images, scale, vec_grad
    )
    grad_hidden, conv_one_a, conv_one_b, temb_one, vec_grad = res_backward(
        first_kept, grad_hidden, 0, conv_low, vectors, temb_act, images, vec_grad
    )
    in_grad = lax.dot_general(
        grad_hidden.astype(jnp.bfloat16),
        input_columns,
        CONTRACT_ROWS,
        preferred_element_type=jnp.float32,
    )
    vec_grad = vec_grad.at[12].add(jnp.sum(grad_hidden, axis=1))
    conv_grad = jnp.stack([conv_one_a, conv_one_b, conv_two_a, conv_two_b], axis=0)
    temb_grad = jnp.stack([temb_one, temb_two], axis=0)
    in_grad, conv_grad, temb_grad, attn_grad, out_grad, vec_grad, loss = lax.psum(
        (in_grad, conv_grad, temb_grad, attn_grad, out_grad, vec_grad, local_loss), "dp"
    )
    count_step = step_count[0].astype(jnp.float32)
    in_first, in_second, in_dir = adapt(in_grad, m_in, v_in, count_step)
    conv_first, conv_second, conv_dir = adapt(conv_grad, conv_m, conv_v, count_step)
    temb_first, temb_second, temb_dir = adapt(temb_grad, temb_m, temb_v, count_step)
    attn_first, attn_second, attn_dir = adapt(attn_grad, attn_m, attn_v, count_step)
    out_first, out_second, out_dir = adapt(out_grad, out_m, out_v, count_step)
    vec_first, vec_second, vec_dir = adapt(vec_grad, vec_m, vec_v, count_step)
    in_update = in_dir + DECAY * w_in
    conv_update = conv_dir + DECAY * conv_w
    temb_update = temb_dir + DECAY * temb_w
    attn_update = attn_dir + DECAY * attn_w
    out_update = out_dir + DECAY * out_w
    update_squares = jnp.concatenate(
        [
            square_sums(in_update),
            square_sums(conv_update),
            square_sums(temb_update),
            square_sums(attn_update),
        ]
    )
    weight_squares, update_squares = lax.psum((weight_squares, update_squares), "chan")
    out_weight_sq = square_sums(out_w)
    out_update_sq = square_sums(out_update)
    all_weight_sq = jnp.concatenate([weight_squares, out_weight_sq])
    all_update_sq = jnp.concatenate([update_squares, out_update_sq])
    ratio = jnp.sqrt(all_weight_sq / (all_update_sq + 1e-06))
    matrix_norms = jnp.stack([jnp.sqrt(all_weight_sq), jnp.sqrt(all_update_sq)], axis=1)
    in_new = apply_ratio(w_in, in_update, ratio[0:1])
    conv_new = apply_ratio(conv_w, conv_update, ratio[1:5])
    temb_new = apply_ratio(temb_w, temb_update, ratio[5:7])
    attn_new = apply_ratio(attn_w, attn_update, ratio[7:11])
    out_new = apply_ratio(out_w, out_update, ratio[11:12])
    vec_new = vectors - RATE * vec_dir
    return (
        loss,
        matrix_norms,
        in_new,
        in_first,
        in_second,
        conv_new,
        conv_first,
        conv_second,
        conv_new.astype(jnp.bfloat16),
        temb_new,
        temb_first,
        temb_second,
        temb_new.astype(jnp.bfloat16),
        attn_new,
        attn_first,
        attn_second,
        attn_new.astype(jnp.bfloat16),
        out_new,
        out_first,
        out_second,
        vec_new,
        vec_first,
        vec_second,
        attn_grad,
    )


def solution(mesh):
    return jax.shard_map(
        per_device,
        mesh=mesh,
        in_specs=(
            P("dp", None, None, None),
            P("dp", None),
            P("dp"),
            P(None, "dp", None),
            P(),
            P("chan", None),
            P("chan", None),
            P("chan", None),
            P(None, "chan", None),
            P(None, "chan", None),
            P(None, "chan", None),
            P(None, "chan", None),
            P(None, "chan", None),
            P(None, "chan", None),
            P(None, "chan", None),
            P(None, "chan", None),
            P(None, "chan", None),
            P(),
            P(),
            P(),
            P(None, "chan"),
            P(None, "chan"),
            P(None, "chan"),
        ),
        out_specs=(
            P(),
            P(),
            P("chan", None),
            P("chan", None),
            P("chan", None),
            P(None, "chan", None),
            P(None, "chan", None),
            P(None, "chan", None),
            P(None, "chan", None),
            P(None, "chan", None),
            P(None, "chan", None),
            P(None, "chan", None),
            P(None, "chan", None),
            P(None, "chan", None),
            P(None, "chan", None),
            P(None, "chan", None),
            P(None, "chan", None),
            P(),
            P(),
            P(),
            P(None, "chan"),
            P(None, "chan"),
            P(None, "chan"),
            P(None, "chan", None),
        ),
        check_vma=False,
    )
```

profile of v0, /device:TPU:0, one launch (start us, length us, event | category | flops | bytes accessed | tf_op | source)
XLA Modules:
  0.0 1535.4 jit_solution(11270205615337394335)
XLA Ops:
  21.2 5.7 copy.377
  35.0 32.5 %all_gather.21 = bf16[256,512]{1,0:T(8,128)(2,1)S(1)} all-gather(bf16[32,512]{1,0:T(8,128)(2,1)S(1)} %get-tuple-element.383), channel_id=1, replica_groups=mesh['dp'=4,'chan'=8] {'chan'}, dimensions={0}, use_global_device_ids=true | all-gather | bytes 294912 | tf_op jit(solution)/shard_map/all_gather | solution.py:82
  74.6 15.8 %copy.390 = bf16[256,9,2,16,16]{4,3,2,1,0:T(8,128)(2,1)} copy(bf16[256,9,2,16,16]{0,4,3,2,1:T(8,128)(2,1)} %fusion.31) | data formatting | bytes 4718592 | tf_op jit(solution)/shard_map/stack | solution.py:32
  90.4 31.2 %reshape.1301 = bf16[2304,512]{1,0:T(8,128)(2,1)S(1)} reshape(bf16[256,9,2,16,16]{4,3,2,1,0:T(8,128)(2,1)} %copy.390) | data formatting | bytes 4718592 | tf_op jit(solution)/shard_map/reshape | solution.py:32
  123.9 30.7 %all_gather.22 = bf16[256,512]{1,0:T(8,128)(2,1)S(1)} all-gather(bf16[32,512]{1,0:T(8,128)(2,1)S(1)} %get-tuple-element.381), channel_id=1, replica_groups=mesh['dp'=4,'chan'=8] {'chan'}, dimensions={0}, use_global_device_ids=true | all-gather | bytes 294912 | tf_op jit(solution)/shard_map/all_gather | solution.py:82
  161.6 15.8 %copy.394 = bf16[256,9,2,16,16]{4,3,2,1,0:T(8,128)(2,1)} copy(bf16[256,9,2,16,16]{0,4,3,2,1:T(8,128)(2,1)} %fusion.47) | data formatting | bytes 4718592 | tf_op jit(solution)/shard_map/stack | solution.py:32
  177.4 31.2 %reshape.1304 = bf16[2304,512]{1,0:T(8,128)(2,1)S(1)} reshape(bf16[256,9,2,16,16]{4,3,2,1,0:T(8,128)(2,1)} %copy.394) | data formatting | bytes 4718592 | tf_op jit(solution)/shard_map/reshape | solution.py:32
  210.4 31.1 %all_gather.23 = bf16[256,512]{1,0:T(8,128)(2,1)S(1)} all-gather(bf16[32,512]{1,0:T(8,128)(2,1)S(1)} %get-tuple-element.378), channel_id=1, replica_groups=mesh['dp'=4,'chan'=8] {'chan'}, dimensions={0}, use_global_device_ids=true | all-gather | bytes 294912 | tf_op jit(solution)/shard_map/all_gather | solution.py:82
  245.2 6.2 psum.88
  254.3 62.7 %all-reduce.59.cloned.1.call-done = f32[2,256,256]{2,1,0:T(8,128)} async-done(((f32[2,256,256]{2,1,0:T(8,128)}), f32[2,256,256]{2,1,0:T(8,128)}) %all-reduce.59.cloned.1.call-update) | async-done | bytes 524304 | tf_op jit(solution)/shard_map/psum | solution.py:175
  321.0 30.9 %all_gather.24 = bf16[256,512]{1,0:T(8,128)(2,1)S(1)} all-gather(bf16[32,512]{1,0:T(8,128)(2,1)S(1)} %bitcast.885), channel_id=1, replica_groups=mesh['dp'=4,'chan'=8] {'chan'}, dimensions={0}, use_global_device_ids=true | all-gather | bytes 294912 | tf_op jit(solution)/shard_map/all_gather | solution.py:82
  355.3 30.9 %all_gather.25 = bf16[256,512]{1,0:T(8,128)(2,1)S(1)} all-gather(bf16[32,512]{1,0:T(8,128)(2,1)S(1)} %get-tuple-element.375), channel_id=1, replica_groups=mesh['dp'=4,'chan'=8] {'chan'}, dimensions={0}, use_global_device_ids=true | all-gather | bytes 294912 | tf_op jit(solution)/shard_map/all_gather | solution.py:82
  387.0 14.2 copy.401
  401.2 31.2 %reshape.1312 = bf16[2304,512]{1,0:T(8,128)(2,1)S(1)} reshape(bf16[256,9,2,16,16]{4,3,2,1,0:T(8,128)(2,1)} %copy.401) | data formatting | bytes 4718592 | tf_op jit(solution)/shard_map/reshape | solution.py:32
  435.4 32.8 %all_gather.26 = bf16[256,512]{1,0:T(8,128)(2,1)} all-gather(bf16[32,512]{1,0:T(8,128)(2,1)S(1)} %get-tuple-element.373), channel_id=1, replica_groups=mesh['dp'=4,'chan'=8] {'chan'}, dimensions={0}, use_global_device_ids=true | all-gather | bytes 294912 | tf_op jit(solution)/shard_map/all_gather | solution.py:82
  476.2 15.8 %copy.405 = bf16[256,9,2,16,16]{4,3,2,1,0:T(8,128)(2,1)} copy(bf16[256,9,2,16,16]{0,4,3,2,1:T(8,128)(2,1)} %fusion.79) | data formatting | bytes 4718592 | tf_op jit(solution)/shard_map/stack | solution.py:32
  492.0 32.0 %reshape.1315 = bf16[2304,512]{1,0:T(8,128)(2,1)} reshape(bf16[256,9,2,16,16]{4,3,2,1,0:T(8,128)(2,1)} %copy.405) | data formatting | bytes 4718592 | tf_op jit(solution)/shard_map/reshape | solution.py:32
  527.8 32.7 %all_gather.27 = bf16[256,512]{1,0:T(8,128)(2,1)} all-gather(bf16[32,512]{1,0:T(8,128)(2,1)S(1)} %get-tuple-element.370), channel_id=1, replica_groups=mesh['dp'=4,'chan'=8] {'chan'}, dimensions={0}, use_global_device_ids=true | all-gather | bytes 294912 | tf_op jit(solution)/shard_map/all_gather | solution.py:82
  568.5 27.4 %copy.408 = bf16[256,9,2,16,16]{4,3,2,1,0:T(8,128)(2,1)} copy(bf16[256,9,2,16,16]{0,4,3,2,1:T(8,128)(2,1)} %fusion.95) | data formatting | bytes 4718592 | tf_op jit(solution)/shard_map/stack | solution.py:32
  595.9 32.0 %reshape.1318 = bf16[2304,512]{1,0:T(8,128)(2,1)} reshape(bf16[256,9,2,16,16]{4,3,2,1,0:T(8,128)(2,1)} %copy.408) | data formatting | bytes 4718592 | tf_op jit(solution)/shard_map/reshape | solution.py:32
  632.4 4.1 reshape.1320
  636.5 2.8 slice_bitcast_fusion.44
  648.6 2.9 convolution_bitcast_fusion.3
  651.5 6.1 copy.420
  657.6 22.2 %reshape.1323 = f32[256,9,2,16,16]{4,3,2,1,0:T(8,128)} reshape(f32[2304,512]{1,0:T(8,128)} %copy.420) | data formatting | bytes 9437184 | tf_op jit(solution)/shard_map/transpose(jvp())/reshape | solution.py:32
  679.8 26.8 %slice_bitcast_fusion.35 = (f32[256,2,16,16]{3,2,1,0:T(8,128)}, f32[256,2,16,16]{3,2,1,0:T(8,128)}, f32[256,2,16,16]{3,2,1,0:T(8,128)}, f32[256,2,16,16]{3,2,1,0...) fusion(f32[256,9,2,16,16]{4,3,2,1,0:T(8,128)} %reshape.1323), kind=kLoop, calls=%fused_computation.69 | loop fusion | bytes 9437184 | tf_op jit(solution)/shard_map/transpose(jvp())/unstack | solution.py:32
  706.6 6.5 pad_add_fusion.3
  713.7 10.5 pad_add_fusion.22
  724.2 4.3 copy.429
  733.0 58.6 %reduce-scatter.9.cloned.1.call-done = f32[32,512]{1,0:T(8,128)} async-done(((f32[256,512]{1,0:T(8,128)}), f32[32,512]{1,0:T(8,128)}) %reduce-scatter.9.cloned.1.call-update) | async-done | bytes 65552 | tf_op jit(solution)/shard_map/reduce_scatter | solution.py:98
  796.8 2.9 convolution_bitcast_fusion.2
  799.7 6.5 copy.431
  806.2 22.2 %reshape.1326 = f32[256,9,2,16,16]{4,3,2,1,0:T(8,128)} reshape(f32[2304,512]{1,0:T(8,128)} %copy.431) | data formatting | bytes 9437184 | tf_op jit(solution)/shard_map/transpose(jvp())/reshape | solution.py:32
  828.4 26.8 %slice_bitcast_fusion.26 = (f32[256,2,16,16]{3,2,1,0:T(8,128)}, f32[256,2,16,16]{3,2,1,0:T(8,128)}, f32[256,2,16,16]{3,2,1,0:T(8,128)}, f32[256,2,16,16]{3,2,1,0...) fusion(f32[256,9,2,16,16]{4,3,2,1,0:T(8,128)} %reshape.1326), kind=kLoop, calls=%fused_computation.54 | loop fusion | bytes 9437184 | tf_op jit(solution)/shard_map/transpose(jvp())/unstack | solution.py:32
  855.2 6.5 pad_add_fusion.2
  862.3 10.5 pad_add_fusion.16
  872.8 4.3 copy.440
  883.0 57.3 %reduce-scatter.11.cloned.1.call-done = f32[32,512]{1,0:T(8,128)} async-done(((f32[256,512]{1,0:T(8,128)}), f32[32,512]{1,0:T(8,128)}) %reduce-scatter.11.cloned.1.call-update) | async-done | bytes 65552 | tf_op jit(solution)/shard_map/reduce_scatter | solution.py:98
  950.0 3.2 convolution_bitcast_fusion.4
  956.5 3.7 fusion.183
  966.2 44.8 %reduce-scatter.19.cloned.1.call-done = f32[32,512]{1,0:T(8,128)} async-done(((f32[256,512]{1,0:T(8,128)}), f32[32,512]{1,0:T(8,128)}) %reduce-scatter.19.cloned.1.call-update) | async-done | bytes 65552
  1020.7 65.6 %all-reduce.61.cloned.1.call-done = f32[2,256,256]{2,1,0:T(8,128)} async-done(((f32[2,256,256]{2,1,0:T(8,128)}), f32[2,256,256]{2,1,0:T(8,128)}) %all-reduce.61.cloned.1.call-update) | async-done | bytes 524304 | tf_op jit(solution)/shard_map/psum | solution.py:199
  1100.8 51.7 %reduce-scatter.13.cloned.1.call-done = f32[32,512]{1,0:T(8,128)} async-done(((f32[256,512]{1,0:T(8,128)}), f32[32,512]{1,0:T(8,128)}) %reduce-scatter.13.cloned.1.call-update) | async-done | bytes 65552 | tf_op jit(solution)/shard_map/reduce_scatter | solution.py:98
  1155.5 2.9 convolution_bitcast_fusion.1
  1158.4 6.1 copy.451
  1164.5 22.2 %reshape.1331 = f32[256,9,2,16,16]{4,3,2,1,0:T(8,128)} reshape(f32[2304,512]{1,0:T(8,128)} %copy.451) | data formatting | bytes 9437184 | tf_op jit(solution)/shard_map/transpose(jvp())/reshape | solution.py:32
  1186.7 25.4 %slice_bitcast_fusion.17 = (f32[256,2,16,16]{3,2,1,0:T(8,128)S(1)}, f32[256,2,16,16]{3,2,1,0:T(8,128)}, f32[256,2,16,16]{3,2,1,0:T(8,128)}, f32[256,2,16,16]{3,2...) fusion(f32[256,9,2,16,16]{4,3,2,1,0:T(8,128)} %reshape.1331), kind=kLoop, calls=%fused_computation.39 | loop fusion | bytes 9437184 | tf_op jit(solution)/shard_map/transpose(jvp())/unstack | solution.py:32
  1212.1 5.9 pad_add_fusion.1
  1218.0 11.2 pad_add_fusion.10
  1229.3 4.3 copy.460
  1244.6 3.2 convolution_bitcast_fusion.6
  1247.7 49.1 %reduce-scatter.15.cloned.1.call-done = f32[32,512]{1,0:T(8,128)} async-done(((f32[256,512]{1,0:T(8,128)}), f32[32,512]{1,0:T(8,128)}) %reduce-scatter.15.cloned.1.call-update) | async-done | bytes 65552 | tf_op jit(solution)/shard_map/reduce_scatter | solution.py:98
  1302.6 2.9 convolution_bitcast_fusion
  1306.0 6.1 copy.462
  1312.1 22.2 %reshape.1334 = f32[256,9,2,16,16]{4,3,2,1,0:T(8,128)} reshape(f32[2304,512]{1,0:T(8,128)} %copy.462) | data formatting | bytes 9437184 | tf_op jit(solution)/shard_map/transpose(jvp())/reshape | solution.py:32
  1334.3 26.8 %slice_bitcast_fusion.8 = (f32[256,2,16,16]{3,2,1,0:T(8,128)}, f32[256,2,16,16]{3,2,1,0:T(8,128)}, f32[256,2,16,16]{3,2,1,0:T(8,128)}, f32[256,2,16,16]{3,2,1,0:...) fusion(f32[256,9,2,16,16]{4,3,2,1,0:T(8,128)} %reshape.1334), kind=kLoop, calls=%fused_computation.24 | loop fusion | bytes 9437184 | tf_op jit(solution)/shard_map/transpose(jvp())/unstack | solution.py:32
  1363.0 6.7 pad_add_fusion
  1371.6 9.9 pad_add_fusion.4
  1381.6 3.7 copy.471
  1386.7 16.5 %all-reduce.63.cloned.1.call-done = (f32[4,32,256]{2,1,0:T(8,128)}, f32[2,32,512]{2,1,0:T(8,128)}, f32[4,32,2304]{2,1,0:T(8,128)}) async-done(((f32[4,32,256]{2,1,0:T(8,128)}, f32[2,32,512]{2,1,0:T(8,128)}, f32[4,32,2304]{2,1,0:T(8,128)}), (f32[4,32,256]{2,1,0:T(8,128)}, f32[2,32,512]{2,1,0:T(8,128)}, f32[4,32,2304]{2,1,0:T(8,128)})) %all-reduce.63.cloned.1.call-update) | async-done | bytes 1441808 | tf_op jit(solution)/shard_map/psum | solution.py:347
  1405.6 5.0 multiply_reduce_fusion
  1410.5 59.0 %reduce-scatter.17.cloned.1.call-done = f32[32,512]{1,0:T(8,128)} async-done(((f32[256,512]{1,0:T(8,128)}), f32[32,512]{1,0:T(8,128)}) %reduce-scatter.17.cloned.1.call-update) | async-done | bytes 65552 | tf_op jit(solution)/shard_map/reduce_scatter | solution.py:98
  1479.3 11.3 all-reduce.53
  1495.3 19.4 %all-reduce.52 = (f32[11]{0:T(128)S(1)}, f32[11]{0:T(128)S(1)}) all-reduce(f32[11]{0:T(128)S(1)} %pad_maximum_fusion.7, f32[11]{0:T(128)S(1)} %pad_maximum_fusion.6), channel_id=1, replica_groups=mesh['dp'=4,'chan'=8] {'chan'}, use_global_device_ids=true, to_apply=%region_61.62 | all-reduce | flops 22 | bytes 176 | tf_op jit(solution)/shard_map/psum | solution.py:370
  (687 shorter events, 201.4 us)
Async XLA Ops:
  7.2 309.8 %all-reduce.59.cloned.1.call-start = ((), (), s32[]{:S(2)}) async-start(), calls=%async_computation.6 | async-start | bytes 1048576 | tf_op jit(solution)/shard_map/psum | solution.py:175
  11.5 111.7 %copy-start.136 = (f32[32]{0:T(128)}, f32[32]{0:T(128)S(1)}, u32[]{:S(2)}) copy-start(f32[32]{0:T(128)S(1)} %get-tuple-element.472) | copy-start | bytes 388
  11.5 111.7 %copy-start.139 = (f32[32]{0:T(128)}, f32[32]{0:T(128)S(1)}, u32[]{:S(2)}) copy-start(f32[32]{0:T(128)S(1)} %get-tuple-element.471) | copy-start | bytes 388
  11.5 198.2 %copy-start.131 = (f32[32]{0:T(128)}, f32[32]{0:T(128)S(1)}, u32[]{:S(2)}) copy-start(f32[32]{0:T(128)S(1)} %get-tuple-element.469) | copy-start | bytes 388
  11.6 198.2 %copy-start.140 = (f32[32]{0:T(128)}, f32[32]{0:T(128)S(1)}, u32[]{:S(2)}) copy-start(f32[32]{0:T(128)S(1)} %get-tuple-element.468) | copy-start | bytes 388
  11.6 342.5 %copy-start.133 = (f32[32]{0:T(128)}, f32[32]{0:T(128)S(1)}, u32[]{:S(2)}) copy-start(f32[32]{0:T(128)S(1)} %get-tuple-element.464) | copy-start | bytes 388
  15.6 106.9 %copy-start.69 = (f32[4,8,2]{1,2,0:T(2,128)}, f32[4,8,2]{1,2,0:T(2,128)S(1)}, u32[]{:S(2)}) copy-start(f32[4,8,2]{1,2,0:T(2,128)S(1)} %copy.391) | copy-start | bytes 772
  17.9 223.6 %copy-start.48 = (bf16[3,32,256]{2,1,0:T(8,128)(2,1)}, bf16[3,32,256]{2,1,0:T(8,128)(2,1)S(1)}, u32[]{:S(2)}) copy-start(bf16[3,32,256]{2,1,0:T(8,128)(2,1)S(1)} %slice.826) | copy-start | bytes 147460
  33.4 175.3 %copy-start.12 = (f32[512,32]{0,1:T(8,128)}, f32[512,32]{0,1:T(8,128)S(1)}, u32[]{:S(2)}) copy-start(f32[512,32]{0,1:T(8,128)S(1)} %convolution_add_fusion.1) | copy-start | bytes 196612
  208.6 112.4 %copy-start.2 = (bf16[2304,512]{1,0:T(8,128)(2,1)}, bf16[2304,512]{1,0:T(8,128)(2,1)S(1)}, u32[]{:S(2)}) copy-start(bf16[2304,512]{1,0:T(8,128)(2,1)S(1)} %reshape.1304) | copy-start | bytes 7077892
  209.2 177.1 %copy-start.16 = (f32[32,512]{1,0:T(8,128)}, f32[32,512]{1,0:T(8,128)S(1)}, u32[]{:S(2)}) copy-start(f32[32,512]{1,0:T(8,128)S(1)} %fusion.9) | copy-start | bytes 196612
  209.6 176.8 %copy-start.116 = (f32[4,2]{1,0:T(4,128)}, f32[4,2]{1,0:T(4,128)S(1)}, u32[]{:S(2)}) copy-start(f32[4,2]{1,0:T(4,128)S(1)} %fusion.165) | copy-start | bytes 100
  209.7 176.7 %copy-start.33 = (f32[4,8,2,256]{3,1,2,0:T(8,128)}, f32[4,8,2,256]{3,1,2,0:T(8,128)S(1)}, u32[]{:S(2)}) copy-start(f32[4,8,2,256]{3,1,2,0:T(8,128)S(1)} %mul.1031) | copy-start | bytes 196612
  242.4 143.9 %copy-start.59 = (bf16[32,512]{1,0:T(8,128)(2,1)}, bf16[32,512]{1,0:T(8,128)(2,1)S(1)}, u32[]{:S(2)}) copy-start(bf16[32,512]{1,0:T(8,128)(2,1)S(1)} %slice.1139) | copy-start | bytes 98308
  242.5 111.3 %copy-start.55 = (bf16[32,512]{1,0:T(8,128)(2,1)}, bf16[32,512]{1,0:T(8,128)(2,1)S(1)}, u32[]{:S(2)}) copy-start(bf16[32,512]{1,0:T(8,128)(2,1)S(1)} %get-tuple-element.432) | copy-start | bytes 98308
  242.5 111.4 %copy-start.89 = (bf16[32,512]{1,0:T(8,128)(2,1)}, bf16[32,512]{1,0:T(8,128)(2,1)S(1)}, u32[]{:S(2)}) copy-start(bf16[32,512]{1,0:T(8,128)(2,1)S(1)} %get-tuple-element.433) | copy-start | bytes 98308
  243.6 548.0 %reduce-scatter.9.cloned.1.call-start = ((), (), s32[]{:S(2)}) async-start(), calls=%async_computation.7 | async-start | bytes 589824 | tf_op jit(solution)/shard_map/reduce_scatter | solution.py:98
  252.9 100.6 %copy-start.145 = (f32[32,2]{0,1:T(2,128)}, f32[32,2]{0,1:T(2,128)S(1)}, u32[]{:S(2)}) copy-start(f32[32,2]{0,1:T(2,128)S(1)} %fusion.13) | copy-start | bytes 772
  724.2 67.4 %copy-start.66 = (f32[32,512]{1,0:T(8,128)S(1)}, f32[32,512]{1,0:T(8,128)}, u32[]{:S(2)}) copy-start(f32[32,512]{1,0:T(8,128)} %get-tuple-element.374) | copy-start | bytes 196612
  724.2 70.0 %copy-start.129 = (f32[4,2]{1,0:T(4,128)S(1)}, f32[4,2]{1,0:T(4,128)}, u32[]{:S(2)}) copy-start(f32[4,2]{1,0:T(4,128)} %copy-done.128) | copy-start | bytes 100
  724.2 70.9 %copy-start.44 = (f32[4,8,2,256]{3,1,2,0:T(8,128)S(1)}, f32[4,8,2,256]{3,1,2,0:T(8,128)}, u32[]{:S(2)}) copy-start(f32[4,8,2,256]{3,1,2,0:T(8,128)} %copy-done.43) | copy-start | bytes 196612
  724.2 70.9 %copy-start.46 = (f32[4,8,2,256]{3,1,2,0:T(8,128)S(1)}, f32[4,8,2,256]{3,1,2,0:T(8,128)}, u32[]{:S(2)}) copy-start(f32[4,8,2,256]{3,1,2,0:T(8,128)} %copy-done.45) | copy-start | bytes 196612
  730.6 209.7 %reduce-scatter.11.cloned.1.call-start = ((), (), s32[]{:S(2)}) async-start(), calls=%async_computation.8 | async-start | bytes 589824 | tf_op jit(solution)/shard_map/reduce_scatter | solution.py:98
  872.8 67.5 %copy-start.134 = (f32[32]{0:T(128)S(1)}, f32[32]{0:T(128)}, u32[]{:S(2)}) copy-start(f32[32]{0:T(128)} %copy-done.133) | copy-start | bytes 388
  872.8 71.9 %copy-start.36 = (f32[4,8,2,256]{3,1,2,0:T(8,128)S(1)}, f32[4,8,2,256]{3,1,2,0:T(8,128)}, u32[]{:S(2)}) copy-start(f32[4,8,2,256]{3,1,2,0:T(8,128)} %copy-done.35) | copy-start | bytes 196612
  872.8 71.9 %copy-start.65 = (f32[32,512]{1,0:T(8,128)S(1)}, f32[32,512]{1,0:T(8,128)}, u32[]{:S(2)}) copy-start(f32[32,512]{1,0:T(8,128)} %get-tuple-element.377) | copy-start | bytes 196612
  879.2 131.8 %reduce-scatter.19.cloned.1.call-start = ((), (), s32[]{:S(2)}) async-start(), calls=%async_computation.13 | async-start | bytes 589824
  949.9 136.3 %all-reduce.61.cloned.1.call-start = ((), (), s32[]{:S(2)}) async-start(), calls=%async_computation.9 | async-start | bytes 1048576 | tf_op jit(solution)/shard_map/psum | solution.py:199
  962.7 126.4 %copy-start.56 = (bf16[32,512]{1,0:T(8,128)(2,1)S(1)}, bf16[32,512]{1,0:T(8,128)(2,1)}, u32[]{:S(2)}) copy-start(bf16[32,512]{1,0:T(8,128)(2,1)} %copy-done.55) | copy-start | bytes 98308
  962.7 126.6 %copy-start.60 = (bf16[32,512]{1,0:T(8,128)(2,1)S(1)}, bf16[32,512]{1,0:T(8,128)(2,1)}, u32[]{:S(2)}) copy-start(bf16[32,512]{1,0:T(8,128)(2,1)} %copy-done.59) | copy-start | bytes 98308
  962.7 127.4 %copy-start.49 = (bf16[3,32,256]{2,1,0:T(8,128)(2,1)S(1)}, bf16[3,32,256]{2,1,0:T(8,128)(2,1)}, u32[]{:S(2)}) copy-start(bf16[3,32,256]{2,1,0:T(8,128)(2,1)} %copy-done.48) | copy-start | bytes 147460
  964.2 127.1 %copy-start.159 = (f32[32]{0:T(128)S(1)}, f32[32]{0:T(128)}, u32[]{:S(2)}) copy-start(f32[32]{0:T(128)} %get-tuple-element.294) | copy-start | bytes 388
  964.2 129.1 %copy-start.163 = (f32[32]{0:T(128)S(1)}, f32[32]{0:T(128)}, u32[]{:S(2)}) copy-start(f32[32]{0:T(128)} %get-tuple-element.365) | copy-start | bytes 388
  964.2 131.0 %copy-start.158 = (f32[32]{0:T(128)S(1)}, f32[32]{0:T(128)}, u32[]{:S(2)}) copy-start(f32[32]{0:T(128)} %get-tuple-element.363) | copy-start | bytes 388
  964.2 133.0 %copy-start.162 = (f32[32]{0:T(128)S(1)}, f32[32]{0:T(128)}, u32[]{:S(2)}) copy-start(f32[32]{0:T(128)} %get-tuple-element.439) | copy-start | bytes 388
  964.2 135.0 %copy-start.21 = (bf16[256,512]{1,0:T(8,128)(2,1)S(1)}, bf16[256,512]{1,0:T(8,128)(2,1)}, u32[]{:S(2)}) copy-start(bf16[256,512]{1,0:T(8,128)(2,1)} %copy-done.20) | copy-start | bytes 786436
  1013.7 138.8 %copy-start.64 = (f32[32,512]{1,0:T(8,128)S(1)}, f32[32,512]{1,0:T(8,128)}, u32[]{:S(2)}) copy-start(f32[32,512]{1,0:T(8,128)} %get-tuple-element.379) | copy-start | bytes 196612
  1013.7 138.8 %copy-start.132 = (f32[32]{0:T(128)S(1)}, f32[32]{0:T(128)}, u32[]{:S(2)}) copy-start(f32[32]{0:T(128)} %copy-done.131) | copy-start | bytes 388
  1013.7 138.8 %copy-start.141 = (f32[32]{0:T(128)S(1)}, f32[32]{0:T(128)}, u32[]{:S(2)}) copy-start(f32[32]{0:T(128)} %copy-done.140) | copy-start | bytes 388
  1013.7 140.5 %copy-start.17 = (f32[32,512]{1,0:T(8,128)S(1)}, f32[32,512]{1,0:T(8,128)}, u32[]{:S(2)}) copy-start(f32[32,512]{1,0:T(8,128)} %copy-done.16) | copy-start | bytes 196612
  1013.7 140.5 %copy-start.101 = (f32[4,2]{1,0:T(4,128)S(1)}, f32[4,2]{1,0:T(4,128)}, u32[]{:S(2)}) copy-start(f32[4,2]{1,0:T(4,128)} %copy-done.100) | copy-start | bytes 100
  1013.7 140.5 %copy-start.117 = (f32[4,2]{1,0:T(4,128)S(1)}, f32[4,2]{1,0:T(4,128)}, u32[]{:S(2)}) copy-start(f32[4,2]{1,0:T(4,128)} %copy-done.116) | copy-start | bytes 100
  1013.7 140.7 %copy-start.126 = (f32[4,2]{1,0:T(4,128)S(1)}, f32[4,2]{1,0:T(4,128)}, u32[]{:S(2)}) copy-start(f32[4,2]{1,0:T(4,128)} %copy-done.125) | copy-start | bytes 100
  1013.8 141.0 %copy-start.34 = (f32[4,8,2,256]{3,1,2,0:T(8,128)S(1)}, f32[4,8,2,256]{3,1,2,0:T(8,128)}, u32[]{:S(2)}) copy-start(f32[4,8,2,256]{3,1,2,0:T(8,128)} %copy-done.33) | copy-start | bytes 196612
  1013.8 141.0 %copy-start.63 = (f32[32,512]{1,0:T(8,128)S(1)}, f32[32,512]{1,0:T(8,128)}, u32[]{:S(2)}) copy-start(f32[32,512]{1,0:T(8,128)} %get-tuple-element.380) | copy-start | bytes 196612
  1013.8 138.7 %reduce-scatter.13.cloned.1.call-start = ((), (), s32[]{:S(2)}) async-start(), calls=%async_computation.10 | async-start | bytes 589824 | tf_op jit(solution)/shard_map/reduce_scatter | solution.py:98
  1091.2 205.7 %reduce-scatter.15.cloned.1.call-start = ((), (), s32[]{:S(2)}) async-start(), calls=%async_computation.11 | async-start | bytes 589824 | tf_op jit(solution)/shard_map/reduce_scatter | solution.py:98
  1155.5 89.1 %copy-start.27 = (f32[32,512]{1,0:T(8,128)}, f32[32,512]{1,0:T(8,128)S(1)}, u32[]{:S(2)}) copy-start(f32[32,512]{1,0:T(8,128)S(1)} %get-tuple-element.355) | copy-start | bytes 196612
  1229.2 69.9 %copy-start.70 = (f32[4,8,2]{1,2,0:T(2,128)S(1)}, f32[4,8,2]{1,2,0:T(2,128)}, u32[]{:S(2)}) copy-start(f32[4,8,2]{1,2,0:T(2,128)} %copy-done.69) | copy-start | bytes 772
  1229.2 69.9 %copy-start.94 = (f32[4,2]{1,0:T(4,128)S(1)}, f32[4,2]{1,0:T(4,128)}, u32[]{:S(2)}) copy-start(f32[4,2]{1,0:T(4,128)} %copy-done.92) | copy-start | bytes 100
  1229.3 69.9 %copy-start.108 = (f32[4,2]{1,0:T(4,128)S(1)}, f32[4,2]{1,0:T(4,128)}, u32[]{:S(2)}) copy-start(f32[4,2]{1,0:T(4,128)} %copy-done.106) | copy-start | bytes 100
  1229.3 70.1 %copy-start.124 = (f32[4,2]{1,0:T(4,128)S(1)}, f32[4,2]{1,0:T(4,128)}, u32[]{:S(2)}) copy-start(f32[4,2]{1,0:T(4,128)} %copy-done.123) | copy-start | bytes 100
  1233.6 68.2 %copy-start.1 = (bf16[2304,512]{1,0:T(8,128)(2,1)S(1)}, bf16[2304,512]{1,0:T(8,128)(2,1)}, u32[]{:S(2)}) copy-start(bf16[2304,512]{1,0:T(8,128)(2,1)} %copy-done) | copy-start | bytes 7077892
  1235.8 167.4 %all-reduce.63.cloned.1.call-start = ((), (), s32[]{:S(2)}) async-start(), calls=%async_computation.14 | async-start | bytes 2883584 | tf_op jit(solution)/shard_map/psum | solution.py:347
  1362.9 106.6 %reduce-scatter.17.cloned.1.call-start = ((), (), s32[]{:S(2)}) async-start(), calls=%async_computation.12 | async-start | bytes 589824 | tf_op jit(solution)/shard_map/reduce_scatter | solution.py:98
  1405.4 67.0 %copy-start.28 = (f32[32,512]{1,0:T(8,128)S(1)}, f32[32,512]{1,0:T(8,128)}, u32[]{:S(2)}) copy-start(f32[32,512]{1,0:T(8,128)} %copy-done.27) | copy-start | bytes 196612
  1405.5 67.0 %copy-start.30 = (f32[4,8,2,256]{3,1,2,0:T(8,128)S(1)}, f32[4,8,2,256]{3,1,2,0:T(8,128)}, u32[]{:S(2)}) copy-start(f32[4,8,2,256]{3,1,2,0:T(8,128)} %copy-done.29) | copy-start | bytes 196612
  1405.5 67.8 %copy-start.58 = (bf16[27,512]{1,0:T(8,128)(2,1)S(1)}, bf16[27,512]{1,0:T(8,128)(2,1)}, u32[]{:S(2)}) copy-start(bf16[27,512]{1,0:T(8,128)(2,1)} %copy-done.57) | copy-start | bytes 82948
  1405.5 72.0 %copy-start.25 = (f32[4,32,256]{2,1,0:T(8,128)S(1)}, f32[4,32,256]{2,1,0:T(8,128)}, u32[]{:S(2)}) copy-start(f32[4,32,256]{2,1,0:T(8,128)} %param.81) | copy-start | bytes 393220
  1405.5 72.0 %copy-start.47 = (f32[4,32,256]{2,1,0:T(8,128)S(1)}, f32[4,32,256]{2,1,0:T(8,128)}, u32[]{:S(2)}) copy-start(f32[4,32,256]{2,1,0:T(8,128)} %get-tuple-element.530) | copy-start | bytes 393220
  1405.5 72.0 %copy-start.88 = (f32[4,32,256]{2,1,0:T(8,128)S(1)}, f32[4,32,256]{2,1,0:T(8,128)}, u32[]{:S(2)}) copy-start(f32[4,32,256]{2,1,0:T(8,128)} %param.83) | copy-start | bytes 393220
  1405.5 73.7 %copy-start.85 = (f32[3,2304]{1,0:T(4,128)S(1)}, f32[3,2304]{1,0:T(4,128)}, u32[]{:S(2)}) copy-start(f32[3,2304]{1,0:T(4,128)} %fusion.183) | copy-start | bytes 82948
  1405.5 85.1 %copy-start.68 = (f32[32,27]{1,0:T(8,128)S(1)}, f32[32,27]{1,0:T(8,128)}, u32[]{:S(2)}) copy-start(f32[32,27]{1,0:T(8,128)} %param.72) | copy-start | bytes 10372
  1405.5 109.2 %copy-start.52 = (f32[3,2304]{1,0:T(4,128)S(1)}, f32[3,2304]{1,0:T(4,128)}, u32[]{:S(2)}) copy-start(f32[3,2304]{1,0:T(4,128)} %param.84) | copy-start | bytes 82948
  (110 other events, 2691.7 us)
Sparse Core Ops, SparseCore 0:
  243.8 73.1 all-reduce.58
  730.7 60.8 reduce-scatter.8
  879.3 60.9 reduce-scatter.10
  950.1 60.9 reduce-scatter.18
  1014.8 71.3 all-reduce.60
  1091.3 61.1 reduce-scatter.12
  1235.9 60.9 reduce-scatter.14
  1363.0 40.1 all-reduce.62
  1407.5 61.9 reduce-scatter.16
where the time goes:
time: 1550 us; the launch traced here: 1540 us
  local copies, waits for them, and re-layouts  583 us (38%)
  waiting for transfers between devices  466 us (30%)
  blocking collectives  259 us (17%)
  other arithmetic  159 us (10%)
  matrix products  48.2 us (3%)
  between operations  20.6 us (1%)
    reduce_scatter x5, waiting for transfers between devices, linear_back(): lax.psum_scatter(from_columns(part_columns, images) if kernel == 3 else p...  276 us
    reshape x11, local copies, waits for them, and re-layouts, to_columns(): return jnp.stack(shifted, axis=1).reshape(field_depth * 9, images * HW * HW)  251 us
    all_gather x7, blocking collectives, gather_act(): return lax.all_gather(value_low, 'chan', axis=0, tiled=True)  222 us
    another operation x25, local copies, waits for them, and re-layouts, to_columns(): return jnp.stack(shifted, axis=1).reshape(field_depth * 9, images * HW * HW)  204 us
    add_any x10, other arithmetic, to_columns(): padded[:, :, row_off:row_off + HW, col_off:col_off + HW]  69.8 us
    psum x1, waiting for transfers between devices, attn_backward(): lax.psum((partial_scores(query, key_part, images), probs_part), 'chan')  65.6 us
    psum x1, waiting for transfers between devices, attn_forward(): scores = lax.psum(partial_scores(query, key_part, images), 'chan') * scale  62.7 us
    unnamed x394, local copies, waits for them, and re-layouts  48.7 us
  transfers between devices with their start and end apart: 9, of which 9 were waited for; matrix products, arithmetic and copies ran while one was open for 5% of the time, Pallas kernels for 0%

commit v1 on v0

v1 whole, which is shorter than its diff:
```python
import functools
import math

import jax
import jax.numpy as jnp
from jax import lax
from jax.experimental import pallas as pl
from jax.experimental.pallas import tpu as pltpu
from jax.sharding import PartitionSpec as P

TEMB = 512
HW = 16
PIX = HW * HW
GSIZE = 8
C = 256
TAPS = 9
KW = C * TAPS
HALF = 128 * TAPS
LANES = KW + C

NORM_EPS = 1e-05
BETA_ONE = 0.9
BETA_TWO = 0.95
ADAM_EPS = 1e-06
DECAY = 0.01
RATE = 0.3
F32 = jnp.float32
BF16 = jnp.bfloat16
HIGH = lax.Precision.HIGHEST
MESH = pl.DeviceIdType.MESH
NN = (((1,), (0,)), ((), ()))
NT = (((1,), (1,)), ((), ()))
TN = (((0,), (0,)), ((), ()))
MIB = 1024 * 1024

VEC_ROWS = 22
LOSS_ROW = 24
MAIN = HALF + 128 + 128
SUM_ROWS = 16


def dot(a, b, dims, precision=None):
    return lax.dot_general(a, b, dims, precision=precision, preferred_element_type=F32)


def iota(shape, axis):
    return lax.broadcasted_iota(jnp.int32, shape, axis)


def tap_order():
    wanted = (iota((1, HALF), 1) & 127) * TAPS + (iota((1, HALF), 1) >> 7)
    return jnp.where(iota((HALF, 1), 0) == wanted, 1.0, 0.0).astype(BF16)


def prep_kernel(lr, images, crop, conv_w, attn_w, w_in, temb_w, temb_act, vectors, out_w,
                shard, small, count, out_taps, rows_scr, in_scr, out_scr):
    order = tap_order()
    for k in range(4):
        weight = conv_w[k].astype(BF16)
        both = jnp.concatenate([weight[:, :HALF], weight[:, HALF:]], axis=0)
        mixed = dot(both, order, NN).astype(BF16)
        for tap in range(TAPS):
            for h in range(2):
                lanes = slice(tap * C + h * 128, tap * C + h * 128 + 128)
                shard[k * lr:(k + 1) * lr, lanes] = mixed[h * lr:(h + 1) * lr, tap * 128:(tap + 1) * 128]
        shard[k * lr:(k + 1) * lr, KW:LANES] = attn_w[k].astype(BF16)

    out_scr[...] = jnp.zeros_like(out_scr)
    for h in range(2):
        out_scr[h * 8:h * 8 + 3, :] = out_w[:, h * HALF:(h + 1) * HALF]
    out_mixed = dot(out_scr[...].astype(BF16), order, NN)
    for tap in range(TAPS):
        for h in range(2):
            out_taps[tap * 8:tap * 8 + 8, h * 128:(h + 1) * 128] = out_mixed[
                h * 8:h * 8 + 8, tap * 128:(tap + 1) * 128
            ]

    rows_scr[...] = jnp.zeros_like(rows_scr)
    rows_scr[0:VEC_ROWS, 0:lr] = vectors[...]
    for block in range(2):
        shift = dot(temb_act[...], temb_w[block].astype(BF16), NT)
        for b in range(images):
            row = VEC_ROWS + block * images + b
            rows_scr[row:row + 1, 0:lr] = (
                shift[b:b + 1, :] + vectors[17 + block:18 + block, :]
            ) + vectors[13 + 2 * block:14 + 2 * block, :]
    in_scr[...] = jnp.zeros_like(in_scr)
    in_scr[0:lr, 0:27] = w_in[...]
    turned = in_scr[...].T
    packed = [jnp.zeros((8, 128), F32), jnp.zeros((8, 128), F32)]
    for g in range(4):
        for i, rows in enumerate((rows_scr[g * 8:g * 8 + 8, :], turned[g * 8:g * 8 + 8, :])):
            packed[i] += rows if g == 0 else pltpu.roll(rows, g * lr, 1)
    small[0:8, :] = packed[0]
    small[8:16, :] = packed[1]

    total = jnp.int32(0)
    for b in range(images):
        side = jnp.minimum(jnp.maximum(crop[b, 2], 0), HW)
        total += 3 * side * side
    count[...] = jnp.full((8, 128), total, jnp.int32).astype(F32)


def gather_kernel(n, ny, nz, nx, dp, width, shard, small, count, whole, smalls, counts,
                  own_sem, near_send, near_recv, x_send, x_recv, core_send, core_recv,
                  small_send, small_recv, count_send, count_recv):
    me = lax.axis_index("chan")
    part = lax.axis_index("dp")
    z, y = me // ny, me % ny
    x, core = part // 2, part % 2

    def chan_of(k, l):
        return lax.rem(z + k + nz, nz) * ny + lax.rem(y + l + ny, ny)

    def part_of(m, c):
        return lax.rem(x + m + nx, nx) * 2 + c

    def lanes_of(p):
        return pl.ds(pl.multiple_of(p * width, 128), width)

    barrier = pltpu.get_barrier_semaphore()
    for k in range(1, n):
        pl.semaphore_signal(barrier, inc=1, device_id=(part, lax.rem(me + k, n)), device_id_type=MESH)
    for k in range(1, dp):
        pl.semaphore_signal(barrier, inc=1, device_id=(lax.rem(part + k, dp), me), device_id_type=MESH)

    own = [
        pltpu.make_async_copy(shard, whole.at[me], own_sem.at[0]),
        pltpu.make_async_copy(small, smalls.at[me], own_sem.at[1]),
        pltpu.make_async_copy(count, counts.at[part], own_sem.at[2]),
    ]
    for copy in own:
        copy.start()
    pl.semaphore_wait(barrier, n + dp - 2)

    sends = []

    def remote(src, dst, send_sem, recv_sem, target):
        return pltpu.make_async_remote_copy(
            src_ref=src, dst_ref=dst, send_sem=send_sem, recv_sem=recv_sem,
            device_id=target, device_id_type=MESH,
        )

    def send(*args):
        copy = remote(*args)
        copy.start()
        sends.append(copy)

    mine = lanes_of(part)
    order = [(k, l) for k in range(nz) for l in range(ny)][1:]
    place = {kl: o for o, kl in enumerate(order)}

    def slot(src, p):
        return whole.at[src, :, lanes_of(p)]

    for k in range(1, nz):
        send(shard.at[:, mine], slot(me, part), near_send.at[place[(k, 0)]],
             near_recv.at[place[(k, 0)]], (part, chan_of(k, 0)))
    for l in range(1, ny):
        send(shard.at[:, mine], slot(me, part), near_send.at[place[(0, l)]],
             near_recv.at[place[(0, l)]], (part, chan_of(0, l)))
    for k in range(1, n):
        target = lax.rem(me + k, n)
        send(small, smalls.at[me], small_send.at[k - 1], small_recv.at[k - 1], (part, target))
    for k in range(1, dp):
        target = lax.rem(part + k, dp)
        send(count, counts.at[part], count_send.at[k - 1], count_recv.at[k - 1], (target, me))

    def forward(kl):
        o = place[kl]
        src = chan_of(-kl[0], -kl[1])
        remote(shard.at[:, mine], slot(src, part), near_send.at[o], near_recv.at[o],
               (part, src)).wait_recv()
        for m in range(1, nx):
            send(slot(src, part), slot(src, part), x_send.at[m - 1, o], x_recv.at[m - 1, o],
                 (part_of(m, core), me))
        send(slot(src, part), slot(src, part), core_send.at[0, o], core_recv.at[0, o],
             (part_of(0, 1 - core), me))

    for k in range(1, nz):
        src = chan_of(-k, 0)
        o = place[(k, 0)]
        forward((k, 0))
        for l in range(1, ny):
            send(slot(src, part), slot(src, part), near_send.at[place[(k, l)]],
                 near_recv.at[place[(k, l)]], (part, chan_of(0, l)))
    for l in range(1, ny):
        forward((0, l))
    for k in range(1, nz):
        for l in range(1, ny):
            forward((k, l))
    for o, (k, l) in enumerate(order):
        src = chan_of(-k, -l)
        for m in range(1, nx):
            p = part_of(-m, core)
            remote(slot(src, p), slot(src, p), x_send.at[m - 1, o], x_recv.at[m - 1, o],
                   (p, me)).wait_recv()
            send(slot(src, p), slot(src, p), core_send.at[m, o], core_recv.at[m, o],
                 (part_of(0, 1 - core), me))
    for k in range(1, n):
        src = lax.rem(me - k + n, n)
        remote(small, smalls.at[src], small_send.at[k - 1], small_recv.at[k - 1],
               (part, src)).wait_recv()
    for k in range(1, dp):
        p = lax.rem(part - k + dp, dp)
        remote(count, counts.at[p], count_send.at[k - 1], count_recv.at[k - 1], (p, me)).wait_recv()
    for o, (k, l) in enumerate(order):
        src = chan_of(-k, -l)
        for m in range(nx):
            p = part_of(-m, 1 - core)
            remote(slot(src, p), slot(src, p), core_send.at[m, o], core_recv.at[m, o],
                   (part_of(0, 1 - core), me)).wait_recv()
    for copy in sends:
        copy.wait_send()
    for copy in own:
        copy.wait()


def group_sum(row):
    lane = iota(row.shape, 1)
    step = 1
    while step < GSIZE:
        up = pltpu.roll(row, C - step, 1)
        down = pltpu.roll(row, step, 1)
        row = row + jnp.where((lane & step) == 0, up, down)
        step *= 2
    return row


def row_sum(value):
    return jnp.sum(value, axis=0, keepdims=True)


def group_mean(row):
    wide = jnp.broadcast_to(row, (8, C))
    return group_sum(wide)[0:1] * (1.0 / (GSIZE * PIX))


def compute_kernel(n, lr, dp, images, crop, coefs, whole, smalls, counts, out_taps, temb_act,
                   canvas, noise, main, misc_out, misc_vec,
                   vec, w_in, hidden, xhat, dact, rstd, col0, col1, col2, col3, taps0, rows_scr, acts,
                   q_scr, k_scr, v_scr, probs, mixed_scr, gvec, gconv, gsum):
    cols = (col0, col1, col2, col3)
    d = lax.axis_index("chan")
    rows_all = images * PIX
    scale = C ** -0.5

    def span(b):
        return slice(b * PIX, (b + 1) * PIX)

    def conv_weight(k):
        return whole[:, k * lr:(k + 1) * lr, 0:KW].reshape(C, KW)

    def attn_weight(k):
        return whole[:, k * lr:(k + 1) * lr, KW:LANES].reshape(C, C)

    vec[...] = jnp.zeros_like(vec)
    w_in[...] = jnp.zeros_like(w_in)
    lane_wide = iota((16, C), 1)
    for j in range(n):
        block = jnp.concatenate([smalls[j], jnp.zeros((16, 128), F32)], axis=1)
        for g in range(4):
            piece = jnp.where((lane_wide >= g * lr) & (lane_wide < (g + 1) * lr), block, 0.0)
            move = (j - g) * lr % C
            if move:
                piece = pltpu.roll(piece, move, 1)
            vec[g * 8:g * 8 + 8, :] += piece[0:8]
            w_in[g * 8:g * 8 + 8, :] += piece[8:16]

    def vrow(i):
        return vec[i:i + 1, :]

    total = counts[0, 0:1, 0:1]
    for k in range(1, dp):
        total = total + counts[k, 0:1, 0:1]

    lane = iota((1, PIX), 1)
    pix_x, pix_y = lane & (HW - 1), lane >> 4
    size = canvas.shape[2]
    noise_rows = []
    mask_rows = []
    noisy_rows = []
    for b in range(images):
        pick = jnp.where(iota((size, PIX), 0) == crop[b, 1] + pix_x, 1.0, 0.0)
        flat = canvas[b].reshape(3 * size, size)
        spread = dot(flat, pick, NN, HIGH).reshape(3, size, PIX)
        chosen = iota((size, PIX), 0) == crop[b, 0] + pix_y
        clean = jnp.sum(jnp.where(chosen[None], spread, 0.0), axis=1)
        noise_b = noise[:, b, :]
        noisy_rows.append(coefs[0, b] * clean + coefs[1, b] * noise_b)
        noise_rows.append(noise_b)
        side = crop[b, 2]
        mask_rows.append(jnp.where((pix_x < side) & (pix_y < side), 1.0, 0.0))
    zeros5 = jnp.zeros((5, rows_all), F32)
    noisy = jnp.concatenate([jnp.concatenate(noisy_rows, axis=1), zeros5], axis=0)
    noise_all = jnp.concatenate([jnp.concatenate(noise_rows, axis=1), zeros5], axis=0)
    mask_all = jnp.concatenate(mask_rows, axis=1)

    lane_all = iota((8, rows_all), 1)
    px, py = lane_all & (HW - 1), (lane_all >> 4) & (HW - 1)

    def tap_shift(field, tap):
        dy, dx = tap // 3 - 1, tap % 3 - 1
        move = -(dy * HW + dx) % rows_all
        out = pltpu.roll(field, move, 1) if move else field
        inside = (px + dx >= 0) & (px + dx < HW) & (py + dy >= 0) & (py + dy < HW)
        return jnp.where(inside, out, 0.0)

    noisy = noisy.astype(BF16).astype(F32)
    rows_scr[...] = jnp.zeros_like(rows_scr)
    for tap in range(TAPS):
        moved = tap_shift(noisy, tap)
        for colour in range(3):
            rows_scr[colour * TAPS + tap:colour * TAPS + tap + 1, :] = moved[colour:colour + 1]
    taps0[...] = rows_scr[...].astype(BF16)
    hidden[0] = dot(taps0[...], w_in[...].astype(BF16), TN) + vrow(12)

    col_x = iota((PIX, C), 0) & (HW - 1)

    def norm_fwd(i, value, gain, shift, store):
        for b in range(images):
            part = value[span(b)]
            centred = part - group_mean(row_sum(part))
            inv = lax.rsqrt(group_mean(row_sum(centred * centred)) + NORM_EPS)
            normed = centred * inv
            scaled = normed * gain + shift
            gate = 0.5 * jnp.tanh(0.5 * scaled) + 0.5
            act = scaled * gate
            xhat[i, span(b), :] = normed
            dact[i, span(b), :] = gate + act * (1.0 - gate)
            rstd[i * images + b:i * images + b + 1, :] = inv
            store(b, act)

    def norm_back(i, grad, gain_row):
        outs = []
        gain = vrow(gain_row)
        gain_sum = jnp.zeros((1, C), F32)
        shift_sum = jnp.zeros((1, C), F32)
        for b in range(images):
            slope = grad[span(b)] * dact[i, span(b), :]
            normed = xhat[i, span(b), :]
            shift_b = row_sum(slope)
            gain_b = row_sum(slope * normed)
            mean_one = group_mean(shift_b * gain)
            mean_two = group_mean(gain_b * gain)
            inv = rstd[i * images + b:i * images + b + 1, :]
            outs.append(inv * (slope * gain - mean_one - normed * mean_two))
            gain_sum += gain_b
            shift_sum += shift_b
        gvec[gain_row:gain_row + 1, :] = gain_sum
        gvec[6 + gain_row:7 + gain_row, :] = shift_sum
        return jnp.concatenate(outs, axis=0)

    blank = jnp.zeros((HW, C), BF16)

    def store_cols(ref, b, act):
        left = jnp.where(col_x > 0, pltpu.roll(act, 1, 0), 0.0)
        right = jnp.where(col_x < HW - 1, pltpu.roll(act, PIX - 1, 0), 0.0)
        for dx, moved in enumerate((left, act, right)):
            low = moved.astype(BF16)
            for dy in range(3):
                lanes = slice((3 * dy + dx) * C, (3 * dy + dx + 1) * C)
                base = b * PIX
                if dy == 0:
                    ref[base:base + HW, lanes] = blank
                    ref[base + HW:base + PIX, lanes] = low[:PIX - HW]
                elif dy == 1:
                    ref[base:base + PIX, lanes] = low
                else:
                    ref[base:base + PIX - HW, lanes] = low[HW:]
                    ref[base + PIX - HW:base + PIX, lanes] = blank

    def add_rows(value, first):
        return jnp.concatenate(
            [value[span(b)] + vrow(first + b) for b in range(images)], axis=0
        )

    def block_fwd(block, source, target):
        norm_fwd(3 * block, hidden[source], vrow(3 * block), vrow(6 + 3 * block),
                 functools.partial(store_cols, cols[2 * block]))
        middle = dot(cols[2 * block][...], conv_weight(2 * block), NT)
        middle = add_rows(middle, VEC_ROWS + block * images)
        norm_fwd(3 * block + 1, middle, vrow(3 * block + 1), vrow(7 + 3 * block),
                 functools.partial(store_cols, cols[2 * block + 1]))
        branch = dot(cols[2 * block + 1][...], conv_weight(2 * block + 1), NT)
        hidden[target] = hidden[source] + (branch + vrow(14 + 2 * block))

    def store_act(index):
        def store(b, act):
            acts[index, span(b), :] = act.astype(BF16)
        return store

    block_fwd(0, 0, 1)

    norm_fwd(2, hidden[1], vrow(2), vrow(8), store_act(0))
    q_scr[...] = (dot(acts[0], attn_weight(0), NT) + vrow(19)).astype(BF16)
    k_scr[...] = dot(acts[0], attn_weight(1), NT).astype(BF16)
    v_scr[...] = (dot(acts[0], attn_weight(2), NT) + vrow(20)).astype(BF16)
    for b in range(images):
        scores = dot(q_scr[span(b), :], k_scr[span(b), :], NT) * scale
        raised = jnp.exp(scores - jnp.max(scores, axis=1, keepdims=True))
        soft = raised / jnp.sum(raised, axis=1, keepdims=True)
        probs[b] = soft
        mixed_scr[span(b), :] = dot(soft.astype(BF16), v_scr[span(b), :], NN).astype(BF16)
    hidden[0] = hidden[1] + (dot(mixed_scr[...], attn_weight(3), NT) + vrow(21))

    block_fwd(1, 0, 1)
    norm_fwd(5, hidden[1], vrow(5), vrow(11), store_act(1))

    out_low = out_taps[...].astype(BF16)
    fanned = dot(out_low, acts[1], NT)
    pred = jnp.zeros((8, rows_all), F32)
    for tap in range(TAPS):
        pred += tap_shift(fanned[tap * 8:tap * 8 + 8], tap)
    error = pred - noise_all
    masked = mask_all * error
    inverse = 1.0 / total
    loss = jnp.sum(jnp.sum(masked * error, axis=1, keepdims=True), axis=0, keepdims=True) * inverse
    grad_pred = (2.0 * masked * inverse).astype(BF16).astype(F32)
    spread_pred = jnp.concatenate(
        [tap_shift(grad_pred, TAPS - 1 - tap) for tap in range(TAPS)], axis=0
    ).astype(BF16)
    out_grad = dot(spread_pred, acts[1], NN)
    grad = dot(spread_pred, out_low, TN)

    gvec[...] = jnp.zeros_like(gvec)
    pick_own = jnp.where(
        iota((lr, C), 1) == iota((lr, C), 0) + d * lr, 1.0, 0.0
    ).astype(BF16)

    def own_rows(low):
        return dot(pick_own, low, NT).astype(BF16)

    def conv_back(k, low):
        gconv[k * lr:(k + 1) * lr, 0:KW] = dot(own_rows(low), cols[k][...], NN)
        parts = dot(low, conv_weight(k), NN)
        outs = []
        hole = jnp.zeros((HW, C), F32)
        for b in range(images):
            sides = []
            for dx in range(3):
                up = parts[span(b), dx * C:(dx + 1) * C]
                mid = parts[span(b), (3 + dx) * C:(4 + dx) * C]
                down = parts[span(b), (6 + dx) * C:(7 + dx) * C]
                sides.append(
                    mid
                    + jnp.concatenate([up[HW:], hole], axis=0)
                    + jnp.concatenate([hole, down[:PIX - HW]], axis=0)
                )
            left = pltpu.roll(jnp.where(col_x > 0, sides[0], 0.0), PIX - 1, 0)
            right = pltpu.roll(jnp.where(col_x < HW - 1, sides[2], 0.0), 1, 0)
            outs.append(sides[1] + left + right)
        return jnp.concatenate(outs, axis=0)

    def block_back(block, grad):
        gvec[14 + 2 * block:15 + 2 * block, :] = row_sum(grad)
        back = conv_back(2 * block + 1, grad.astype(BF16))
        middle = norm_back(3 * block + 1, back, 3 * block + 1)
        gsum[...] = jnp.zeros_like(gsum)
        for b in range(images):
            gsum[b:b + 1, :] = row_sum(middle[span(b)])
        whole_sum = row_sum(gsum[...])
        gvec[13 + 2 * block:14 + 2 * block, :] = whole_sum
        gvec[17 + block:18 + block, :] = whole_sum
        own = dot(pick_own, gsum[...].astype(BF16), NT).astype(BF16)
        temb = dot(own, temb_act[...], NN)
        for j in range(4):
            top = (j % 2) * 2 * lr + block * lr
            gconv[top:top + lr, LANES + (j // 2) * 128:LANES + (j // 2) * 128 + 128] = (
                temb[:, j * 128:(j + 1) * 128]
            )
        back = conv_back(2 * block, middle.astype(BF16))
        return grad + norm_back(3 * block, back, 3 * block)

    grad = norm_back(5, grad, 5)
    grad = block_back(1, grad)

    gvec[21:22, :] = row_sum(grad)
    low = grad.astype(BF16)
    gconv[3 * lr:4 * lr, KW:LANES] = dot(own_rows(low), mixed_scr[...], NN)
    mixed_low = dot(low, attn_weight(3), NN).astype(BF16)
    grads_q, grads_k, grads_v = [], [], []
    for b in range(images):
        part = mixed_low[span(b)]
        soft = probs[b]
        grad_soft = dot(part, v_scr[span(b), :], NT)
        grads_v.append(dot(soft.astype(BF16), part, TN))
        weighed = soft * grad_soft
        slope = (weighed - soft * jnp.sum(weighed, axis=1, keepdims=True)).astype(BF16)
        grads_q.append(scale * dot(slope, k_scr[span(b), :], NN))
        grads_k.append(scale * dot(slope, q_scr[span(b), :], TN))
    back = jnp.zeros((rows_all, C), F32)
    for i, grads in enumerate((grads_q, grads_k, grads_v)):
        full = jnp.concatenate(grads, axis=0)
        if i != 1:
            gvec[19 + i // 2:20 + i // 2, :] = row_sum(full)
        low = full.astype(BF16)
        gconv[i * lr:(i + 1) * lr, KW:LANES] = dot(own_rows(low), acts[0], NN)
        back += dot(low, attn_weight(i), NN)
    grad = grad + norm_back(2, back, 2)

    grad = block_back(0, grad)
    gvec[12:13, :] = row_sum(grad)
    in_grad = dot(own_rows(grad.astype(BF16)), taps0[...], NT)

    order = tap_order()
    shaped = []
    for h in range(2):
        shaped.append(jnp.concatenate(
            [gconv[:, tap * C + h * 128:tap * C + h * 128 + 128] for tap in range(TAPS)], axis=1
        ).astype(BF16))
    for h in range(2):
        shaped.append(jnp.concatenate(
            [
                jnp.concatenate(
                    [out_grad[tap * 8:tap * 8 + 8, h * 128:(h + 1) * 128] for tap in range(TAPS)], axis=1
                ),
                jnp.zeros((8, HALF), F32),
            ], axis=0,
        ).astype(BF16))
    natural = dot(jnp.concatenate(shaped, axis=0), order, NT)
    for h in range(2):
        main[h, :, 0:HALF] = natural[h * 4 * lr:(h + 1) * 4 * lr].astype(BF16)
        main[h, :, HALF:HALF + 128] = gconv[:, KW + h * 128:KW + h * 128 + 128].astype(BF16)
        main[h, :, HALF + 128:MAIN] = gconv[:, LANES + h * 128:LANES + h * 128 + 128].astype(BF16)
        misc_out[h] = natural[8 * lr + h * 16:8 * lr + h * 16 + 8]
    own_vec = pltpu.roll(gvec[...], lax.rem(C - d * lr, C), 1)
    misc_vec[0] = own_vec[:, 0:128]
    misc_vec[0, LOSS_ROW:LOSS_ROW + 1, :] = jnp.broadcast_to(loss, (1, 128))
    misc_vec[1] = jnp.zeros((32, 128), F32)
    misc_vec[1, 0:lr, 0:32] = in_grad


def adapt(grad, first, second, fix_one, fix_two):
    first_new = BETA_ONE * first + (1.0 - BETA_ONE) * grad
    second_new = BETA_TWO * second + (1.0 - BETA_TWO) * grad * grad
    direction = first_new * fix_one / (jnp.sqrt(second_new * fix_two) + ADAM_EPS)
    return first_new, second_new, direction


def update_of(grad, first, second, weight, fix_one, fix_two):
    first_new, second_new, direction = adapt(grad, first, second, fix_one, fix_two)
    return first_new, second_new, direction + DECAY * weight


def matrix_parts(lr):
    parts = []
    for k in range(4):
        for h in range(2):
            parts.append((1 + k, "conv", k, slice(h * HALF, (h + 1) * HALF), h,
                          slice(k * lr, (k + 1) * lr), slice(0, HALF)))
    for k in range(2):
        for j in range(4):
            top = (j % 2) * 2 * lr + k * lr
            parts.append((5 + k, "temb", k, slice(j * 128, (j + 1) * 128), j // 2,
                          slice(top, top + lr), slice(HALF + 128, MAIN)))
    for k in range(4):
        for h in range(2):
            parts.append((7 + k, "attn", k, slice(h * 128, (h + 1) * 128), h,
                          slice(k * lr, (k + 1) * lr), slice(HALF, HALF + 128)))
    return parts


def reduce_kernel(n, lr, dp, nx, fixes, main, misc_out, misc_vec, w_in, m_in, v_in, conv_w, conv_m, conv_v,
                  temb_w, temb_m, temb_v, attn_w, attn_m, attn_v, out_w, out_m, out_v,
                  gmain, gout, gvec, norms,
                  one_main, one_out, one_vec, two_main, two_out, two_vec, last_main, last_out, last_vec,
                  mine, others, send_one, recv_one, send_two, recv_two, send_three, recv_three,
                  sum_send, sum_recv):
    me = lax.axis_index("chan")
    part = lax.axis_index("dp")
    x, core = part // 2, part % 2
    sibling = (x * 2 + 1 - core, me)

    barrier = pltpu.get_barrier_semaphore()
    for k in range(1, n):
        pl.semaphore_signal(barrier, inc=1, device_id=(part, lax.rem(me + k, n)), device_id_type=MESH)
    for m in range(1, nx):
        pl.semaphore_signal(barrier, inc=1, device_id=(lax.rem(x + m, nx) * 2 + core, me), device_id_type=MESH)
    pl.semaphore_signal(barrier, inc=1, device_id=sibling, device_id_type=MESH)
    pl.semaphore_wait(barrier, n + nx - 1)

    def remote(src, dst, send_sem, recv_sem, target):
        return pltpu.make_async_remote_copy(
            src_ref=src, dst_ref=dst, send_sem=send_sem, recv_sem=recv_sem,
            device_id=target, device_id_type=MESH,
        )

    trio = ((main, one_main, two_main, last_main), (misc_out, one_out, two_out, last_out),
            (misc_vec, one_vec, two_vec, last_vec))
    first = []
    for i, (source, landed, slots, last) in enumerate(trio):
        copy = remote(source.at[1 - core], landed, send_one.at[i], recv_one.at[i], sibling)
        copy.start()
        first.append(copy)
    second = []
    for i, (source, landed, slots, last) in enumerate(trio):
        first[i].wait_recv()
        slots[x] = (source[core].astype(F32) + landed[...].astype(F32)).astype(slots.dtype)
        for m in range(1, nx):
            copy = remote(slots.at[x], slots.at[x], send_two.at[i, m - 1], recv_two.at[i, m - 1],
                          (lax.rem(x + m, nx) * 2 + core, me))
            copy.start()
            second.append(copy)
    third = []
    for i, (source, landed, slots, last) in enumerate(trio):
        for m in range(1, nx):
            sender = lax.rem(x - m + nx, nx)
            remote(slots.at[sender], slots.at[sender], send_two.at[i, m - 1], recv_two.at[i, m - 1],
                   (sender * 2 + core, me)).wait_recv()
        summed = slots[0].astype(F32)
        for m in range(1, nx):
            summed = summed + slots[m].astype(F32)
        last[core] = summed.astype(last.dtype)
        copy = remote(last.at[core], last.at[core], send_three.at[i], recv_three.at[i], sibling)
        copy.start()
        third.append(copy)
    for i, (source, landed, slots, last) in enumerate(trio):
        remote(last.at[1 - core], last.at[1 - core], send_three.at[i], recv_three.at[i], sibling).wait_recv()
    gmain[...] = last_main[...].astype(F32)
    gout[...] = last_out[...]
    gvec[...] = last_vec[...]

    fix_one, fix_two = fixes[0], fixes[1]
    arrays = {"conv": (conv_w, conv_m, conv_v), "temb": (temb_w, temb_m, temb_v), "attn": (attn_w, attn_m, attn_v)}

    def squares(value):
        return jnp.sum(jnp.sum(value * value, axis=1, keepdims=True), axis=0, keepdims=True)

    sums = {}

    def note(number, weight, update):
        pair = (squares(weight), squares(update))
        if number in sums:
            pair = (sums[number][0] + pair[0], sums[number][1] + pair[1])
        sums[number] = pair

    for number, name, k, lanes, h, rows, held in matrix_parts(lr):
        w_ref, m_ref, v_ref = arrays[name]
        weight = w_ref[k, :, lanes]
        update = update_of(gmain[h, rows, held], m_ref[k, :, lanes], v_ref[k, :, lanes], weight, fix_one, fix_two)[2]
        note(number, weight, update)
    weight = w_in[...]
    note(0, weight, update_of(gvec[1, 0:lr, 0:27], m_in[...], v_in[...], weight, fix_one, fix_two)[2])
    for h in range(2):
        lanes = slice(h * HALF, (h + 1) * HALF)
        weight = out_w[:, lanes]
        note(11, weight, update_of(gout[h, 0:3, :], out_m[:, lanes], out_v[:, lanes], weight, fix_one, fix_two)[2])

    row = iota((SUM_ROWS, 128), 0)
    lane = iota((SUM_ROWS, 128), 1)
    table = jnp.zeros((SUM_ROWS, 128), F32)
    for number in range(11):
        for side in range(2):
            table = jnp.where((row == number) & (lane == side), sums[number][side], table)
    mine[...] = table
    copies = []
    for k in range(1, n):
        copy = remote(mine, others.at[me], sum_send.at[k - 1], sum_recv.at[k - 1], (part, lax.rem(me + k, n)))
        copy.start()
        copies.append(copy)
    others[me] = table
    for k in range(1, n):
        src = lax.rem(me - k + n, n)
        remote(mine, others.at[src], sum_send.at[k - 1], sum_recv.at[k - 1], (part, src)).wait_recv()
    total = others[0]
    for k in range(1, n):
        total = total + others[k]
    for side in range(2):
        total = jnp.where((row == 11) & (lane == side), sums[11][side], total)
    norms[...] = total
    for copy in first + second + third + copies:
        copy.wait_send()


def update_kernel(lr, fixes, gmain, gout, gvec, norms, w_in, m_in, v_in, conv_w, conv_m, conv_v,
                  temb_w, temb_m, temb_v, attn_w, attn_m, attn_v, out_w, out_m, out_v, vectors, vec_m, vec_v,
                  norms_new, in_new, in_first, in_second, conv_new, conv_first, conv_second, conv_low,
                  temb_new, temb_first, temb_second, temb_low, attn_new, attn_first, attn_second, attn_low,
                  out_new, out_first, out_second, vec_new, vec_first, vec_second, attn_grad):
    fix_one, fix_two = fixes[0], fixes[1]
    norms_new[...] = jnp.sqrt(norms[0:12, 0:2])

    def ratio(number):
        squares = norms[number:number + 1, 0:2]
        return RATE * jnp.sqrt(squares[:, 0:1] / (squares[:, 1:2] + 1e-06))

    arrays = {
        "conv": (conv_w, conv_m, conv_v, conv_new, conv_first, conv_second, conv_low),
        "temb": (temb_w, temb_m, temb_v, temb_new, temb_first, temb_second, temb_low),
        "attn": (attn_w, attn_m, attn_v, attn_new, attn_first, attn_second, attn_low),
    }
    for number, name, k, lanes, h, rows, held in matrix_parts(lr):
        w_ref, m_ref, v_ref, new_ref, first_ref, second_ref, low_ref = arrays[name]
        weight = w_ref[k, :, lanes]
        grad = gmain[h, rows, held]
        first, second, update = update_of(grad, m_ref[k, :, lanes], v_ref[k, :, lanes], weight, fix_one, fix_two)
        new = weight - ratio(number) * update
        first_ref[k, :, lanes] = first
        second_ref[k, :, lanes] = second
        new_ref[k, :, lanes] = new
        low_ref[k, :, lanes] = new.astype(BF16)
        if name == "attn":
            attn_grad[k, :, lanes] = grad
    weight = w_in[...]
    first, second, update = update_of(gvec[1, 0:lr, 0:27], m_in[...], v_in[...], weight, fix_one, fix_two)
    in_new[...] = weight - ratio(0) * update
    in_first[...] = first
    in_second[...] = second
    for h in range(2):
        lanes = slice(h * HALF, (h + 1) * HALF)
        weight = out_w[:, lanes]
        first, second, update = update_of(gout[h, 0:3, :], out_m[:, lanes], out_v[:, lanes], weight, fix_one, fix_two)
        out_new[:, lanes] = weight - ratio(11) * update
        out_first[:, lanes] = first
        out_second[:, lanes] = second
    first, second, direction = adapt(gvec[0, 0:VEC_ROWS, 0:lr], vec_m[...], vec_v[...], fix_one, fix_two)
    vec_new[...] = vectors[...] - RATE * direction
    vec_first[...] = first
    vec_second[...] = second


def vmem(count):
    return [pl.BlockSpec(memory_space=pltpu.VMEM)] * count


def smem(count):
    return [pl.BlockSpec(memory_space=pltpu.SMEM)] * count


def anywhere(count):
    return [pl.BlockSpec(memory_space=pl.ANY)] * count


def shape(dims, kind=F32):
    return jax.ShapeDtypeStruct(dims, kind)


def per_device(n, dp, canvas, crop_boxes, time_steps, noise_field, step_count, w_in, m_in, v_in,
               conv_w, conv_m, conv_v, temb_w, temb_m, temb_v, attn_w, attn_m, attn_v,
               out_w, out_m, out_v, vectors, vec_m, vec_v):
    images = canvas.shape[0]
    rows_all = images * PIX
    lr = conv_w.shape[1]
    nx = dp // 2
    ny = 1 << ((n.bit_length() - 2) // 2)
    nz = n // ny
    width = 128 * -(-(LANES // 128) // dp)

    steps = time_steps.astype(F32)
    phase = (steps / 1000.0 + 0.008) / 1.008
    alpha_bar = jnp.cos(phase * (math.pi / 2)) ** 2
    coefs = jnp.stack([jnp.sqrt(alpha_bar), jnp.sqrt(1.0 - alpha_bar)])
    frequency = jnp.exp(-math.log(10000.0) * jnp.arange(TEMB // 2, dtype=F32) / (TEMB // 2))
    angles = steps[:, None] * frequency[None, :]
    embedding = jnp.concatenate([jnp.sin(angles), jnp.cos(angles)], axis=1)
    temb_act = jnp.pad(jax.nn.silu(embedding), ((0, 16 - images), (0, 0))).astype(BF16)
    count_step = step_count[0].astype(F32)
    fixes = jnp.stack([1.0 / (1.0 - BETA_ONE ** count_step), 1.0 / (1.0 - BETA_TWO ** count_step)])

    shard, small, count, out_taps = pl.pallas_call(
        functools.partial(prep_kernel, lr, images),
        out_shape=(shape((4 * lr, dp * width), BF16), shape((16, 128)), shape((8, 128)), shape((72, C))),
        in_specs=smem(1) + vmem(7),
        out_specs=vmem(4),
        scratch_shapes=[pltpu.VMEM((32, 128), F32), pltpu.VMEM((128, 128), F32), pltpu.VMEM((16, HALF), F32)],
        compiler_params=pltpu.CompilerParams(vmem_limit_bytes=32 * MIB),
        name="prep",
    )(crop_boxes, conv_w, attn_w, w_in, temb_w, temb_act, vectors, out_w)

    dma = pltpu.SemaphoreType.DMA
    whole, smalls, counts = pl.pallas_call(
        functools.partial(gather_kernel, n, ny, nz, nx, dp, width),
        out_shape=(shape((n, 4 * lr, dp * width), BF16), shape((n, 16, 128)), shape((dp, 8, 128))),
        in_specs=anywhere(3),
        out_specs=anywhere(3),
        scratch_shapes=[
            dma((3,)), dma((n - 1,)), dma((n - 1,)),
            dma((max(nx - 1, 1), n - 1)), dma((max(nx - 1, 1), n - 1)), dma((nx, n - 1)), dma((nx, n - 1)),
            dma((n - 1,)), dma((n - 1,)), dma((dp - 1,)), dma((dp - 1,)),
        ],
        compiler_params=pltpu.CompilerParams(collective_id=1, has_side_effects=True),
        name="gather",
    )(shard, small, count)

    main, misc_out, misc_vec = pl.pallas_call(
        functools.partial(compute_kernel, n, lr, dp, images),
        out_shape=(shape((2, 4 * lr, MAIN), BF16), shape((2, 8, HALF)), shape((2, 32, 128))),
        in_specs=smem(2) + vmem(7),
        out_specs=vmem(3),
        scratch_shapes=[
            pltpu.VMEM((32, C), F32), pltpu.VMEM((32, C), F32), pltpu.VMEM((2, rows_all, C), F32),
            pltpu.VMEM((6, rows_all, C), F32), pltpu.VMEM((6, rows_all, C), F32),
            pltpu.VMEM((-(-6 * images // 8) * 8, C), F32),
            pltpu.VMEM((rows_all, KW), BF16), pltpu.VMEM((rows_all, KW), BF16),
            pltpu.VMEM((rows_all, KW), BF16), pltpu.VMEM((rows_all, KW), BF16),
            pltpu.VMEM((32, rows_all), BF16), pltpu.VMEM((32, rows_all), F32),
            pltpu.VMEM((2, rows_all, C), BF16),
            pltpu.VMEM((rows_all, C), BF16), pltpu.VMEM((rows_all, C), BF16), pltpu.VMEM((rows_all, C), BF16),
            pltpu.VMEM((images, PIX, PIX), F32), pltpu.VMEM((rows_all, C), BF16),
            pltpu.VMEM((32, C), F32), pltpu.VMEM((4 * lr, LANES + C), F32), pltpu.VMEM((16, C), F32),
        ],
        compiler_params=pltpu.CompilerParams(vmem_limit_bytes=56 * MIB),
        name="compute",
    )(crop_boxes, coefs, whole, smalls, counts, out_taps, temb_act, canvas, noise_field)

    state = (w_in, m_in, v_in, conv_w, conv_m, conv_v, temb_w, temb_m, temb_v, attn_w, attn_m, attn_v,
             out_w, out_m, out_v)
    half_main, half_out, half_vec = (4 * lr, MAIN), (8, HALF), (32, 128)
    gmain, gout, gvec, norms = pl.pallas_call(
        functools.partial(reduce_kernel, n, lr, dp, nx),
        out_shape=(shape((2,) + half_main), shape((2,) + half_out), shape((2,) + half_vec),
                   shape((SUM_ROWS, 128))),
        in_specs=smem(1) + vmem(3 + len(state)),
        out_specs=vmem(4),
        scratch_shapes=[
            pltpu.VMEM(half_main, BF16), pltpu.VMEM(half_out, F32), pltpu.VMEM(half_vec, F32),
            pltpu.VMEM((nx,) + half_main, BF16), pltpu.VMEM((nx,) + half_out, F32), pltpu.VMEM((nx,) + half_vec, F32),
            pltpu.VMEM((2,) + half_main, BF16), pltpu.VMEM((2,) + half_out, F32), pltpu.VMEM((2,) + half_vec, F32),
            pltpu.VMEM((SUM_ROWS, 128), F32), pltpu.VMEM((n, SUM_ROWS, 128), F32),
            dma((3,)), dma((3,)), dma((3, max(nx - 1, 1))), dma((3, max(nx - 1, 1))), dma((3,)), dma((3,)),
            dma((n - 1,)), dma((n - 1,)),
        ],
        compiler_params=pltpu.CompilerParams(
            collective_id=2, has_side_effects=True, vmem_limit_bytes=40 * MIB
        ),
        name="reduce",
    )(fixes, main, misc_out, misc_vec, *state)

    outs = [shape((12, 2))]
    for array, low in ((w_in, False), (conv_w, True), (temb_w, True), (attn_w, True), (out_w, False), (vectors, False)):
        outs += [shape(array.shape)] * 3
        if low:
            outs.append(shape(array.shape, BF16))
    outs.append(shape(attn_w.shape))
    updated = pl.pallas_call(
        functools.partial(update_kernel, lr),
        out_shape=tuple(outs),
        in_specs=smem(1) + vmem(4 + len(state) + 3),
        out_specs=vmem(len(outs)),
        compiler_params=pltpu.CompilerParams(vmem_limit_bytes=40 * MIB),
        name="update",
    )(fixes, gmain, gout, gvec, norms, *state, vectors, vec_m, vec_v)
    return (gvec[0, LOSS_ROW, 0],) + tuple(updated)


def solution(mesh):
    chan_row = P("chan", None)
    chan_mid = P(None, "chan", None)
    chan_vec = P(None, "chan")
    return jax.shard_map(
        functools.partial(per_device, mesh.shape["chan"], mesh.shape["dp"]),
        mesh=mesh,
        in_specs=(P("dp", None, None, None), P("dp", None), P("dp"), P(None, "dp", None), P())
        + (chan_row,) * 3 + (chan_mid,) * 9 + (P(),) * 3 + (chan_vec,) * 3,
        out_specs=(P(), P()) + (chan_row,) * 3 + (chan_mid,) * 12 + (P(),) * 3 + (chan_vec,) * 3 + (chan_mid,),
        check_vma=False,
    )
```

time: 1550 us -> 118 us (0.08)
  local copies, waits for them, and re-layouts: 583 us -> 12.6 us
  waiting for transfers between devices: 466 us -> 0 us
  blocking collectives: 259 us -> 0 us
  other arithmetic: 159 us -> 1.55 us
  Pallas kernels: 0 us -> 101 us
  matrix products: 48.2 us -> 0 us
  between operations: 20.6 us -> 1.79 us
    reduce_scatter x5 -> x0, waiting for transfers between devices: 276 us -> none  [linear_back(): lax.psum_scatter(from_columns(part_columns, images) if kernel == 3 else p...]
    reshape x20 -> x0, local copies, waits for them, and re-layouts: 259 us -> none  [the longest x11 251 us: to_columns(): return jnp.stack(shifted, axis=1).reshape(field_depth * 9, images * HW * HW)]
    all_gather x7 -> x0, blocking collectives: 222 us -> none  [gather_act(): return lax.all_gather(value_low, 'chan', axis=0, tiled=True)]
    another operation x25 -> x0, local copies, waits for them, and re-layouts: 204 us -> none  [to_columns(): return jnp.stack(shifted, axis=1).reshape(field_depth * 9, images * HW * HW)]
    psum x3 -> x0, waiting for transfers between devices: 145 us -> none  [the longest x1 65.6 us: attn_backward(): lax.psum((partial_scores(query, key_part, images), probs_part), 'chan')]
    pallas_call x0 -> x5, Pallas kernels: none -> 101 us  [the longest x1 44.1 us: per_device(): pl.pallas_call(functools.partial(gather_kernel, n, ny, nz, nx, dp, width)...]
    add_any x10 -> x0, other arithmetic: 69.8 us -> none  [to_columns(): padded[:, :, row_off:row_off + HW, col_off:col_off + HW]]
    dot_general x33 -> x0, matrix products: 48.2 us -> none  [the longest x6 14.5 us: linear_back(): lax.dot_general(weight_low, grad_low, CONTRACT_COLS, preferred_element_ty...]
  transfers between devices with their start and end apart: 9 -> 0, of which waited for: 9 -> 0; matrix products, arithmetic and copies ran while one was open for 5% -> 0% of each run, Pallas kernels for 0% -> 0%
where the time goes in v1:
time: 118 us; the launch traced here: 117 us
  Pallas kernels  101 us (86%)
  local copies, waits for them, and re-layouts  12.6 us (11%)
  between operations  1.79 us (2%)
  other arithmetic  1.55 us (1%)
    pallas_call x1, Pallas kernels, per_device(): pl.pallas_call(functools.partial(gather_kernel, n, ny, nz, nx, dp, width)...  44.1 us
    pallas_call x1, Pallas kernels, per_device(): pl.pallas_call(functools.partial(compute_kernel, n, lr, dp, images), out_...  26.3 us
    pallas_call x1, Pallas kernels, per_device(): pl.pallas_call(functools.partial(reduce_kernel, n, lr, dp, nx), out_shape...  23.7 us
    unnamed x69, local copies, waits for them, and re-layouts  12.1 us
    pallas_call x1, Pallas kernels, per_device(): pl.pallas_call(functools.partial(update_kernel, lr), out_shape=tuple(outs...  4.34 us
    pallas_call x1, Pallas kernels, per_device(): pl.pallas_call(functools.partial(prep_kernel, lr, images), out_shape=(sha...  2.93 us

profile of v1, /device:TPU:0, one launch (start us, length us, event | category | flops | bytes accessed | tf_op | source)
XLA Modules:
  0.0 117.3 jit_solution(2947542094744702955)
XLA Ops:
  0.7 0.0 copy-start.33
  0.7 0.7 convert_element_type.11
  1.4 0.1 multiply_sine_fusion
  1.6 0.0 copy-start
  1.6 1.3 %copy-done = f32[4,32,2304]{2,1,0:T(8,128)S(1)} copy-done((f32[4,32,2304]{2,1,0:T(8,128)S(1)}, f32[4,32,2304]{2,1,0:T(8,128)}, u32[]{:S(2)}) %copy-start) | copy-done | bytes 1179672
  2.8 0.0 copy-start.4
  2.8 0.9 copy-done.4
  3.7 0.0 copy-start.6
  3.7 0.9 copy-done.6
  4.6 0.0 copy-start.14
  4.6 0.8 copy-done.14
  5.4 0.7 copy-done.18
  6.1 0.7 copy-done.25
  6.8 0.7 copy-done.32
  7.5 2.9 %prep.1 = (bf16[128,2560]{1,0:T(8,128)(2,1)S(1)}, f32[16,128]{1,0:T(8,128)S(1)}, f32[8,128]{1,0:T(8,128)S(1)}, f32[72,256]{1,0:T(8,128)S(1)}) custom-call(s32[2,3]{1,0:T(2,128)S(1)} %copy-done.32, f32[4,32,2304]{2,1,0:T(8,128)S(1)} %copy-done, f32[4,32,256]{2,1,0:T(8,128)S(1)} %copy-done.4, f32[32,27]{1,0:T(8,128)S(1)} %copy-done.18, ...), custom_call_target="tpu_custom_call" | custom-call | tf_op jit(solution)/shard_map/prep/pallas_call | solution.py:761
  10.4 0.8 copy-done.9
  11.3 0.6 copy-done.22
  11.9 0.6 copy-done.30
  12.5 0.6 copy-done.31
  13.1 44.1 %gather.1 = (bf16[8,128,2560]{2,1,0:T(8,128)(2,1)}, f32[8,16,128]{2,1,0:T(8,128)}, f32[4,8,128]{2,1,0:T(8,128)}) custom-call(bf16[128,2560]{1,0:T(8,128)(2,1)} %copy-done.9, f32[16,128]{1,0:T(8,128)} %copy-done.30, f32[8,128]{1,0:T(8,128)} %copy-done.31), custom_call_target="tpu_custom_call" | custom-call | tf_op jit(solution)/shard_map/gather/pallas_call | solution.py:772
  57.2 0.0 copy-done.33
  57.2 0.1 sqrt_bitcast_fusion.1
  57.3 0.6 pad_maximum_fusion.1.coefs
  57.8 0.0 copy-done.20
  57.9 0.0 copy-start.5
  57.9 0.0 copy-start.7
  57.9 0.0 copy-start.10
  57.9 0.0 copy-start.11
  57.9 0.0 copy-start.12
  57.9 0.0 copy-start.13
  57.9 0.0 copy-start.15
  57.9 0.0 copy-start.16
  58.0 0.0 copy-start.17
  58.0 0.0 copy-start.19
  58.0 0.0 copy-start.23
  58.0 0.0 copy-start.24
  58.0 26.3 %compute.1 = (bf16[2,128,1408]{2,1,0:T(8,128)(2,1)}, f32[2,8,1152]{2,1,0:T(8,128)}, f32[2,32,128]{2,1,0:T(8,128)}) custom-call(s32[2,3]{1,0:T(2,128)} %crop.3, f32[2,2]{1,0:T(2,128)} %pad_maximum_fusion.1.coefs, bf16[8,128,2560]{2,1,0:T(8,128)(2,1)} %get-tuple-element.64.whole, f32[8,16,128]{2,1,0:T(8,128)} %get-tuple-element.65.smalls, ...), custom_call_target="tpu_custom_call" | custom-call | tf_op jit(solution)/shard_map/compute/pallas_call | solution.py:786
  85.1 0.1 pad_maximum_fusion.2.fixes
  85.2 0.0 copy-done.1
  85.2 0.0 copy-done.2
  85.2 0.0 copy-done.3
  85.2 0.0 copy-done.5
  85.2 0.0 copy-done.7
  85.2 0.0 copy-done.10
  85.2 0.0 copy-done.11
  85.2 0.0 copy-done.12
  85.2 0.0 copy-done.13
  85.2 0.0 copy-done.15
  85.2 0.0 copy-done.16
  85.3 0.0 copy-done.17
  85.3 0.0 copy-done.19
  85.3 0.0 copy-done.23
  85.3 0.0 copy-done.24
  85.3 0.0 copy-start.8
  85.3 1.1 copy-done.8
  86.4 0.9 copy-done.21
  87.3 0.8 copy-done.27
  88.1 23.7 %reduce.1 = (f32[2,128,1408]{2,1,0:T(8,128)S(1)}, f32[2,8,1152]{2,1,0:T(8,128)S(1)}, f32[2,32,128]{2,1,0:T(8,128)S(1)}, f32[16,128]{1,0:T(8,128)S(1)}) custom-call(f32[2]{0:T(128)S(1)} %pad_maximum_fusion.2.fixes, bf16[2,128,1408]{2,1,0:T(8,128)(2,1)S(1)} %copy-done.8, f32[2,8,1152]{2,1,0:T(8,128)S(1)} %copy-done.21, f32[2,32,128]{2,1,0:T(8,128)S(1)} %copy-done.27, ...), custom_call_target="tpu_custom_call" | custom-call | tf_op jit(solution)/shard_map/reduce/pallas_call | solution.py:810
  111.8 0.0 copy-done.26
  111.8 0.0 copy-done.28
  111.8 0.0 copy-done.29
  111.8 4.3 %update.1 = (f32[12,2]{1,0:T(8,128)S(1)}, f32[32,27]{1,0:T(8,128)}, f32[32,27]{1,0:T(8,128)}, f32[32,27]{1,0:T(8,128)}, f32[4,32,2304]{2,1,0:T(8,128)}, /*index=...) custom-call(f32[2]{0:T(128)S(1)} %pad_maximum_fusion.2.fixes, ...), custom_call_target="tpu_custom_call" | custom-call | tf_op jit(solution)/shard_map/update/pallas_call | solution.py:836
  116.2 0.6 copy.47
  116.8 0.5 slice.3
  (19 shorter events, 0.1 us)
Async XLA Ops:
  0.7 56.5 %copy-start.33 = (s32[2]{0:T(128)S(1)}, s32[2]{0:T(128)}, u32[]{:S(2)}) copy-start(s32[2]{0:T(128)} %param.25) | copy-start | bytes 28
  1.6 1.3 %copy-start = (f32[4,32,2304]{2,1,0:T(8,128)S(1)}, f32[4,32,2304]{2,1,0:T(8,128)}, u32[]{:S(2)}) copy-start(f32[4,32,2304]{2,1,0:T(8,128)} %conv_w.5) | copy-start | bytes 3538948
  2.8 0.9 copy-start.4
  3.7 0.9 copy-start.6
  4.6 0.8 copy-start.14
  5.4 0.7 copy-start.18
  6.1 0.7 copy-start.25
  6.8 0.7 copy-start.32
  7.5 50.3 %copy-start.20 = (bf16[16,512]{1,0:T(8,128)(2,1)}, bf16[16,512]{1,0:T(8,128)(2,1)S(1)}, u32[]{:S(2)}) copy-start(bf16[16,512]{1,0:T(8,128)(2,1)S(1)} %pad.5.temb_act) | copy-start | bytes 49156
  10.4 0.8 copy-start.9
  11.3 0.6 copy-start.22
  11.9 0.6 copy-start.30
  12.5 0.6 copy-start.31
  57.8 27.3 %copy-start.1 = (f32[4,32,2304]{2,1,0:T(8,128)S(1)}, f32[4,32,2304]{2,1,0:T(8,128)}, u32[]{:S(2)}) copy-start(f32[4,32,2304]{2,1,0:T(8,128)} %conv_w.5) | copy-start | bytes 3538948
  57.8 27.3 %copy-start.2 = (f32[4,32,2304]{2,1,0:T(8,128)S(1)}, f32[4,32,2304]{2,1,0:T(8,128)}, u32[]{:S(2)}) copy-start(f32[4,32,2304]{2,1,0:T(8,128)} %conv_m.3) | copy-start | bytes 3538948
  57.8 27.3 %copy-start.3 = (f32[4,32,2304]{2,1,0:T(8,128)S(1)}, f32[4,32,2304]{2,1,0:T(8,128)}, u32[]{:S(2)}) copy-start(f32[4,32,2304]{2,1,0:T(8,128)} %conv_v.3) | copy-start | bytes 3538948
  57.9 27.3 %copy-start.5 = (f32[4,32,256]{2,1,0:T(8,128)S(1)}, f32[4,32,256]{2,1,0:T(8,128)}, u32[]{:S(2)}) copy-start(f32[4,32,256]{2,1,0:T(8,128)} %attn_w.5) | copy-start | bytes 393220
  57.9 27.3 %copy-start.7 = (f32[2,32,512]{2,1,0:T(8,128)S(1)}, f32[2,32,512]{2,1,0:T(8,128)}, u32[]{:S(2)}) copy-start(f32[2,32,512]{2,1,0:T(8,128)} %temb_w.5) | copy-start | bytes 393220
  57.9 27.3 %copy-start.10 = (f32[2,32,512]{2,1,0:T(8,128)S(1)}, f32[2,32,512]{2,1,0:T(8,128)}, u32[]{:S(2)}) copy-start(f32[2,32,512]{2,1,0:T(8,128)} %temb_m.3) | copy-start | bytes 393220
  57.9 27.3 %copy-start.11 = (f32[2,32,512]{2,1,0:T(8,128)S(1)}, f32[2,32,512]{2,1,0:T(8,128)}, u32[]{:S(2)}) copy-start(f32[2,32,512]{2,1,0:T(8,128)} %temb_v.3) | copy-start | bytes 393220
  57.9 27.3 %copy-start.12 = (f32[4,32,256]{2,1,0:T(8,128)S(1)}, f32[4,32,256]{2,1,0:T(8,128)}, u32[]{:S(2)}) copy-start(f32[4,32,256]{2,1,0:T(8,128)} %attn_m.3) | copy-start | bytes 393220
  57.9 27.3 %copy-start.13 = (f32[4,32,256]{2,1,0:T(8,128)S(1)}, f32[4,32,256]{2,1,0:T(8,128)}, u32[]{:S(2)}) copy-start(f32[4,32,256]{2,1,0:T(8,128)} %attn_v.3) | copy-start | bytes 393220
  57.9 27.3 %copy-start.15 = (f32[3,2304]{1,0:T(4,128)S(1)}, f32[3,2304]{1,0:T(4,128)}, u32[]{:S(2)}) copy-start(f32[3,2304]{1,0:T(4,128)} %out_w.5) | copy-start | bytes 82948
  57.9 27.3 %copy-start.16 = (f32[3,2304]{1,0:T(4,128)S(1)}, f32[3,2304]{1,0:T(4,128)}, u32[]{:S(2)}) copy-start(f32[3,2304]{1,0:T(4,128)} %out_m.3) | copy-start | bytes 82948
  58.0 27.3 %copy-start.17 = (f32[3,2304]{1,0:T(4,128)S(1)}, f32[3,2304]{1,0:T(4,128)}, u32[]{:S(2)}) copy-start(f32[3,2304]{1,0:T(4,128)} %out_v.3) | copy-start | bytes 82948
  58.0 27.3 %copy-start.19 = (f32[32,27]{1,0:T(8,128)S(1)}, f32[32,27]{1,0:T(8,128)}, u32[]{:S(2)}) copy-start(f32[32,27]{1,0:T(8,128)} %w_in.5) | copy-start | bytes 10372
  58.0 27.3 %copy-start.23 = (f32[32,27]{1,0:T(8,128)S(1)}, f32[32,27]{1,0:T(8,128)}, u32[]{:S(2)}) copy-start(f32[32,27]{1,0:T(8,128)} %m_in.3) | copy-start | bytes 10372
  58.0 27.3 %copy-start.24 = (f32[32,27]{1,0:T(8,128)S(1)}, f32[32,27]{1,0:T(8,128)}, u32[]{:S(2)}) copy-start(f32[32,27]{1,0:T(8,128)} %v_in.3) | copy-start | bytes 10372
  85.3 1.1 copy-start.8
  86.4 0.9 copy-start.21
  87.3 0.8 copy-start.27
  88.0 23.8 %copy-start.26 = (f32[22,32]{1,0:T(8,128)S(1)}, f32[22,32]{1,0:T(8,128)}, u32[]{:S(2)}) copy-start(f32[22,32]{1,0:T(8,128)} %vectors.3) | copy-start | bytes 8452
  88.1 23.8 %copy-start.28 = (f32[22,32]{1,0:T(8,128)S(1)}, f32[22,32]{1,0:T(8,128)}, u32[]{:S(2)}) copy-start(f32[22,32]{1,0:T(8,128)} %vec_m.1) | copy-start | bytes 8452
  88.1 23.8 %copy-start.29 = (f32[22,32]{1,0:T(8,128)S(1)}, f32[22,32]{1,0:T(8,128)}, u32[]{:S(2)}) copy-start(f32[22,32]{1,0:T(8,128)} %vec_v.1) | copy-start | bytes 8452

commit v2 on v1

--- a/solution.py
+++ b/solution.py
@@ -52,170 +52,6 @@
     return jnp.where(iota((HALF, 1), 0) == wanted, 1.0, 0.0).astype(BF16)
 
 
-def prep_kernel(lr, images, crop, conv_w, attn_w, w_in, temb_w, temb_act, vectors, out_w,
-                shard, small, count, out_taps, rows_scr, in_scr, out_scr):
-    order = tap_order()
-    for k in range(4):
-        weight = conv_w[k].astype(BF16)
-        both = jnp.concatenate([weight[:, :HALF], weight[:, HALF:]], axis=0)
-        mixed = dot(both, order, NN).astype(BF16)
-        for tap in range(TAPS):
-            for h in range(2):
-                lanes = slice(tap * C + h * 128, tap * C + h * 128 + 128)
-                shard[k * lr:(k + 1) * lr, lanes] = mixed[h * lr:(h + 1) * lr, tap * 128:(tap + 1) * 128]
-        shard[k * lr:(k + 1) * lr, KW:LANES] = attn_w[k].astype(BF16)
-
-    out_scr[...] = jnp.zeros_like(out_scr)
-    for h in range(2):
-        out_scr[h * 8:h * 8 + 3, :] = out_w[:, h * HALF:(h + 1) * HALF]
-    out_mixed = dot(out_scr[...].astype(BF16), order, NN)
-    for tap in range(TAPS):
-        for h in range(2):
-            out_taps[tap * 8:tap * 8 + 8, h * 128:(h + 1) * 128] = out_mixed[
-                h * 8:h * 8 + 8, tap * 128:(tap + 1) * 128
-            ]
-
-    rows_scr[...] = jnp.zeros_like(rows_scr)
-    rows_scr[0:VEC_ROWS, 0:lr] = vectors[...]
-    for block in range(2):
-        shift = dot(temb_act[...], temb_w[block].astype(BF16), NT)
-        for b in range(images):
-            row = VEC_ROWS + block * images + b
-            rows_scr[row:row + 1, 0:lr] = (
-                shift[b:b + 1, :] + vectors[17 + block:18 + block, :]
-            ) + vectors[13 + 2 * block:14 + 2 * block, :]
-    in_scr[...] = jnp.zeros_like(in_scr)
-    in_scr[0:lr, 0:27] = w_in[...]
-    turned = in_scr[...].T
-    packed = [jnp.zeros((8, 128), F32), jnp.zeros((8, 128), F32)]
-    for g in range(4):
-        for i, rows in enumerate((rows_scr[g * 8:g * 8 + 8, :], turned[g * 8:g * 8 + 8, :])):
-            packed[i] += rows if g == 0 else pltpu.roll(rows, g * lr, 1)
-    small[0:8, :] = packed[0]
-    small[8:16, :] = packed[1]
-
-    total = jnp.int32(0)
-    for b in range(images):
-        side = jnp.minimum(jnp.maximum(crop[b, 2], 0), HW)
-        total += 3 * side * side
-    count[...] = jnp.full((8, 128), total, jnp.int32).astype(F32)
-
-
-def gather_kernel(n, ny, nz, nx, dp, width, shard, small, count, whole, smalls, counts,
-                  own_sem, near_send, near_recv, x_send, x_recv, core_send, core_recv,
-                  small_send, small_recv, count_send, count_recv):
-    me = lax.axis_index("chan")
-    part = lax.axis_index("dp")
-    z, y = me // ny, me % ny
-    x, core = part // 2, part % 2
-
-    def chan_of(k, l):
-        return lax.rem(z + k + nz, nz) * ny + lax.rem(y + l + ny, ny)
-
-    def part_of(m, c):
-        return lax.rem(x + m + nx, nx) * 2 + c
-
-    def lanes_of(p):
-        return pl.ds(pl.multiple_of(p * width, 128), width)
-
-    barrier = pltpu.get_barrier_semaphore()
-    for k in range(1, n):
-        pl.semaphore_signal(barrier, inc=1, device_id=(part, lax.rem(me + k, n)), device_id_type=MESH)
-    for k in range(1, dp):
-        pl.semaphore_signal(barrier, inc=1, device_id=(lax.rem(part + k, dp), me), device_id_type=MESH)
-
-    own = [
-        pltpu.make_async_copy(shard, whole.at[me], own_sem.at[0]),
-        pltpu.make_async_copy(small, smalls.at[me], own_sem.at[1]),
-        pltpu.make_async_copy(count, counts.at[part], own_sem.at[2]),
-    ]
-    for copy in own:
-        copy.start()
-    pl.semaphore_wait(barrier, n + dp - 2)
-
-    sends = []
-
-    def remote(src, dst, send_sem, recv_sem, target):
-        return pltpu.make_async_remote_copy(
-            src_ref=src, dst_ref=dst, send_sem=send_sem, recv_sem=recv_sem,
-            device_id=target, device_id_type=MESH,
-        )
-
-    def send(*args):
-        copy = remote(*args)
-        copy.start()
-        sends.append(copy)
-
-    mine = lanes_of(part)
-    order = [(k, l) for k in range(nz) for l in range(ny)][1:]
-    place = {kl: o for o, kl in enumerate(order)}
-
-    def slot(src, p):
-        return whole.at[src, :, lanes_of(p)]
-
-    for k in range(1, nz):
-        send(shard.at[:, mine], slot(me, part), near_send.at[place[(k, 0)]],
-             near_recv.at[place[(k, 0)]], (part, chan_of(k, 0)))
-    for l in range(1, ny):
-        send(shard.at[:, mine], slot(me, part), near_send.at[place[(0, l)]],
-             near_recv.at[place[(0, l)]], (part, chan_of(0, l)))
-    for k in range(1, n):
-        target = lax.rem(me + k, n)
-        send(small, smalls.at[me], small_send.at[k - 1], small_recv.at[k - 1], (part, target))
-    for k in range(1, dp):
-        target = lax.rem(part + k, dp)
-        send(count, counts.at[part], count_send.at[k - 1], count_recv.at[k - 1], (target, me))
-
-    def forward(kl):
-        o = place[kl]
-        src = chan_of(-kl[0], -kl[1])
-        remote(shard.at[:, mine], slot(src, part), near_send.at[o], near_recv.at[o],
-               (part, src)).wait_recv()
-        for m in range(1, nx):
-            send(slot(src, part), slot(src, part), x_send.at[m - 1, o], x_recv.at[m - 1, o],
-                 (part_of(m, core), me))
-        send(slot(src, part), slot(src, part), core_send.at[0, o], core_recv.at[0, o],
-             (part_of(0, 1 - core), me))
-
-    for k in range(1, nz):
-        src = chan_of(-k, 0)
-        o = place[(k, 0)]
-        forward((k, 0))
-        for l in range(1, ny):
-            send(slot(src, part), slot(src, part), near_send.at[place[(k, l)]],
-                 near_recv.at[place[(k, l)]], (part, chan_of(0, l)))
-    for l in range(1, ny):
-        forward((0, l))
-    for k in range(1, nz):
-        for l in range(1, ny):
-            forward((k, l))
-    for o, (k, l) in enumerate(order):
-        src = chan_of(-k, -l)
-        for m in range(1, nx):
-            p = part_of(-m, core)
-            remote(slot(src, p), slot(src, p), x_send.at[m - 1, o], x_recv.at[m - 1, o],
-                   (p, me)).wait_recv()
-            send(slot(src, p), slot(src, p), core_send.at[m, o], core_recv.at[m, o],
-                 (part_of(0, 1 - core), me))
-    for k in range(1, n):
-        src = lax.rem(me - k + n, n)
-        remote(small, smalls.at[src], small_send.at[k - 1], small_recv.at[k - 1],
-               (part, src)).wait_recv()
-    for k in range(1, dp):
-        p = lax.rem(part - k + dp, dp)
-        remote(count, counts.at[p], count_send.at[k - 1], count_recv.at[k - 1], (p, me)).wait_recv()
-    for o, (k, l) in enumerate(order):
-        src = chan_of(-k, -l)
-        for m in range(nx):
-            p = part_of(-m, 1 - core)
-            remote(slot(src, p), slot(src, p), core_send.at[m, o], core_recv.at[m, o],
-                   (part_of(0, 1 - core), me)).wait_recv()
-    for copy in sends:
-        copy.wait_send()
-    for copy in own:
-        copy.wait()
-
-
 def group_sum(row):
     lane = iota(row.shape, 1)
     step = 1
@@ -236,7 +72,7 @@
     return group_sum(wide)[0:1] * (1.0 / (GSIZE * PIX))
 
 
-def compute_kernel(n, lr, dp, images, crop, coefs, whole, smalls, counts, out_taps, temb_act,
+def compute(n, lr, dp, images, crop, coefs, whole, attn_all, smalls, counts, out_taps, temb_act,
                    canvas, noise, main, misc_out, misc_vec,
                    vec, w_in, hidden, xhat, dact, rstd, col0, col1, col2, col3, taps0, rows_scr, acts,
                    q_scr, k_scr, v_scr, probs, mixed_scr, gvec, gconv, gsum):
@@ -249,10 +85,10 @@
         return slice(b * PIX, (b + 1) * PIX)
 
     def conv_weight(k):
-        return whole[:, k * lr:(k + 1) * lr, 0:KW].reshape(C, KW)
+        return whole[:, k * lr:(k + 1) * lr, :].reshape(C, KW)
 
     def attn_weight(k):
-        return whole[:, k * lr:(k + 1) * lr, KW:LANES].reshape(C, C)
+        return attn_all[:, k * lr:(k + 1) * lr, :].reshape(C, C)
 
     vec[...] = jnp.zeros_like(vec)
     w_in[...] = jnp.zeros_like(w_in)
@@ -531,6 +367,235 @@
     misc_vec[1, 0:lr, 0:32] = in_grad
 
 
+def flip(value, mask):
+    bit = 1
+    while bit <= mask:
+        if mask & bit:
+            value = value + bit * (1 - 2 * ((value // bit) % 2))
+        bit *= 2
+    return value
+
+
+def remote(src, dst, send_sem, recv_sem, target):
+    return pltpu.make_async_remote_copy(
+        src_ref=src, dst_ref=dst, send_sem=send_sem, recv_sem=recv_sem,
+        device_id=target, device_id_type=MESH,
+    )
+
+
+def step_kernel(n, ny, nz, nx, dp, lr, images, crop, coefs, conv_hbm, attn_hbm, temb_hbm, in_hbm, out_hbm,
+                vec_hbm, temb_act, canvas, noise, main, misc_out, misc_vec,
+                conv_w, attn_w, temb_w, w_in_own, out_w, vectors,
+                whole, attn_all, smalls, counts, load_sem,
+                near_send, near_recv, x_send, x_recv, core_send, core_recv,
+                small_send, small_recv, count_send, count_recv,
+                own_rows_scr, in_scr, out_scr, out_taps, *rest):
+    me = lax.axis_index("chan")
+    part = lax.axis_index("dp")
+    z, y = me // ny, me % ny
+    x, core = part // 2, part % 2
+    sibling = (x * 2 + 1 - core, me)
+
+    loads = [
+        pltpu.make_async_copy(conv_hbm.at[k], conv_w.at[k], load_sem.at[k]) for k in range(4)
+    ] + [
+        pltpu.make_async_copy(src, dst, load_sem.at[4 + i])
+        for i, (src, dst) in enumerate(
+            ((attn_hbm, attn_w), (temb_hbm, temb_w), (in_hbm, w_in_own), (out_hbm, out_w), (vec_hbm, vectors))
+        )
+    ]
+    for load in loads:
+        load.start()
+
+    offsets = [(i, j) for i in range(nz) for j in range(ny)][1:]
+    place = {o: i for i, o in enumerate(offsets)}
+
+    def chan_at(o):
+        return flip(z, o[0]) * ny + flip(y, o[1])
+
+    barrier = pltpu.get_barrier_semaphore()
+    for o in offsets:
+        pl.semaphore_signal(barrier, inc=1, device_id=(part, chan_at(o)), device_id_type=MESH)
+    for k in range(1, dp):
+        pl.semaphore_signal(barrier, inc=1, device_id=(lax.rem(part + k, dp), me), device_id_type=MESH)
+
+    core_lanes = KW // 2
+    x_lanes = 3 * 128 if nx == 2 else 0
+    near_lanes = core_lanes - x_lanes
+    chunk_rows = max(lr, 16)
+    conv_chunks = 4 * lr // chunk_rows
+    chunks = list(range(conv_chunks)) + [None]
+
+    def rows_of(chunk):
+        return pl.ds(chunk * chunk_rows, chunk_rows)
+
+    def near_ref(chunk, src, c):
+        if chunk is None:
+            return attn_all.at[src, pl.ds(pl.multiple_of(c * 2 * lr, 16), 2 * lr), :]
+        start = c * core_lanes + x * x_lanes if x_lanes else c * core_lanes
+        return whole.at[src, rows_of(chunk), pl.ds(pl.multiple_of(start, 128), near_lanes)]
+
+    def x_ref(chunk, src, c, side):
+        start = c * core_lanes + side * near_lanes
+        return whole.at[src, rows_of(chunk), pl.ds(pl.multiple_of(start, 128), x_lanes)]
+
+    sends = []
+
+    def send(*args):
+        copy = remote(*args)
+        copy.start()
+        sends.append(copy)
+
+    def index(chunk):
+        return conv_chunks if chunk is None else chunk
+
+    def send_near(chunk, src, o, target):
+        i = index(chunk)
+        ref = near_ref(chunk, src, core)
+        send(ref, ref, near_send.at[i, place[o]], near_recv.at[i, place[o]], target)
+
+    def send_core(chunk, src, o, piece):
+        i = index(chunk)
+        ref = near_ref(chunk, src, core) if piece == 0 else x_ref(chunk, src, core, 1 - x)
+        send(ref, ref, core_send.at[piece, i, place[o]], core_recv.at[piece, i, place[o]], sibling)
+
+    def begin(chunk):
+        for i in range(1, nz):
+            send_near(chunk, me, (i, 0), (part, chan_at((i, 0))))
+        for j in range(1, ny):
+            send_near(chunk, me, (0, j), (part, chan_at((0, j))))
+
+    def near_in(chunk, o):
+        i = index(chunk)
+        src = chan_at(o)
+        ref = near_ref(chunk, src, core)
+        remote(ref, ref, near_send.at[i, place[o]], near_recv.at[i, place[o]], (part, src)).wait_recv()
+        if o[1] == 0:
+            for j in range(1, ny):
+                send_near(chunk, src, (o[0], j), (part, chan_at((0, j))))
+        if x_lanes and chunk is not None:
+            ref = x_ref(chunk, src, core, x)
+            send(ref, ref, x_send.at[i, place[o]], x_recv.at[i, place[o]], ((1 - x) * 2 + core, me))
+        send_core(chunk, src, o, 0)
+
+    def x_in(chunk, o):
+        if x_lanes and chunk is not None:
+            i = index(chunk)
+            src = chan_at(o)
+            ref = x_ref(chunk, src, core, 1 - x)
+            remote(ref, ref, x_send.at[i, place[o]], x_recv.at[i, place[o]], ((1 - x) * 2 + core, me)).wait_recv()
+            send_core(chunk, src, o, 1)
+
+    def core_in(chunk, o):
+        i = index(chunk)
+        src = chan_at(o)
+        pieces = [near_ref(chunk, src, 1 - core)]
+        if x_lanes and chunk is not None:
+            pieces.append(x_ref(chunk, src, 1 - core, 1 - x))
+        for piece, ref in enumerate(pieces):
+            remote(ref, ref, core_send.at[piece, i, place[o]], core_recv.at[piece, i, place[o]], sibling).wait_recv()
+
+    def stage_one(chunk):
+        for i in range(1, nz):
+            near_in(chunk, (i, 0))
+
+    def stage_two(chunk):
+        for j in range(1, ny):
+            near_in(chunk, (0, j))
+        for i in range(1, nz):
+            for j in range(1, ny):
+                near_in(chunk, (i, j))
+
+    def stage_three(chunk):
+        for o in offsets:
+            x_in(chunk, o)
+
+    def stage_four(chunk):
+        for o in offsets:
+            core_in(chunk, o)
+
+    order = tap_order()
+    pl.semaphore_wait(barrier, n + dp - 2)
+    begun = 0
+    for k in range(4):
+        loads[k].wait()
+        weight = conv_w[k].astype(BF16)
+        both = jnp.concatenate([weight[:, :HALF], weight[:, HALF:]], axis=0)
+        mixed = dot(both, order, NN).astype(BF16)
+        for tap in range(TAPS):
+            for h in range(2):
+                lanes = slice(tap * C + h * 128, tap * C + h * 128 + 128)
+                whole[me, k * lr:(k + 1) * lr, lanes] = mixed[h * lr:(h + 1) * lr, tap * 128:(tap + 1) * 128]
+        if (k + 1) * lr >= (begun + 1) * chunk_rows:
+            if begun < 2:
+                begin(begun)
+            begun += 1
+        if k == 0:
+            for load in loads[5:]:
+                load.wait()
+            own_rows_scr[...] = jnp.zeros_like(own_rows_scr)
+            own_rows_scr[0:VEC_ROWS, 0:lr] = vectors[...]
+            for block in range(2):
+                shift = dot(temb_act[...], temb_w[block].astype(BF16), NT)
+                for b in range(images):
+                    row = VEC_ROWS + block * images + b
+                    own_rows_scr[row:row + 1, 0:lr] = (
+                        shift[b:b + 1, :] + vectors[17 + block:18 + block, :]
+                    ) + vectors[13 + 2 * block:14 + 2 * block, :]
+            in_scr[...] = jnp.zeros_like(in_scr)
+            in_scr[0:lr, 0:27] = w_in_own[...]
+            turned = in_scr[...].T
+            packed = [jnp.zeros((8, 128), F32), jnp.zeros((8, 128), F32)]
+            for g in range(4):
+                for i, rows in enumerate((own_rows_scr[g * 8:g * 8 + 8, :], turned[g * 8:g * 8 + 8, :])):
+                    packed[i] += rows if g == 0 else pltpu.roll(rows, g * lr, 1)
+            smalls[me, 0:8, :] = packed[0]
+            smalls[me, 8:16, :] = packed[1]
+            total = jnp.int32(0)
+            for b in range(images):
+                side = jnp.minimum(jnp.maximum(crop[b, 2], 0), HW)
+                total += 3 * side * side
+            counts[part] = jnp.full((8, 128), total, jnp.int32).astype(F32)
+            for o in offsets:
+                i = place[o]
+                send(smalls.at[me], smalls.at[me], small_send.at[i], small_recv.at[i], (part, chan_at(o)))
+            for i in range(1, dp):
+                send(counts.at[part], counts.at[part], count_send.at[i - 1], count_recv.at[i - 1],
+                     (lax.rem(part + i, dp), me))
+    loads[4].wait()
+    for k in range(4):
+        attn_all[me, k * lr:(k + 1) * lr, :] = attn_w[k].astype(BF16)
+
+    out_scr[...] = jnp.zeros_like(out_scr)
+    for h in range(2):
+        out_scr[h * 8:h * 8 + 3, :] = out_w[:, h * HALF:(h + 1) * HALF]
+    out_mixed = dot(out_scr[...].astype(BF16), order, NN)
+    for tap in range(TAPS):
+        for h in range(2):
+            out_taps[tap * 8:tap * 8 + 8, h * 128:(h + 1) * 128] = out_mixed[
+                h * 8:h * 8 + 8, tap * 128:(tap + 1) * 128
+            ]
+
+    for i in range(len(chunks) + 3):
+        for stage, delay in ((stage_one, 0), (stage_two, 1), (stage_three, 2), (stage_four, 3)):
+            if 0 <= i - delay < len(chunks):
+                stage(chunks[i - delay])
+            if delay == 0 and 2 <= i + 2 < len(chunks):
+                begin(chunks[i + 2])
+    for o in offsets:
+        src = chan_at(o)
+        remote(smalls.at[src], smalls.at[src], small_send.at[place[o]], small_recv.at[place[o]],
+               (part, src)).wait_recv()
+    for i in range(1, dp):
+        p = lax.rem(part - i + dp, dp)
+        remote(counts.at[p], counts.at[p], count_send.at[i - 1], count_recv.at[i - 1], (p, me)).wait_recv()
+    for copy in sends:
+        copy.wait_send()
+
+    compute(n, lr, dp, images, crop, coefs, whole, attn_all, smalls, counts, out_taps, temb_act,
+            canvas, noise, main, misc_out, misc_vec, *rest)
+
+
 def adapt(grad, first, second, fix_one, fix_two):
     first_new = BETA_ONE * first + (1.0 - BETA_ONE) * grad
     second_new = BETA_TWO * second + (1.0 - BETA_TWO) * grad * grad
@@ -561,7 +626,19 @@
     return parts
 
 
-def reduce_kernel(n, lr, dp, nx, fixes, main, misc_out, misc_vec, w_in, m_in, v_in, conv_w, conv_m, conv_v,
+def reduce_kernel(n, lr, dp, nx, fixes, main, misc_out, misc_vec, *refs):
+    state_hbm, refs = refs[:15], refs[15:]
+    (gmain, gout, gvec, norms), refs = refs[:4], refs[4:]
+    state, refs = refs[:15], refs[15:]
+    loads = [
+        pltpu.make_async_copy(src, dst, refs[-1].at[i]) for i, (src, dst) in enumerate(zip(state_hbm, state))
+    ]
+    for load in loads:
+        load.start()
+    reduce_body(n, lr, dp, nx, loads, fixes, main, misc_out, misc_vec, *state, gmain, gout, gvec, norms, *refs[:-1])
+
+
+def reduce_body(n, lr, dp, nx, loads, fixes, main, misc_out, misc_vec, w_in, m_in, v_in, conv_w, conv_m, conv_v,
                   temb_w, temb_m, temb_v, attn_w, attn_m, attn_v, out_w, out_m, out_v,
                   gmain, gout, gvec, norms,
                   one_main, one_out, one_vec, two_main, two_out, two_vec, last_main, last_out, last_vec,
@@ -579,12 +656,6 @@
         pl.semaphore_signal(barrier, inc=1, device_id=(lax.rem(x + m, nx) * 2 + core, me), device_id_type=MESH)
     pl.semaphore_signal(barrier, inc=1, device_id=sibling, device_id_type=MESH)
     pl.semaphore_wait(barrier, n + nx - 1)
-
-    def remote(src, dst, send_sem, recv_sem, target):
-        return pltpu.make_async_remote_copy(
-            src_ref=src, dst_ref=dst, send_sem=send_sem, recv_sem=recv_sem,
-            device_id=target, device_id_type=MESH,
-        )
 
     trio = ((main, one_main, two_main, last_main), (misc_out, one_out, two_out, last_out),
             (misc_vec, one_vec, two_vec, last_vec))
@@ -621,6 +692,8 @@
     gout[...] = last_out[...]
     gvec[...] = last_vec[...]
 
+    for load in loads:
+        load.wait()
     fix_one, fix_two = fixes[0], fixes[1]
     arrays = {"conv": (conv_w, conv_m, conv_v), "temb": (temb_w, temb_m, temb_v), "attn": (attn_w, attn_m, attn_v)}
 
@@ -728,8 +801,8 @@
     return [pl.BlockSpec(memory_space=pltpu.SMEM)] * count
 
 
-def anywhere(count):
-    return [pl.BlockSpec(memory_space=pl.ANY)] * count
+def hbm(count):
+    return [pl.BlockSpec(memory_space=pltpu.HBM)] * count
 
 
 def shape(dims, kind=F32):
@@ -745,7 +818,6 @@
     nx = dp // 2
     ny = 1 << ((n.bit_length() - 2) // 2)
     nz = n // ny
-    width = 128 * -(-(LANES // 128) // dp)
 
     steps = time_steps.astype(F32)
     phase = (steps / 1000.0 + 0.008) / 1.008
@@ -758,37 +830,23 @@
     count_step = step_count[0].astype(F32)
     fixes = jnp.stack([1.0 / (1.0 - BETA_ONE ** count_step), 1.0 / (1.0 - BETA_TWO ** count_step)])
 
-    shard, small, count, out_taps = pl.pallas_call(
-        functools.partial(prep_kernel, lr, images),
-        out_shape=(shape((4 * lr, dp * width), BF16), shape((16, 128)), shape((8, 128)), shape((72, C))),
-        in_specs=smem(1) + vmem(7),
-        out_specs=vmem(4),
-        scratch_shapes=[pltpu.VMEM((32, 128), F32), pltpu.VMEM((128, 128), F32), pltpu.VMEM((16, HALF), F32)],
-        compiler_params=pltpu.CompilerParams(vmem_limit_bytes=32 * MIB),
-        name="prep",
-    )(crop_boxes, conv_w, attn_w, w_in, temb_w, temb_act, vectors, out_w)
-
     dma = pltpu.SemaphoreType.DMA
-    whole, smalls, counts = pl.pallas_call(
-        functools.partial(gather_kernel, n, ny, nz, nx, dp, width),
-        out_shape=(shape((n, 4 * lr, dp * width), BF16), shape((n, 16, 128)), shape((dp, 8, 128))),
-        in_specs=anywhere(3),
-        out_specs=anywhere(3),
-        scratch_shapes=[
-            dma((3,)), dma((n - 1,)), dma((n - 1,)),
-            dma((max(nx - 1, 1), n - 1)), dma((max(nx - 1, 1), n - 1)), dma((nx, n - 1)), dma((nx, n - 1)),
-            dma((n - 1,)), dma((n - 1,)), dma((dp - 1,)), dma((dp - 1,)),
-        ],
-        compiler_params=pltpu.CompilerParams(collective_id=1, has_side_effects=True),
-        name="gather",
-    )(shard, small, count)
-
+    chunks = 4 * lr // max(lr, 16) + 1
     main, misc_out, misc_vec = pl.pallas_call(
-        functools.partial(compute_kernel, n, lr, dp, images),
+        functools.partial(step_kernel, n, ny, nz, nx, dp, lr, images),
         out_shape=(shape((2, 4 * lr, MAIN), BF16), shape((2, 8, HALF)), shape((2, 32, 128))),
-        in_specs=smem(2) + vmem(7),
+        in_specs=smem(2) + hbm(6) + vmem(3),
         out_specs=vmem(3),
         scratch_shapes=[
+            pltpu.VMEM(conv_w.shape, F32), pltpu.VMEM(attn_w.shape, F32), pltpu.VMEM(temb_w.shape, F32),
+            pltpu.VMEM(w_in.shape, F32), pltpu.VMEM(out_w.shape, F32), pltpu.VMEM(vectors.shape, F32),
+            pltpu.VMEM((n, 4 * lr, KW), BF16), pltpu.VMEM((n, 4 * lr, C), BF16),
+            pltpu.VMEM((n, 16, 128), F32), pltpu.VMEM((dp, 8, 128), F32), dma((9,)),
+            dma((chunks, n - 1)), dma((chunks, n - 1)), dma((chunks, n - 1)), dma((chunks, n - 1)),
+            dma((2, chunks, n - 1)), dma((2, chunks, n - 1)),
+            dma((n - 1,)), dma((n - 1,)), dma((dp - 1,)), dma((dp - 1,)),
+            pltpu.VMEM((32, 128), F32), pltpu.VMEM((128, 128), F32), pltpu.VMEM((16, HALF), F32),
+            pltpu.VMEM((72, C), F32),
             pltpu.VMEM((32, C), F32), pltpu.VMEM((32, C), F32), pltpu.VMEM((2, rows_all, C), F32),
             pltpu.VMEM((6, rows_all, C), F32), pltpu.VMEM((6, rows_all, C), F32),
             pltpu.VMEM((-(-6 * images // 8) * 8, C), F32),
@@ -800,9 +858,11 @@
             pltpu.VMEM((images, PIX, PIX), F32), pltpu.VMEM((rows_all, C), BF16),
             pltpu.VMEM((32, C), F32), pltpu.VMEM((4 * lr, LANES + C), F32), pltpu.VMEM((16, C), F32),
         ],
-        compiler_params=pltpu.CompilerParams(vmem_limit_bytes=56 * MIB),
-        name="compute",
-    )(crop_boxes, coefs, whole, smalls, counts, out_taps, temb_act, canvas, noise_field)
+        compiler_params=pltpu.CompilerParams(
+            collective_id=1, has_side_effects=True, vmem_limit_bytes=56 * MIB
+        ),
+        name="step",
+    )(crop_boxes, coefs, conv_w, attn_w, temb_w, w_in, out_w, vectors, temb_act, canvas, noise_field)
 
     state = (w_in, m_in, v_in, conv_w, conv_m, conv_v, temb_w, temb_m, temb_v, attn_w, attn_m, attn_v,
              out_w, out_m, out_v)
@@ -811,15 +871,15 @@
         functools.partial(reduce_kernel, n, lr, dp, nx),
         out_shape=(shape((2,) + half_main), shape((2,) + half_out), shape((2,) + half_vec),
                    shape((SUM_ROWS, 128))),
-        in_specs=smem(1) + vmem(3 + len(state)),
+        in_specs=smem(1) + vmem(3) + hbm(len(state)),
         out_specs=vmem(4),
-        scratch_shapes=[
+        scratch_shapes=[pltpu.VMEM(array.shape, F32) for array in state] + [
             pltpu.VMEM(half_main, BF16), pltpu.VMEM(half_out, F32), pltpu.VMEM(half_vec, F32),
             pltpu.VMEM((nx,) + half_main, BF16), pltpu.VMEM((nx,) + half_out, F32), pltpu.VMEM((nx,) + half_vec, F32),
             pltpu.VMEM((2,) + half_main, BF16), pltpu.VMEM((2,) + half_out, F32), pltpu.VMEM((2,) + half_vec, F32),
             pltpu.VMEM((SUM_ROWS, 128), F32), pltpu.VMEM((n, SUM_ROWS, 128), F32),
             dma((3,)), dma((3,)), dma((3, max(nx - 1, 1))), dma((3, max(nx - 1, 1))), dma((3,)), dma((3,)),
-            dma((n - 1,)), dma((n - 1,)),
+            dma((n - 1,)), dma((n - 1,)), dma((len(state),)),
         ],
         compiler_params=pltpu.CompilerParams(
             collective_id=2, has_side_effects=True, vmem_limit_bytes=40 * MIB

time: 118 us -> 106 us (0.90)
  Pallas kernels: 101 us -> 90.5 us
  local copies, waits for them, and re-layouts: 12.6 us -> 11.1 us
    pallas_call x3 -> x1, Pallas kernels: 73.3 us -> 62.5 us  [per_device(): pl.pallas_call(functools.partial(step_kernel, n, ny, nz, nx, dp, lr, imag...]
    unnamed x69 -> x43, local copies, waits for them, and re-layouts: 12.1 us -> 10 us
where the time goes in v2:
time: 106 us
  Pallas kernels  90.5 us (85%)
  local copies, waits for them, and re-layouts  11.1 us (10%)
  other arithmetic  2.27 us (2%)
  between operations  1.66 us (2%)
    pallas_call x1, Pallas kernels, per_device(): pl.pallas_call(functools.partial(step_kernel, n, ny, nz, nx, dp, lr, imag...  62.5 us
    pallas_call x1, Pallas kernels, per_device(): pl.pallas_call(functools.partial(reduce_kernel, n, lr, dp, nx), out_shape...  23.7 us
    unnamed x43, local copies, waits for them, and re-layouts  10 us
    pallas_call x1, Pallas kernels, per_device(): pl.pallas_call(functools.partial(update_kernel, lr), out_shape=tuple(outs...  4.35 us

profile of v2, /device:TPU:0, one launch (start us, length us, event | category | flops | bytes accessed | tf_op | source)
XLA Modules:
  0.0 105.6 jit_solution(14184405300160139225)
XLA Ops:
  0.7 0.0 copy-start.13
  0.7 0.0 copy-start
  0.7 0.0 copy-start.4
  0.7 0.0 copy-start.3
  0.7 0.0 copy-start.10
  0.7 0.0 copy-start.6
  0.7 0.0 copy-start.7
  0.7 0.0 copy-start.11
  0.8 0.8 convert_element_type.11
  1.5 0.1 multiply_sine_fusion
  1.7 0.6 pad.5.temb_act
  2.3 0.7 sqrt_bitcast_fusion.1
  3.0 0.6 pad_maximum_fusion.1.coefs
  3.6 62.5 %step.1 = (bf16[2,128,1408]{2,1,0:T(8,128)(2,1)}, f32[2,8,1152]{2,1,0:T(8,128)}, f32[2,32,128]{2,1,0:T(8,128)}) custom-call(s32[2,3]{1,0:T(2,128)} %crop.1, f32[2,2]{1,0:T(2,128)} %pad_maximum_fusion.1.coefs, f32[4,32,2304]{2,1,0:T(8,128)} %conv_w.1, f32[4,32,256]{2,1,0:T(8,128)} %attn_w.1, f32[2,32,512]{2,1,0:T(8,128)} %temb_w.1, f32[32,27]{1,0:T(8,128)} %w_in.1, ...), custom_call_target="tpu_custom_call" | custom-call | tf_op jit(solution)/shard_map/step/pallas_call | solution.py:835
  66.9 0.1 pad_maximum_fusion.2.fixes
  67.0 0.0 copy-done.13
  67.0 0.0 copy-done
  67.0 0.0 copy-done.4
  67.0 0.0 copy-done.3
  67.0 0.0 copy-done.10
  67.0 0.0 copy-done.6
  67.0 0.0 copy-done.7
  67.0 0.0 copy-done.11
  67.0 0.0 copy-start.1
  67.0 1.3 %copy-done.1 = f32[4,32,2304]{2,1,0:T(8,128)S(1)} copy-done((f32[4,32,2304]{2,1,0:T(8,128)S(1)}, f32[4,32,2304]{2,1,0:T(8,128)}, u32[]{:S(2)}) %copy-start.1) | copy-done | bytes 1179672
  68.3 0.0 copy-start.2
  68.3 1.3 %copy-done.2 = f32[4,32,2304]{2,1,0:T(8,128)S(1)} copy-done((f32[4,32,2304]{2,1,0:T(8,128)S(1)}, f32[4,32,2304]{2,1,0:T(8,128)}, u32[]{:S(2)}) %copy-start.2) | copy-done | bytes 1179672
  69.6 0.0 copy-start.5
  69.6 1.1 %copy-done.5 = bf16[2,128,1408]{2,1,0:T(8,128)(2,1)S(1)} copy-done((bf16[2,128,1408]{2,1,0:T(8,128)(2,1)S(1)}, bf16[2,128,1408]{2,1,0:T(8,128)(2,1)}, u32[]{:S(2)}) %copy-start.5) | copy-done | bytes 720920
  70.7 0.0 copy-start.8
  70.7 0.9 copy-done.8
  71.6 0.0 copy-start.9
  71.6 0.9 copy-done.9
  72.5 0.0 copy-start.12
  72.5 0.8 copy-done.12
  73.2 0.0 copy-start.14
  73.3 0.9 copy-done.14
  74.1 0.0 copy-start.15
  74.1 0.7 copy-done.15
  74.9 0.0 copy-start.16
  74.9 0.7 copy-done.16
  75.6 0.0 copy-start.18
  75.6 0.8 copy-done.18
  76.3 0.0 copy-start.17
  76.3 0.0 copy-start.19
  76.3 0.0 copy-start.20
  76.3 23.7 %reduce.1 = (f32[2,128,1408]{2,1,0:T(8,128)S(1)}, f32[2,8,1152]{2,1,0:T(8,128)S(1)}, f32[2,32,128]{2,1,0:T(8,128)S(1)}, f32[16,128]{1,0:T(8,128)S(1)}) custom-call(f32[2]{0:T(128)S(1)} %pad_maximum_fusion.2.fixes, bf16[2,128,1408]{2,1,0:T(8,128)(2,1)S(1)} %copy-done.5, f32[2,8,1152]{2,1,0:T(8,128)S(1)} %copy-done.14, f32[2,32,128]{2,1,0:T(8,128)S(1)} %copy-done.18, ...), custom_call_target="tpu_custom_call" | custom-call | tf_op jit(solution)/shard_map/reduce/pallas_call | solution.py:870
  100.0 0.0 copy-done.17
  100.1 0.0 copy-done.19
  100.1 0.0 copy-done.20
  100.1 4.3 %update.1 = (f32[12,2]{1,0:T(8,128)S(1)}, f32[32,27]{1,0:T(8,128)}, f32[32,27]{1,0:T(8,128)}, f32[32,27]{1,0:T(8,128)}, f32[4,32,2304]{2,1,0:T(8,128)}, /*index=...) custom-call(f32[2]{0:T(128)S(1)} %pad_maximum_fusion.2.fixes, ...), custom_call_target="tpu_custom_call" | custom-call | tf_op jit(solution)/shard_map/update/pallas_call | solution.py:896
  104.4 0.6 copy.47
  105.1 0.5 slice.3
  (2 shorter events, 0.0 us)
Async XLA Ops:
  0.7 66.3 %copy-start.13 = (f32[32,27]{1,0:T(8,128)S(1)}, f32[32,27]{1,0:T(8,128)}, u32[]{:S(2)}) copy-start(f32[32,27]{1,0:T(8,128)} %w_in.1) | copy-start | bytes 10372
  0.7 66.3 %copy-start = (f32[4,32,2304]{2,1,0:T(8,128)S(1)}, f32[4,32,2304]{2,1,0:T(8,128)}, u32[]{:S(2)}) copy-start(f32[4,32,2304]{2,1,0:T(8,128)} %conv_w.1) | copy-start | bytes 3538948
  0.7 66.3 %copy-start.4 = (f32[2,32,512]{2,1,0:T(8,128)S(1)}, f32[2,32,512]{2,1,0:T(8,128)}, u32[]{:S(2)}) copy-start(f32[2,32,512]{2,1,0:T(8,128)} %temb_w.1) | copy-start | bytes 393220
  0.7 66.3 %copy-start.3 = (f32[4,32,256]{2,1,0:T(8,128)S(1)}, f32[4,32,256]{2,1,0:T(8,128)}, u32[]{:S(2)}) copy-start(f32[4,32,256]{2,1,0:T(8,128)} %attn_w.1) | copy-start | bytes 393220
  0.7 66.3 %copy-start.10 = (f32[3,2304]{1,0:T(4,128)S(1)}, f32[3,2304]{1,0:T(4,128)}, u32[]{:S(2)}) copy-start(f32[3,2304]{1,0:T(4,128)} %out_w.1) | copy-start | bytes 82948
  0.7 66.3 %copy-start.6 = (f32[2,32,512]{2,1,0:T(8,128)S(1)}, f32[2,32,512]{2,1,0:T(8,128)}, u32[]{:S(2)}) copy-start(f32[2,32,512]{2,1,0:T(8,128)} %temb_m.1) | copy-start | bytes 393220
  0.7 66.3 %copy-start.7 = (f32[2,32,512]{2,1,0:T(8,128)S(1)}, f32[2,32,512]{2,1,0:T(8,128)}, u32[]{:S(2)}) copy-start(f32[2,32,512]{2,1,0:T(8,128)} %temb_v.1) | copy-start | bytes 393220
  0.7 66.3 %copy-start.11 = (f32[3,2304]{1,0:T(4,128)S(1)}, f32[3,2304]{1,0:T(4,128)}, u32[]{:S(2)}) copy-start(f32[3,2304]{1,0:T(4,128)} %out_m.1) | copy-start | bytes 82948
  67.0 1.3 %copy-start.1 = (f32[4,32,2304]{2,1,0:T(8,128)S(1)}, f32[4,32,2304]{2,1,0:T(8,128)}, u32[]{:S(2)}) copy-start(f32[4,32,2304]{2,1,0:T(8,128)} %conv_m.1) | copy-start | bytes 3538948
  68.3 1.3 %copy-start.2 = (f32[4,32,2304]{2,1,0:T(8,128)S(1)}, f32[4,32,2304]{2,1,0:T(8,128)}, u32[]{:S(2)}) copy-start(f32[4,32,2304]{2,1,0:T(8,128)} %conv_v.1) | copy-start | bytes 3538948
  69.6 1.1 %copy-start.5 = (bf16[2,128,1408]{2,1,0:T(8,128)(2,1)S(1)}, bf16[2,128,1408]{2,1,0:T(8,128)(2,1)}, u32[]{:S(2)}) copy-start(bf16[2,128,1408]{2,1,0:T(8,128)(2,1)} %get-tuple-element.54.main) | copy-start | bytes 2162692
  70.7 0.9 copy-start.8
  71.6 0.9 copy-start.9
  72.5 0.8 copy-start.12
  73.2 0.9 copy-start.14
  74.1 0.7 copy-start.15
  74.9 0.7 copy-start.16
  75.6 0.8 copy-start.18
  76.3 23.7 %copy-start.17 = (f32[22,32]{1,0:T(8,128)S(1)}, f32[22,32]{1,0:T(8,128)}, u32[]{:S(2)}) copy-start(f32[22,32]{1,0:T(8,128)} %vectors.1) | copy-start | bytes 8452
  76.3 23.7 %copy-start.19 = (f32[22,32]{1,0:T(8,128)S(1)}, f32[22,32]{1,0:T(8,128)}, u32[]{:S(2)}) copy-start(f32[22,32]{1,0:T(8,128)} %vec_m.1) | copy-start | bytes 8452
  76.3 23.7 %copy-start.20 = (f32[22,32]{1,0:T(8,128)S(1)}, f32[22,32]{1,0:T(8,128)}, u32[]{:S(2)}) copy-start(f32[22,32]{1,0:T(8,128)} %vec_v.1) | copy-start | bytes 8452

commit v3 on v1

v3 whole, which is shorter than its diff:
```python
import functools
import math

import jax
import jax.numpy as jnp
from jax import lax
from jax.experimental import pallas as pl
from jax.experimental.pallas import tpu as pltpu
from jax.sharding import PartitionSpec as P

TEMB = 512
HW = 16
PIX = HW * HW
GSIZE = 8
C = 256
TAPS = 9
KW = C * TAPS
HALF = 128 * TAPS

NORM_EPS = 1e-05
BETA_ONE = 0.9
BETA_TWO = 0.95
ADAM_EPS = 1e-06
DECAY = 0.01
RATE = 0.3
F32 = jnp.float32
BF16 = jnp.bfloat16
HIGH = lax.Precision.HIGHEST
MESH = pl.DeviceIdType.MESH
NN = (((1,), (0,)), ((), ()))
NT = (((1,), (1,)), ((), ()))
TN = (((0,), (0,)), ((), ()))
MIB = 1024 * 1024

XL = (3, 3, 3, 4)
DELAYS = (2, 5, 2)
VEC_ROWS = 22
LOSS_ROW = 24
MAIN = HALF + 128 + 128
SUM_ROWS = 16
CONV, TMB, ATTN = tuple(dict(conv=0, temb=0, attn=0))
HERE, W_IN = tuple(dict(_here=0, w_in=0))
LOG_TEN_THOUSAND = math.log(10000.0)


def dot(a, b, dims, precision=None):
    return lax.dot_general(a, b, dims, precision=precision, preferred_element_type=F32)


def iota(shape, axis):
    return lax.broadcasted_iota(jnp.int32, shape, axis)


def tap_order():
    wanted = (iota((1, HALF), 1) & 127) * TAPS + (iota((1, HALF), 1) >> 7)
    return jnp.where(iota((HALF, 1), 0) == wanted, 1.0, 0.0).astype(BF16)


def flip(value, mask):
    bit = 1
    while bit <= mask:
        if mask & bit:
            value = value + bit * (1 - 2 * ((value // bit) % 2))
        bit *= 2
    return value


def remote(src, dst, send_sem, recv_sem, target):
    return pltpu.make_async_remote_copy(
        src_ref=src, dst_ref=dst, send_sem=send_sem, recv_sem=recv_sem,
        device_id=target, device_id_type=MESH,
    )


def row_sum(value):
    return jnp.sum(value, axis=0, keepdims=True)


def group_mean(row):
    row = jnp.broadcast_to(row, (8, C))
    lane = iota(row.shape, 1)
    step = 1
    while step < GSIZE:
        up = pltpu.roll(row, C - step, 1)
        down = pltpu.roll(row, step, 1)
        row = row + jnp.where((lane & step) == 0, up, down)
        step *= 2
    return row[0:1] * (1.0 / (GSIZE * PIX))


def squares(value):
    return jnp.sum(jnp.sum(value * value, axis=1, keepdims=True), axis=0, keepdims=True)


def matrix_parts(lr):
    parts = []
    for k in range(4):
        for h in range(2):
            parts.append((1 + k, CONV, k, slice(h * HALF, (h + 1) * HALF), h,
                          slice(k * lr, (k + 1) * lr), slice(0, HALF)))
    for k in range(2):
        for j in range(4):
            top = (j % 2) * 2 * lr + k * lr
            parts.append((5 + k, TMB, k, slice(j * 128, (j + 1) * 128), j // 2,
                          slice(top, top + lr), slice(HALF + 128, MAIN)))
    for k in range(4):
        for h in range(2):
            parts.append((7 + k, ATTN, k, slice(h * 128, (h + 1) * 128), h,
                          slice(k * lr, (k + 1) * lr), slice(HALF, HALF + 128)))
    return parts


STATE = tuple(dict(
    w_in=0, m_in=0, v_in=0, conv_w=0, conv_m=0, conv_v=0, temb_w=0, temb_m=0, temb_v=0, attn_w=0, attn_m=0,
    attn_v=0, out_w=0, out_m=0, out_v=0, vectors=0, vec_m=0, vec_v=0,
))
PASSED = tuple(dict(
    in_first=0, in_second=0, conv_first=0, conv_second=0, temb_first=0, temb_second=0, attn_first=0,
    attn_second=0, out_first=0, out_second=0, vec_new=0, vec_first=0, vec_second=0, attn_grad=0,
))
UPDATES = tuple(dict(
    in_update=0, conv_update=0, temb_update=0, attn_update=0, out_update=0,
))
WEIGHTS = tuple(dict(
    w_in=0, conv_w=0, temb_w=0, attn_w=0, out_w=0,
))


class Names:
    def __init__(self, names, refs):
        assert len(names) == len(refs)
        self.__dict__.update(zip(names, refs))


def step_kernel(n, ny, nz, nx, dp, lr, images, names, *refs):
    r = Names(names, refs)
    rows_all = images * PIX
    scale = C ** -0.5
    me = lax.axis_index("chan")
    part = lax.axis_index("dp")
    z, y = me // ny, me % ny
    x, core = part // 2, part % 2
    sibling = (x * 2 + 1 - core, me)

    loads = {}

    def load(i, name):
        src, dst = getattr(r, name + "_hbm"), getattr(r, name)
        loads[name] = pltpu.make_async_copy(src, dst, r.load_sem.at[i])
        loads[name].start()

    for k in range(4):
        loads[k] = pltpu.make_async_copy(r.conv_w_hbm.at[k], r.conv_w.at[k], r.conv_sem.at[k])
        loads[k].start()
    for name in ("vectors", W_IN, "temb_w", "attn_w", "out_w"):
        load(STATE.index(name), name)
    for i, name in enumerate(("canvas", "noise")):
        load(len(STATE) + i, name)
    for i, name in enumerate(STATE):
        if name not in loads and name != "conv_w":
            load(i, name)

    offsets = [(i, j) for i in range(nz) for j in range(ny)][1:]
    place = {o: i for i, o in enumerate(offsets)}

    def chan_at(o):
        return flip(z, o[0]) * ny + flip(y, o[1])

    def next_part(k):
        return lax.rem(part + k, dp)

    barrier = pltpu.get_barrier_semaphore()
    for o in offsets:
        pl.semaphore_signal(barrier, inc=1, device_id=(part, chan_at(o)), device_id_type=MESH)
    for k in range(1, dp):
        pl.semaphore_signal(barrier, inc=1, device_id=(next_part(k), me), device_id_type=MESH)

    core_lanes = KW // 2
    use_x = nx == 2
    chunk_rows = max(lr, 16)
    conv_chunks = 4 * lr // chunk_rows
    chunks = list(range(conv_chunks))
    chunks.insert((conv_chunks + 1) // 2, None)

    def x_lanes(chunk):
        return (XL[chunk % 4]) * 128 if use_x else 0

    def rows_of(chunk):
        return pl.ds(chunk * chunk_rows, chunk_rows)

    attn_x = lr // 2 if use_x and lr >= 32 else 0

    def near_ref(chunk, src, c):
        if chunk is None:
            start = c * 2 * lr + x * attn_x if attn_x else c * 2 * lr
            return r.attn_all.at[src, pl.ds(pl.multiple_of(start, 16), 2 * lr - attn_x), :]
        wide = x_lanes(chunk)
        start = c * core_lanes + x * wide if wide else c * core_lanes
        return r.whole.at[src, rows_of(chunk), pl.ds(pl.multiple_of(start, 128), core_lanes - wide)]

    def x_ref(chunk, src, c, side):
        if chunk is None:
            start = c * 2 * lr + side * (2 * lr - attn_x)
            return r.attn_all.at[src, pl.ds(pl.multiple_of(start, 16), attn_x), :]
        wide = x_lanes(chunk)
        start = c * core_lanes + side * (core_lanes - wide)
        return r.whole.at[src, rows_of(chunk), pl.ds(pl.multiple_of(start, 128), wide)]

    def has_x(chunk):
        return attn_x > 0 if chunk is None else x_lanes(chunk) > 0

    sends = []

    def send(*args):
        copy = remote(*args)
        copy.start()
        sends.append(copy)

    def index(chunk):
        return conv_chunks if chunk is None else chunk

    def send_near(chunk, src, o, target):
        i = index(chunk)
        ref = near_ref(chunk, src, core)
        send(ref, ref, r.near_send.at[i, place[o]], r.near_recv.at[i, place[o]], target)

    def send_core(chunk, src, o, piece):
        i = index(chunk)
        ref = near_ref(chunk, src, core) if piece == 0 else x_ref(chunk, src, core, 1 - x)
        send(ref, ref, r.core_send.at[piece, i, place[o]], r.core_recv.at[piece, i, place[o]], sibling)

    def begin(chunk):
        for i in range(1, nz):
            send_near(chunk, me, (i, 0), (part, chan_at((i, 0))))
        for j in range(1, ny):
            send_near(chunk, me, (0, j), (part, chan_at((0, j))))

    def near_in(chunk, o):
        i = index(chunk)
        src = chan_at(o)
        ref = near_ref(chunk, src, core)
        remote(ref, ref, r.near_send.at[i, place[o]], r.near_recv.at[i, place[o]], (part, src)).wait_recv()
        if o[1] == 0:
            for j in range(1, ny):
                send_near(chunk, src, (o[0], j), (part, chan_at((0, j))))
        if has_x(chunk):
            ref = x_ref(chunk, src, core, x)
            send(ref, ref, r.x_send.at[i, place[o]], r.x_recv.at[i, place[o]], ((1 - x) * 2 + core, me))
        send_core(chunk, src, o, 0)

    def x_in(chunk, o):
        if has_x(chunk):
            i = index(chunk)
            src = chan_at(o)
            ref = x_ref(chunk, src, core, 1 - x)
            remote(ref, ref, r.x_send.at[i, place[o]], r.x_recv.at[i, place[o]], ((1 - x) * 2 + core, me)).wait_recv()
            send_core(chunk, src, o, 1)

    def core_in(chunk, o):
        i = index(chunk)
        src = chan_at(o)
        pieces = [near_ref(chunk, src, 1 - core)]
        if has_x(chunk):
            pieces.append(x_ref(chunk, src, 1 - core, 1 - x))
        for piece, ref in enumerate(pieces):
            remote(ref, ref, r.core_send.at[piece, i, place[o]], r.core_recv.at[piece, i, place[o]], sibling).wait_recv()

    def stage_one(chunk):
        for i in range(1, nz):
            near_in(chunk, (i, 0))

    def stage_two(chunk):
        for j in range(1, ny):
            near_in(chunk, (0, j))
        for i in range(1, nz):
            for j in range(1, ny):
                near_in(chunk, (i, j))

    def stage_three(chunk):
        for o in offsets:
            x_in(chunk, o)

    def stage_four(chunk):
        for o in offsets:
            core_in(chunk, o)

    turn = [0]

    def gather_turn():
        i = turn[0]
        turn[0] += 1
        for stage, delay in ((stage_one, 0), (stage_two, 1), (stage_three, 2), (stage_four, 3)):
            if 0 <= i - delay < len(chunks):
                stage(chunks[i - delay])
            if delay == 0 and 2 <= i + 2 < len(chunks):
                begin(chunks[i + 2])

    def arrived(chunk):
        while turn[0] < chunks.index(chunk) + 4:
            gather_turn()

    order = tap_order()
    r.order[...] = order

    def prepare(convs, extra=None):
        stack = []
        for k in convs:
            loads[k].wait()
            weight = r.conv_w[k].astype(BF16)
            stack += [weight[:, :HALF], weight[:, HALF:]]
        if extra is not None:
            stack.append(extra)
        mixed = dot(jnp.concatenate(stack, axis=0), r.order[...], NN)
        for i, k in enumerate(convs):
            for tap in range(TAPS):
                for h in range(2):
                    lanes = slice(tap * C + h * 128, tap * C + h * 128 + 128)
                    top = (2 * i + h) * lr
                    r.whole[me, k * lr:(k + 1) * lr, lanes] = mixed[top:top + lr, tap * 128:(tap + 1) * 128].astype(BF16)
        return mixed[2 * len(convs) * lr:]

    steps_row = iota((16, C), 0)
    steps_all = jnp.zeros((16, C), F32)
    for b in range(images):
        steps_all = jnp.where(steps_row == b, r.steps[b].astype(F32), steps_all)
    frequency = jnp.exp(-LOG_TEN_THOUSAND * iota((1, C), 1).astype(F32) / (TEMB // 2))
    angles = steps_all * frequency
    for i, wave in enumerate((jnp.sin(angles), jnp.cos(angles))):
        wave = jnp.where(steps_row < images, wave / (1.0 + jnp.exp(-wave)), 0.0)
        r.temb_act[:, i * C:(i + 1) * C] = wave.astype(BF16)

    pl.semaphore_wait(barrier, n + dp - 2)
    prepare((0, 1))
    begin(chunks[0])
    if conv_chunks > 2:
        begin(chunks[1])

    loads["vectors"].wait()
    loads[W_IN].wait()
    loads["temb_w"].wait()
    r.own_rows[...] = jnp.zeros_like(r.own_rows)
    r.own_rows[0:VEC_ROWS, 0:lr] = r.vectors[...]
    for block in range(2):
        shift = dot(r.temb_act[...], r.temb_w[block].astype(BF16), NT)
        for b in range(images):
            row = VEC_ROWS + block * images + b
            r.own_rows[row:row + 1, 0:lr] = (
                shift[b:b + 1, :] + r.vectors[17 + block:18 + block, :]
            ) + r.vectors[13 + 2 * block:14 + 2 * block, :]
    r.in_scr[...] = jnp.zeros_like(r.in_scr)
    r.in_scr[0:lr, 0:27] = r.w_in[...]
    turned = r.in_scr[...].T
    packed = [jnp.zeros((8, 128), F32), jnp.zeros((8, 128), F32)]
    for g in range(4):
        for i, rows in enumerate((r.own_rows[g * 8:g * 8 + 8, :], turned[g * 8:g * 8 + 8, :])):
            packed[i] += rows if g == 0 else pltpu.roll(rows, g * lr, 1)
    r.smalls[me, 0:8, :] = packed[0]
    r.smalls[me, 8:16, :] = packed[1]
    total = jnp.int32(0)
    for b in range(images):
        side = jnp.minimum(jnp.maximum(r.crop[b, 2], 0), HW)
        total += 3 * side * side
    r.counts[part] = jnp.full((8, 128), total, jnp.int32).astype(F32)
    for o in offsets:
        i = place[o]
        send(r.smalls.at[me], r.smalls.at[me], r.small_send.at[i], r.small_recv.at[i], (part, chan_at(o)))
    for i in range(1, dp):
        send(r.counts.at[part], r.counts.at[part], r.count_send.at[i - 1], r.count_recv.at[i - 1], (next_part(i), me))

    loads["attn_w"].wait()
    for k in range(4):
        r.attn_all[me, k * lr:(k + 1) * lr, :] = r.attn_w[k].astype(BF16)
    loads["out_w"].wait()
    r.out_scr[...] = jnp.zeros_like(r.out_scr)
    for h in range(2):
        r.out_scr[h * 8:h * 8 + 3, :] = r.out_w[:, h * HALF:(h + 1) * HALF]
    out_mixed = prepare((2, 3), r.out_scr[...].astype(BF16))
    for tap in range(TAPS):
        for h in range(2):
            r.out_taps[tap * 8:tap * 8 + 8, h * 128:(h + 1) * 128] = out_mixed[
                h * 8:h * 8 + 8, tap * 128:(tap + 1) * 128
            ]
    if conv_chunks <= 2:
        begin(chunks[1])

    lane = iota((1, PIX), 1)
    pix_x, pix_y = lane & (HW - 1), lane >> 4
    size = r.canvas.shape[2]
    loads["canvas"].wait()
    loads["noise"].wait()
    noise_rows, mask_rows, noisy_rows = [], [], []
    for b in range(images):
        phase = (jnp.broadcast_to(r.steps[b].astype(F32), (1, PIX)) / 1000.0 + 0.008) / 1.008
        alpha_bar = jnp.cos(phase * (math.pi / 2)) ** 2
        pick = jnp.where(iota((size, PIX), 0) == r.crop[b, 1] + pix_x, 1.0, 0.0)
        flat = r.canvas[b].reshape(3 * size, size)
        spread = dot(flat, pick, NN, HIGH).reshape(3, size, PIX)
        chosen = iota((size, PIX), 0) == r.crop[b, 0] + pix_y
        clean = jnp.sum(jnp.where(chosen[None], spread, 0.0), axis=1)
        noise_b = r.noise[:, b, :]
        noisy_rows.append(jnp.sqrt(alpha_bar) * clean + jnp.sqrt(1.0 - alpha_bar) * noise_b)
        noise_rows.append(noise_b)
        side = r.crop[b, 2]
        mask_rows.append(jnp.where((pix_x < side) & (pix_y < side), 1.0, 0.0))
    zeros5 = jnp.zeros((5, rows_all), F32)
    noisy = jnp.concatenate([jnp.concatenate(noisy_rows, axis=1), zeros5], axis=0)
    noise_all = jnp.concatenate([jnp.concatenate(noise_rows, axis=1), zeros5], axis=0)
    mask_all = jnp.concatenate(mask_rows, axis=1)

    lane_all = iota((8, rows_all), 1)
    px, py = lane_all & (HW - 1), (lane_all >> 4) & (HW - 1)

    def tap_shift(field, tap):
        dy, dx = tap // 3 - 1, tap % 3 - 1
        move = -(dy * HW + dx) % rows_all
        out = pltpu.roll(field, move, 1) if move else field
        inside = (px + dx >= 0) & (px + dx < HW) & (py + dy >= 0) & (py + dy < HW)
        return jnp.where(inside, out, 0.0)

    noisy = noisy.astype(BF16).astype(F32)
    r.rows_scr[...] = jnp.zeros_like(r.rows_scr)
    for tap in range(TAPS):
        moved = tap_shift(noisy, tap)
        for colour in range(3):
            r.rows_scr[colour * TAPS + tap:colour * TAPS + tap + 1, :] = moved[colour:colour + 1]
    r.taps0[...] = r.rows_scr[...].astype(BF16)

    gather_turn()

    for o in offsets:
        src = chan_at(o)
        remote(r.smalls.at[src], r.smalls.at[src], r.small_send.at[place[o]], r.small_recv.at[place[o]],
               (part, src)).wait_recv()
    for i in range(1, dp):
        p = lax.rem(part - i + dp, dp)
        remote(r.counts.at[p], r.counts.at[p], r.count_send.at[i - 1], r.count_recv.at[i - 1], (p, me)).wait_recv()
    lane_wide = iota((16, C), 1)
    unpacked = [jnp.zeros((16, C), F32) for g in range(4)]
    for j in range(n):
        block = jnp.concatenate([r.smalls[j], jnp.zeros((16, 128), F32)], axis=1)
        for g in range(4):
            piece = jnp.where((lane_wide >= g * lr) & (lane_wide < (g + 1) * lr), block, 0.0)
            move = (j - g) * lr % C
            unpacked[g] += pltpu.roll(piece, move, 1) if move else piece
    for g in range(4):
        r.vec[g * 8:g * 8 + 8, :] = unpacked[g][0:8]
        r.w_in_all[g * 8:g * 8 + 8, :] = unpacked[g][8:16]
    total = r.counts[0, 0:1, 0:1]
    for k in range(1, dp):
        total = total + r.counts[k, 0:1, 0:1]

    def vrow(i):
        return r.vec[i:i + 1, :]

    def span(b):
        return slice(b * PIX, (b + 1) * PIX)

    def conv_weight(k):
        return r.whole[:, k * lr:(k + 1) * lr, :].reshape(C, KW)

    def attn_weight(k):
        return r.attn_all[:, k * lr:(k + 1) * lr, :].reshape(C, C)

    col_x = iota((PIX, C), 0) & (HW - 1)
    blank = jnp.zeros((HW, C), BF16)
    hidden, xhat, dact, rstd, acts = r.hidden, r.xhat, r.dact, r.rstd, r.acts
    cols = (r.col0, r.col1, r.col2, r.col3)

    def norm_fwd(i, value, gain, shift, store):
        for b in range(images):
            image = value[span(b)]
            centred = image - group_mean(row_sum(image))
            inv = lax.rsqrt(group_mean(row_sum(centred * centred)) + NORM_EPS)
            normed = centred * inv
            scaled = normed * gain + shift
            gate = 0.5 * jnp.tanh(0.5 * scaled) + 0.5
            act = scaled * gate
            xhat[i, span(b), :] = normed
            dact[i, span(b), :] = gate + act * (1.0 - gate)
            rstd[i * images + b:i * images + b + 1, :] = inv
            store(b, act)

    def store_cols(ref, b, act):
        left = jnp.where(col_x > 0, pltpu.roll(act, 1, 0), 0.0)
        right = jnp.where(col_x < HW - 1, pltpu.roll(act, PIX - 1, 0), 0.0)
        for dx, moved in enumerate((left, act, right)):
            low = moved.astype(BF16)
            for dy in range(3):
                lanes = slice((3 * dy + dx) * C, (3 * dy + dx + 1) * C)
                base = b * PIX
                if dy == 0:
                    ref[base:base + HW, lanes] = blank
                    ref[base + HW:base + PIX, lanes] = low[:PIX - HW]
                elif dy == 1:
                    ref[base:base + PIX, lanes] = low
                else:
                    ref[base:base + PIX - HW, lanes] = low[HW:]
                    ref[base + PIX - HW:base + PIX, lanes] = blank

    def add_rows(value, first):
        return jnp.concatenate([value[span(b)] + vrow(first + b) for b in range(images)], axis=0)

    def chunk_of(k):
        return k * lr // chunk_rows

    def block_fwd(block, source, target):
        norm_fwd(3 * block, hidden[source], vrow(3 * block), vrow(6 + 3 * block),
                 functools.partial(store_cols, cols[2 * block]))
        arrived(chunk_of(2 * block))
        middle = dot(cols[2 * block][...], conv_weight(2 * block), NT)
        middle = add_rows(middle, VEC_ROWS + block * images)
        norm_fwd(3 * block + 1, middle, vrow(3 * block + 1), vrow(7 + 3 * block),
                 functools.partial(store_cols, cols[2 * block + 1]))
        arrived(chunk_of(2 * block + 1))
        branch = dot(cols[2 * block + 1][...], conv_weight(2 * block + 1), NT)
        hidden[target] = hidden[source] + (branch + vrow(14 + 2 * block))

    def store_act(i):
        def store(b, act):
            acts[i, span(b), :] = act.astype(BF16)
        return store

    hidden[0] = dot(r.taps0[...], r.w_in_all[...].astype(BF16), TN) + vrow(12)
    block_fwd(0, 0, 1)

    norm_fwd(2, hidden[1], vrow(2), vrow(8), store_act(0))
    arrived(None)
    r.q_scr[...] = (dot(acts[0], attn_weight(0), NT) + vrow(19)).astype(BF16)
    r.k_scr[...] = dot(acts[0], attn_weight(1), NT).astype(BF16)
    r.v_scr[...] = (dot(acts[0], attn_weight(2), NT) + vrow(20)).astype(BF16)
    for b in range(images):
        scores = dot(r.q_scr[span(b), :], r.k_scr[span(b), :], NT) * scale
        raised = jnp.exp(scores - jnp.max(scores, axis=1, keepdims=True))
        soft = raised / jnp.sum(raised, axis=1, keepdims=True)
        r.probs[b] = soft
        r.mixed[span(b), :] = dot(soft.astype(BF16), r.v_scr[span(b), :], NN).astype(BF16)
    hidden[0] = hidden[1] + (dot(r.mixed[...], attn_weight(3), NT) + vrow(21))

    block_fwd(1, 0, 1)
    norm_fwd(5, hidden[1], vrow(5), vrow(11), store_act(1))

    out_low = r.out_taps[...].astype(BF16)
    fanned = dot(out_low, acts[1], NT)
    pred = jnp.zeros((8, rows_all), F32)
    for tap in range(TAPS):
        pred += tap_shift(fanned[tap * 8:tap * 8 + 8], tap)
    error = pred - noise_all
    masked = mask_all * error
    inverse = 1.0 / total
    loss = jnp.sum(jnp.sum(masked * error, axis=1, keepdims=True), axis=0, keepdims=True) * inverse
    grad_pred = (2.0 * masked * inverse).astype(BF16).astype(F32)
    spread_pred = jnp.concatenate(
        [tap_shift(grad_pred, TAPS - 1 - tap) for tap in range(TAPS)], axis=0
    ).astype(BF16)
    out_grad = dot(spread_pred, acts[1], NN)

    lanes_attn, lanes_temb = slice(HALF, HALF + 128), slice(HALF + 128, MAIN)

    def region(chunk):
        if chunk == ATTN:
            return slice(0, 4 * lr), lanes_attn
        if chunk == TMB:
            return slice(0, 4 * lr), lanes_temb
        return slice(chunk * chunk_rows, (chunk + 1) * chunk_rows), slice(0, HALF)

    def family(chunk):
        if chunk == "out":
            return (r.out_local, r.out_one, r.out_two, r.out_last), (slice(None), slice(None)), conv_chunks + 2
        i = conv_chunks + (ATTN, TMB).index(chunk) if isinstance(chunk, str) else chunk
        return (r.local, r.one, r.two, r.last), region(chunk), i

    def view(ref, i, where):
        return ref.at[(i,) + where]

    def reduce_one(chunk):
        (local, one, two, last), where, i = family(chunk)
        send(view(local, 1 - core, where), one.at[where], r.one_send.at[i], r.one_recv.at[i], sibling)

    def reduce_two(chunk):
        (local, one, two, last), where, i = family(chunk)
        remote(view(local, 1 - core, where), one.at[where], r.one_send.at[i], r.one_recv.at[i], sibling).wait_recv()
        both = local[(core,) + where].astype(F32) + one[where].astype(F32)
        two[(x,) + where] = both.astype(two.dtype)
        for m in range(1, nx):
            ref = view(two, x, where)
            send(ref, ref, r.two_send.at[i, m - 1], r.two_recv.at[i, m - 1], (lax.rem(x + m, nx) * 2 + core, me))

    def reduce_three(chunk):
        (local, one, two, last), where, i = family(chunk)
        for m in range(1, nx):
            sender = lax.rem(x - m + nx, nx)
            ref = view(two, sender, where)
            remote(ref, ref, r.two_send.at[i, m - 1], r.two_recv.at[i, m - 1], (sender * 2 + core, me)).wait_recv()
        summed = two[(0,) + where].astype(F32)
        for m in range(1, nx):
            summed = summed + two[(m,) + where].astype(F32)
        last[(core,) + where] = summed.astype(last.dtype)
        ref = view(last, core, where)
        send(ref, ref, r.three_send.at[i], r.three_recv.at[i], sibling)

    def reduce_four(chunk):
        (local, one, two, last), where, i = family(chunk)
        ref = view(last, 1 - core, where)
        remote(ref, ref, r.three_send.at[i], r.three_recv.at[i], sibling).wait_recv()

    due = []
    clock = [0]

    def run_due(entry):
        delay = {1: DELAYS[0], 2: DELAYS[1], 3: DELAYS[2]}
        stage, chunk = entry
        (reduce_one, reduce_two, reduce_three, reduce_four)[stage - 1](chunk)
        if stage < 4:
            due.append((clock[0] + delay[stage], (stage + 1, chunk)))

    def tick():
        clock[0] += 1
        for item in [item for item in due if item[0] <= clock[0]]:
            due.remove(item)
            run_due(item[1])

    def ready(chunk):
        run_due((1, chunk))

    def finish(chunk=None):
        while True:
            left = [item for item in due if chunk is None or item[1][1] == chunk]
            if not left:
                return
            item = min(left, key=lambda item: (item[1][0], item[0]))
            due.remove(item)
            run_due(item[1])

    for h in range(2):
        for tap in range(TAPS):
            r.out_local[h, :, tap * 128:(tap + 1) * 128] = out_grad[tap * 8:tap * 8 + 8, h * 128:(h + 1) * 128]
    ready("out")
    grad = dot(spread_pred, out_low, TN)

    gvec = r.gvec
    gvec[...] = jnp.zeros_like(gvec)
    pick_own = jnp.where(iota((lr, C), 1) == iota((lr, C), 0) + me * lr, 1.0, 0.0).astype(BF16)
    hole = jnp.zeros((HW, C), F32)

    def own_rows(low):
        return dot(pick_own, low, NT).astype(BF16)

    def norm_back(i, grad, gain_row):
        outs = []
        gain = vrow(gain_row)
        gain_sum = jnp.zeros((1, C), F32)
        shift_sum = jnp.zeros((1, C), F32)
        for b in range(images):
            slope = grad[span(b)] * dact[i, span(b), :]
            normed = xhat[i, span(b), :]
            shift_b = row_sum(slope)
            gain_b = row_sum(slope * normed)
            mean_one = group_mean(shift_b * gain)
            mean_two = group_mean(gain_b * gain)
            inv = rstd[i * images + b:i * images + b + 1, :]
            outs.append(inv * (slope * gain - mean_one - normed * mean_two))
            gain_sum += gain_b
            shift_sum += shift_b
        gvec[gain_row:gain_row + 1, :] = gain_sum
        gvec[6 + gain_row:7 + gain_row, :] = shift_sum
        return jnp.concatenate(outs, axis=0)

    def conv_back(k, low):
        own = dot(own_rows(low), cols[k][...], NN)
        for h in range(2):
            for tap in range(TAPS):
                r.local[h, k * lr:(k + 1) * lr, tap * 128:(tap + 1) * 128] = own[
                    :, tap * C + h * 128:tap * C + h * 128 + 128
                ].astype(BF16)
        if k * lr % chunk_rows == 0:
            ready(chunk_of(k))
        tick()
        parts = dot(low, conv_weight(k), NN)
        outs = []
        for b in range(images):
            sides = []
            for dx in range(3):
                up = parts[span(b), dx * C:(dx + 1) * C]
                mid = parts[span(b), (3 + dx) * C:(4 + dx) * C]
                down = parts[span(b), (6 + dx) * C:(7 + dx) * C]
                sides.append(
                    mid
                    + jnp.concatenate([up[HW:], hole], axis=0)
                    + jnp.concatenate([hole, down[:PIX - HW]], axis=0)
                )
            left = pltpu.roll(jnp.where(col_x > 0, sides[0], 0.0), PIX - 1, 0)
            right = pltpu.roll(jnp.where(col_x < HW - 1, sides[2], 0.0), 1, 0)
            outs.append(sides[1] + left + right)
        tick()
        return jnp.concatenate(outs, axis=0)

    def block_back(block, grad):
        gvec[14 + 2 * block:15 + 2 * block, :] = row_sum(grad)
        back = conv_back(2 * block + 1, grad.astype(BF16))
        middle = norm_back(3 * block + 1, back, 3 * block + 1)
        r.gsum[...] = jnp.zeros_like(r.gsum)
        for b in range(images):
            r.gsum[b:b + 1, :] = row_sum(middle[span(b)])
        whole_sum = row_sum(r.gsum[...])
        gvec[13 + 2 * block:14 + 2 * block, :] = whole_sum
        gvec[17 + block:18 + block, :] = whole_sum
        own = dot(pick_own, r.gsum[...].astype(BF16), NT).astype(BF16)
        temb = dot(own, r.temb_act[...], NN)
        for j in range(4):
            top = (j % 2) * 2 * lr + block * lr
            r.local[j // 2, top:top + lr, lanes_temb] = temb[:, j * 128:(j + 1) * 128].astype(BF16)
        if block == 0:
            ready(TMB)
        tick()
        back = conv_back(2 * block, middle.astype(BF16))
        return grad + norm_back(3 * block, back, 3 * block)

    grad = norm_back(5, grad, 5)
    tick()
    grad = block_back(1, grad)
    tick()

    gvec[21:22, :] = row_sum(grad)
    low = grad.astype(BF16)

    def attn_own(k, low, field):
        own = dot(own_rows(low), field, NN)
        for h in range(2):
            r.local[h, k * lr:(k + 1) * lr, lanes_attn] = own[:, h * 128:(h + 1) * 128].astype(BF16)

    attn_own(3, low, r.mixed[...])
    mixed_low = dot(low, attn_weight(3), NN).astype(BF16)
    grads_q, grads_k, grads_v = [], [], []
    for b in range(images):
        image = mixed_low[span(b)]
        soft = r.probs[b]
        grad_soft = dot(image, r.v_scr[span(b), :], NT)
        grads_v.append(dot(soft.astype(BF16), image, TN))
        weighed = soft * grad_soft
        slope = (weighed - soft * jnp.sum(weighed, axis=1, keepdims=True)).astype(BF16)
        grads_q.append(scale * dot(slope, r.k_scr[span(b), :], NN))
        grads_k.append(scale * dot(slope, r.q_scr[span(b), :], TN))
    tick()
    back = jnp.zeros((rows_all, C), F32)
    for i, grads in enumerate((grads_q, grads_k, grads_v)):
        full = jnp.concatenate(grads, axis=0)
        if i != 1:
            gvec[19 + i // 2:20 + i // 2, :] = row_sum(full)
        low = full.astype(BF16)
        attn_own(i, low, acts[0])
        back += dot(low, attn_weight(i), NN)
    ready(ATTN)
    tick()
    grad = grad + norm_back(2, back, 2)
    tick()

    grad = block_back(0, grad)
    tick()
    gvec[12:13, :] = row_sum(grad)
    in_grad = dot(own_rows(grad.astype(BF16)), r.taps0[...], NT)

    own_vec = jnp.where(iota((32, 128), 1) < lr, pltpu.roll(gvec[...], lax.rem(C - me * lr, C), 1)[:, 0:128], 0.0)
    own_vec = jnp.where(iota((32, 128), 0) == LOSS_ROW, loss, own_vec)
    own_vec = jnp.where(iota((32, 128), 1) < lr, own_vec, 0.0)
    packed = [jnp.zeros((8, 128), F32), jnp.zeros((8, 128), F32)]
    for g in range(4):
        rows = own_vec[g * 8:g * 8 + 8, :]
        packed[0] += rows if g == 0 else pltpu.roll(rows, g * lr, 1)
    for g in range(lr // 8):
        rows = jnp.concatenate([in_grad[g * 8:g * 8 + 8, :], jnp.zeros((8, 96), F32)], axis=1)
        packed[1] += rows if g == 0 else pltpu.roll(rows, g * 32, 1)
    r.tiny[part, 0:8, :] = packed[0]
    r.tiny[part, 8:16, :] = packed[1]
    for i in range(1, dp):
        send(r.tiny.at[part], r.tiny.at[part], r.tiny_send.at[i - 1], r.tiny_recv.at[i - 1], (next_part(i), me))
    tick()

    for name in STATE:
        if name in loads and name not in ("vectors", W_IN, "temb_w", "attn_w", "out_w"):
            loads[name].wait()
    count = jnp.broadcast_to(r.count_step[0].astype(F32), (1, 128))
    fix_one = (1.0 / (1.0 - jnp.exp(math.log(BETA_ONE) * count)))[:, 0:1]
    fix_two = (1.0 / (1.0 - jnp.exp(math.log(BETA_TWO) * count)))[:, 0:1]

    def adapt(grad, first, second):
        first_new = BETA_ONE * first + (1.0 - BETA_ONE) * grad
        second_new = BETA_TWO * second + (1.0 - BETA_TWO) * grad * grad
        direction = first_new * fix_one / (jnp.sqrt(second_new * fix_two) + ADAM_EPS)
        return first_new, second_new, direction

    sums = {}

    def lamb(number, name, at, grad):
        names = (W_IN, "m_in", "v_in") if name == "in" else (name + "_w", name + "_m", name + "_v")
        weight, first, second = (getattr(r, each)[at] for each in names)
        first, second, direction = adapt(grad, first, second)
        update = direction + DECAY * weight
        getattr(r, name + "_first")[at] = first
        getattr(r, name + "_second")[at] = second
        getattr(r, name + "_update")[at] = update
        pair = (squares(weight), squares(update))
        if number in sums:
            pair = (sums[number][0] + pair[0], sums[number][1] + pair[1])
        sums[number] = pair

    every = slice(None)
    outward = []

    def put(name, k=None):
        src, dst = getattr(r, name), getattr(r, name + "_hbm")
        if k is not None:
            src, dst = src.at[k], dst.at[k]
        copy = pltpu.make_async_copy(src, dst, r.out_sem.at[len(outward)])
        copy.start()
        outward.append(copy)

    def put_all(name, k=None):
        for kind in ("first", "second", "update"):
            put(name + "_" + kind, k)

    def conv_steps(which, natural):
        for number, name, k, lanes, h, rows, held in matrix_parts(lr):
            if name == CONV and chunk_of(k) in which:
                top = h * len(which) * chunk_rows + k * lr - min(which) * chunk_rows
                lamb(number, name, (k, every, lanes), natural[top:top + lr])
                if h == 1:
                    put_all(CONV, k)

    early = list(range(1, conv_chunks))
    for chunk in early + [ATTN, TMB, "out"]:
        finish(chunk)
    stack = [r.last[h, chunk_rows:4 * lr, 0:HALF] for h in range(2)]
    stack += [jnp.concatenate([r.out_last[h], jnp.zeros((8, HALF), F32)], axis=0).astype(BF16) for h in range(2)]
    natural = dot(jnp.concatenate(stack, axis=0), r.order[...], NT)
    conv_steps(early, natural)
    top = 2 * (4 * lr - chunk_rows)
    for h in range(2):
        lamb(11, "out", (every, slice(h * HALF, (h + 1) * HALF)), natural[top + h * 16:top + h * 16 + 3])
    for number, name, k, lanes, h, rows, held in matrix_parts(lr):
        if name != CONV:
            value = r.last[h, rows, held].astype(F32)
            if name == ATTN:
                r.attn_grad[k, :, lanes] = value
            lamb(number, name, (k, every, lanes), value)
    for name in ("out", TMB, ATTN):
        put_all(name)
    put("attn_grad")
    finish()
    natural = dot(jnp.concatenate([r.last[h, 0:chunk_rows, 0:HALF] for h in range(2)], axis=0), r.order[...], NT)
    conv_steps([0], natural)

    for i in range(1, dp):
        p = lax.rem(part - i + dp, dp)
        remote(r.tiny.at[p], r.tiny.at[p], r.tiny_send.at[i - 1], r.tiny_recv.at[i - 1], (p, me)).wait_recv()
    tiny = r.tiny[0]
    for k in range(1, dp):
        tiny = tiny + r.tiny[k]
    for g in range(4):
        rows = tiny[0:8] if g == 0 else pltpu.roll(tiny[0:8], 128 - g * lr, 1)
        r.own_rows[g * 8:g * 8 + 8, :] = rows
    for g in range(lr // 8):
        rows = tiny[8:16] if g == 0 else pltpu.roll(tiny[8:16], 128 - g * 32, 1)
        r.in_scr[g * 8:g * 8 + 8, :] = rows
    lamb(0, "in", (every, every), r.in_scr[0:lr, 0:27])
    put_all("in")

    row = iota((SUM_ROWS, 128), 0)
    lane = iota((SUM_ROWS, 128), 1)
    table = jnp.zeros((SUM_ROWS, 128), F32)
    for number in range(11):
        for side in range(2):
            table = jnp.where((row == number) & (lane == side), sums[number][side], table)
    r.tables[me] = table
    for o in offsets:
        i = place[o]
        send(r.tables.at[me], r.tables.at[me], r.sum_send.at[i], r.sum_recv.at[i], (part, chan_at(o)))
    first, second, direction = adapt(r.own_rows[0:VEC_ROWS, 0:lr], r.vec_m[...], r.vec_v[...])
    r.vec_new[...] = r.vectors[...] - RATE * direction
    r.vec_first[...] = first
    r.vec_second[...] = second
    for name in ("vec_new", "vec_first", "vec_second"):
        put(name)
    for o in offsets:
        src = chan_at(o)
        remote(r.tables.at[src], r.tables.at[src], r.sum_send.at[place[o]], r.sum_recv.at[place[o]],
               (part, src)).wait_recv()
    total = r.tables[0]
    for k in range(1, n):
        total = total + r.tables[k]
    for side in range(2):
        total = jnp.where((row == 11) & (lane == side), sums[11][side], total)
    total = jnp.where((row == 12) & (lane == 0), r.own_rows[LOSS_ROW:LOSS_ROW + 1, 0:1], total)
    r.norms[...] = total
    put("norms")
    for copy in sends:
        copy.wait_send()
    for copy in outward:
        copy.wait()


def update_kernel(names, *refs):
    r = Names(names, refs)
    copies = []

    def copy(src, dst):
        made = pltpu.make_async_copy(src, dst, r.sem.at[len(copies)])
        made.start()
        copies.append(made)
        return made

    copy(r.norms, r.norms_in)
    loads = {}
    for k in range(4):
        loads[(CONV, k)] = [
            copy(getattr(r, name).at[k], getattr(r, name + HERE).at[k]) for name in ("conv_w", "conv_update")
        ]
    for name in ("in", TMB, ATTN, "out"):
        weight = W_IN if name == "in" else name + "_w"
        loads[name] = [copy(getattr(r, each), getattr(r, each + HERE)) for each in (weight, name + "_update")]
    passing = [(name, copy(getattr(r, name), getattr(r, name + HERE))) for name in PASSED]
    copies[0].wait()
    outward = []

    def ratio(number):
        pair = r.norms_in[number:number + 1, 0:2]
        return RATE * jnp.sqrt(pair[:, 0:1] / (pair[:, 1:2] + 1e-06))

    r.norms_here[...] = jnp.sqrt(r.norms_in[...].T[0:2, 0:12])
    outward.append(copy(r.norms_here, r.norms_out))
    r.loss_out[...] = r.norms_in[12:13, 0:1]
    for number, name, k in [(0, "in", None)] + [(1 + k, CONV, k) for k in range(4)] + [
        (5 + k, TMB, k) for k in range(2)
    ] + [(7 + k, ATTN, k) for k in range(4)] + [(11, "out", None)]:
        weight_name = W_IN if name == "in" else name + "_w"
        for wait in loads.pop((name, k) if name == CONV else name, ()):
            wait.wait()
        at = (slice(None), slice(None)) if k is None else (k, slice(None), slice(None))
        here, target = getattr(r, name + HERE), getattr(r, name + "_new_out")
        new = getattr(r, weight_name + HERE)[at] - ratio(number) * getattr(r, name + "_update_here")[at]
        here[at] = new
        last = k in (None, {CONV: k, TMB: 1, ATTN: 3}.get(name))
        if name == CONV:
            outward.append(copy(here.at[k], target.at[k]))
        elif last:
            outward.append(copy(here, target))
        if k is not None:
            low = getattr(r, name + "_low_here")
            low[at] = new.astype(BF16)
            if name == CONV:
                outward.append(copy(low.at[k], getattr(r, name + "_low_out").at[k]))
            elif last:
                outward.append(copy(low, getattr(r, name + "_low_out")))
    for name, made in passing:
        made.wait()
        outward.append(copy(getattr(r, name + HERE), getattr(r, name + "_out")))
    for made in outward:
        made.wait()


def vmem_spec():
    return pl.BlockSpec(memory_space=pltpu.VMEM)


def smem_spec():
    return pl.BlockSpec(memory_space=pltpu.SMEM)


def hbm_spec():
    return pl.BlockSpec(memory_space=pltpu.HBM)


def shape(dims, kind=F32):
    return jax.ShapeDtypeStruct(dims, kind)


def per_device(n, dp, canvas, crop_boxes, time_steps, noise_field, step_count, *state):
    images = canvas.shape[0]
    rows_all = images * PIX
    own = dict(zip(STATE, state))
    lr = own["conv_w"].shape[1]
    nx = dp // 2
    ny = 1 << ((n.bit_length() - 2) // 2)
    nz = n // ny
    dma = pltpu.SemaphoreType.DMA
    chunk_rows = max(lr, 16)
    chunks = 4 * lr // chunk_rows + 1

    made = {}
    for key, name in (("in", W_IN), (CONV, "conv_w"), (TMB, "temb_w"), (ATTN, "attn_w"), ("out", "out_w")):
        for kind in ("first", "second", "update"):
            made[key + "_" + kind] = own[name].shape
    for name in ("vec_new", "vec_first", "vec_second"):
        made[name] = own["vectors"].shape
    made["attn_grad"] = own["attn_w"].shape
    made["norms"] = (SUM_ROWS, 128)

    inputs = ["crop", "steps", "count_step", "canvas_hbm", "noise_hbm"] + [name + "_hbm" for name in STATE]
    scratch = {name: pltpu.VMEM(own[name].shape, F32) for name in STATE}
    wide = max(nx - 1, 1)
    scratch.update(
        canvas=pltpu.VMEM(canvas.shape, F32), noise=pltpu.VMEM(noise_field.shape, F32),
        load_sem=dma((len(STATE) + 2,)), conv_sem=dma((4,)),
        whole=pltpu.VMEM((n, 4 * lr, KW), BF16), attn_all=pltpu.VMEM((n, 4 * lr, C), BF16),
        smalls=pltpu.VMEM((n, 16, 128), F32), counts=pltpu.VMEM((dp, 8, 128), F32),
        near_send=dma((chunks, n - 1)), near_recv=dma((chunks, n - 1)),
        x_send=dma((chunks, n - 1)), x_recv=dma((chunks, n - 1)),
        core_send=dma((2, chunks, n - 1)), core_recv=dma((2, chunks, n - 1)),
        small_send=dma((n - 1,)), small_recv=dma((n - 1,)), count_send=dma((dp - 1,)), count_recv=dma((dp - 1,)),
        order=pltpu.VMEM((HALF, HALF), BF16), temb_act=pltpu.VMEM((16, TEMB), BF16),
        own_rows=pltpu.VMEM((32, 128), F32), in_scr=pltpu.VMEM((128, 128), F32),
        out_scr=pltpu.VMEM((16, HALF), F32), out_taps=pltpu.VMEM((72, C), F32),
        vec=pltpu.VMEM((32, C), F32), w_in_all=pltpu.VMEM((32, C), F32),
        hidden=pltpu.VMEM((2, rows_all, C), F32), xhat=pltpu.VMEM((6, rows_all, C), F32),
        dact=pltpu.VMEM((6, rows_all, C), F32), rstd=pltpu.VMEM((-(-6 * images // 8) * 8, C), F32),
        col0=pltpu.VMEM((rows_all, KW), BF16), col1=pltpu.VMEM((rows_all, KW), BF16),
        col2=pltpu.VMEM((rows_all, KW), BF16), col3=pltpu.VMEM((rows_all, KW), BF16),
        taps0=pltpu.VMEM((32, rows_all), BF16), rows_scr=pltpu.VMEM((32, rows_all), F32),
        acts=pltpu.VMEM((2, rows_all, C), BF16), q_scr=pltpu.VMEM((rows_all, C), BF16),
        k_scr=pltpu.VMEM((rows_all, C), BF16), v_scr=pltpu.VMEM((rows_all, C), BF16),
        probs=pltpu.VMEM((images, PIX, PIX), F32), mixed=pltpu.VMEM((rows_all, C), BF16),
        gvec=pltpu.VMEM((32, C), F32), gsum=pltpu.VMEM((16, C), F32),
        local=pltpu.VMEM((2, 4 * lr, MAIN), BF16), one=pltpu.VMEM((4 * lr, MAIN), BF16),
        two=pltpu.VMEM((nx, 4 * lr, MAIN), BF16), last=pltpu.VMEM((2, 4 * lr, MAIN), BF16),
        out_local=pltpu.VMEM((2, 8, HALF), F32), out_one=pltpu.VMEM((8, HALF), F32),
        out_two=pltpu.VMEM((nx, 8, HALF), F32), out_last=pltpu.VMEM((2, 8, HALF), F32),
        one_send=dma((chunks + 2,)), one_recv=dma((chunks + 2,)),
        two_send=dma((chunks + 2, wide)), two_recv=dma((chunks + 2, wide)),
        three_send=dma((chunks + 2,)), three_recv=dma((chunks + 2,)),
        tiny=pltpu.VMEM((dp, 16, 128), F32), tiny_send=dma((dp - 1,)), tiny_recv=dma((dp - 1,)),
        tables=pltpu.VMEM((n, SUM_ROWS, 128), F32), sum_send=dma((n - 1,)), sum_recv=dma((n - 1,)),
    )
    scratch.update({name: pltpu.VMEM(dims, F32) for name, dims in made.items()})
    scratch["out_sem"] = dma((40,))
    names = inputs + [name + "_hbm" for name in made] + list(scratch)
    results = pl.pallas_call(
        functools.partial(step_kernel, n, ny, nz, nx, dp, lr, images, names),
        out_shape=tuple(shape(dims) for dims in made.values()),
        in_specs=[smem_spec()] * 3 + [hbm_spec()] * (2 + len(STATE)),
        out_specs=tuple(hbm_spec() for _ in made),
        scratch_shapes=list(scratch.values()),
        compiler_params=pltpu.CompilerParams(
            collective_id=1, has_side_effects=True, vmem_limit_bytes=64 * MIB
        ),
        name="step",
    )(crop_boxes, time_steps, step_count, canvas, noise_field, *state)
    results = dict(zip(made, results))

    outs = {"norms_out": shape((2, 12)), "loss_out": shape((1, 1))}
    for name in PASSED:
        outs[name + "_out"] = shape(made[name])
    for key in ("in", CONV, TMB, ATTN, "out"):
        outs[key + "_new_out"] = shape(made[key + "_update"])
    for key in (CONV, TMB, ATTN):
        outs[key + "_low_out"] = shape(made[key + "_update"], BF16)
    held = {name + HERE: pltpu.VMEM(own[name].shape, F32) for name in WEIGHTS}
    held.update({name + HERE: pltpu.VMEM(made[name], F32) for name in UPDATES + PASSED})
    held["norms_here"] = pltpu.VMEM((2, 12), F32)
    held["norms_in"] = pltpu.VMEM((SUM_ROWS, 128), F32)
    for key in ("in", CONV, TMB, ATTN, "out"):
        held[key + HERE] = pltpu.VMEM(made[key + "_update"], F32)
    for key in (CONV, TMB, ATTN):
        held[key + "_low_here"] = pltpu.VMEM(made[key + "_update"], BF16)
    held["sem"] = dma((80,))
    inputs = ["norms"] + list(WEIGHTS) + list(UPDATES) + list(PASSED)
    names = inputs + list(outs) + list(held)
    updated = pl.pallas_call(
        functools.partial(update_kernel, names),
        out_shape=tuple(outs.values()),
        in_specs=[hbm_spec()] * len(inputs),
        out_specs=tuple(vmem_spec() if name == "loss_out" else hbm_spec() for name in outs),
        scratch_shapes=list(held.values()),
        compiler_params=pltpu.CompilerParams(vmem_limit_bytes=64 * MIB),
        name="update",
    )(results["norms"], *[own[name] for name in WEIGHTS], *[results[name] for name in UPDATES + PASSED])
    done = dict(zip(outs, updated))
    final = [done["loss_out"].reshape(()), done["norms_out"].T]
    for key in ("in", CONV, TMB, ATTN, "out"):
        final += [done[key + "_new_out"], done[key + "_first_out"], done[key + "_second_out"]]
        if key + "_low_out" in done:
            final.append(done[key + "_low_out"])
    final += [done["vec_new_out"], done["vec_first_out"], done["vec_second_out"], done["attn_grad_out"]]
    return tuple(final)


def solution(mesh):
    chan_row = P("chan", None)
    chan_mid = P(None, "chan", None)
    chan_vec = P(None, "chan")
    return jax.shard_map(
        functools.partial(per_device, mesh.shape["chan"], mesh.shape["dp"]),
        mesh=mesh,
        in_specs=(P("dp", None, None, None), P("dp", None), P("dp"), P(None, "dp", None), P())
        + (chan_row,) * 3 + (chan_mid,) * 9 + (P(),) * 3 + (chan_vec,) * 3,
        out_specs=(P(), P()) + (chan_row,) * 3 + (chan_mid,) * 12 + (P(),) * 3 + (chan_vec,) * 3 + (chan_mid,),
        check_vma=False,
    )
```

time: 118 us -> 81 us (0.69)
  Pallas kernels: 101 us -> 79.3 us
  local copies, waits for them, and re-layouts: 12.6 us -> 0 us
  other arithmetic: 1.55 us -> 0 us
    pallas_call x5 -> x2, Pallas kernels: 101 us -> 79.3 us  [the longest x1 73.7 us: per_device(): pl.pallas_call(functools.partial(step_kernel, n, ny, nz, nx, dp, lr, imag...]
    unnamed x69 -> x0, local copies, waits for them, and re-layouts: 12.1 us -> none
where the time goes in v3:
time: 81 us; the launch traced here: 80.8 us
  Pallas kernels  79.3 us (98%)
  between operations  1.48 us (2%)
    pallas_call x1, Pallas kernels, per_device(): pl.pallas_call(functools.partial(step_kernel, n, ny, nz, nx, dp, lr, imag...  73.7 us
    pallas_call x1, Pallas kernels, per_device(): pl.pallas_call(functools.partial(update_kernel, names), out_shape=tuple(o...  5.62 us

profile of v3, /device:TPU:0, one launch (start us, length us, event | category | flops | bytes accessed | tf_op | source)
XLA Modules:
  0.0 80.8 jit_solution(9503404782958155372)
XLA Ops:
  1.3 73.7 %step.1 = (f32[32,27]{1,0:T(8,128)}, f32[32,27]{1,0:T(8,128)}, f32[32,27]{1,0:T(8,128)}, f32[4,32,2304]{2,1,0:T(8,128)}, f32[4,32,2304]{2,1,0:T(8,128)}, /*index...) custom-call(s32[2,3]{1,0:T(2,128)} %refs_0_.1, ...), custom_call_target="tpu_custom_call" | custom-call | tf_op jit(solution)/shard_map/step/pallas_call | solution.py:1035
  75.0 5.6 %update.1 = (f32[2,12]{1,0:T(2,128)}, f32[1,1]{1,0:T(1,128)}, f32[32,27]{1,0:T(8,128)}, f32[32,27]{1,0:T(8,128)}, f32[4,32,2304]{2,1,0:T(8,128)}, /*index=5*/f32...) custom-call(f32[16,128]{1,0:T(8,128)} %get-tuple-element.68.refs_0_,, ...), custom_call_target="tpu_custom_call" | custom-call | tf_op jit(solution)/shard_map/update/pallas_call | solution.py:1066

commit v4 on v3

--- a/solution.py
+++ b/solution.py
@@ -32,8 +32,18 @@
 TN = (((0,), (0,)), ((), ()))
 MIB = 1024 * 1024
 
-XL = (3, 3, 3, 4)
-DELAYS = (2, 5, 2)
+GROWS = 32
+XBIG = 4
+XLAST = 2
+XTAIL = 1
+LEAD = 1
+EARLY = 2
+IMAGE = 3
+LAG_B = 1
+LAG_Z = 1.0
+LAG_X = 1
+LAG_Y = 1
+DELAYS = (2, 7, 2)
 VEC_ROWS = 22
 LOSS_ROW = 24
 MAIN = HALF + 128 + 128
@@ -163,7 +173,18 @@
     offsets = [(i, j) for i in range(nz) for j in range(ny)][1:]
     place = {o: i for i, o in enumerate(offsets)}
 
+    line = False
+    inner = ((z + 1) // 2) % 2
+
+    def z_at(i):
+        if line and i >= 2:
+            return inner * flip(z, 5 - i) + (1 - inner) * flip(z, i)
+        return flip(z, i)
+
     def chan_at(o):
+        return z_at(o[0]) * ny + flip(y, o[1])
+
+    def pair_at(o):
         return flip(z, o[0]) * ny + flip(y, o[1])
 
     def next_part(k):
@@ -177,16 +198,18 @@
 
     core_lanes = KW // 2
     use_x = nx == 2
-    chunk_rows = max(lr, 16)
-    conv_chunks = 4 * lr // chunk_rows
+    sum_rows = max(lr, 16)
+    sum_chunks = 4 * lr // sum_rows
+    gather_rows = min(GROWS, sum_rows)
+    conv_chunks = 4 * lr // gather_rows
     chunks = list(range(conv_chunks))
     chunks.insert((conv_chunks + 1) // 2, None)
 
     def x_lanes(chunk):
-        return (XL[chunk % 4]) * 128 if use_x else 0
+        return (XLAST if chunk >= conv_chunks - XTAIL else XBIG) * 128 if use_x else 0
 
     def rows_of(chunk):
-        return pl.ds(chunk * chunk_rows, chunk_rows)
+        return pl.ds(chunk * gather_rows, gather_rows)
 
     attn_x = lr // 2 if use_x and lr >= 32 else 0
 
@@ -229,17 +252,45 @@
         ref = near_ref(chunk, src, core) if piece == 0 else x_ref(chunk, src, core, 1 - x)
         send(ref, ref, r.core_send.at[piece, i, place[o]], r.core_recv.at[piece, i, place[o]], sibling)
 
-    def begin(chunk):
-        for i in range(1, nz):
-            send_near(chunk, me, (i, 0), (part, chan_at((i, 0))))
+    def pass_on(chunk, src, slot, target):
+        i = index(chunk)
+
+        @pl.when(inner == 1)
+        def _():
+            ref = near_ref(chunk, src, core)
+            remote(ref, ref, r.pass_send.at[i, slot[0]], r.near_recv.at[i, place[(slot[1], 0)]], (part, target)).start()
+
+    def passed(chunk):
+        i = index(chunk)
+
+        @pl.when(inner == 1)
+        def _():
+            for slot in range(4):
+                ref = near_ref(chunk, me, core)
+                remote(ref, ref, r.pass_send.at[i, slot], r.near_recv.at[i, 0], (part, me)).wait_send()
+
+    def begin_y(chunk):
         for j in range(1, ny):
             send_near(chunk, me, (0, j), (part, chan_at((0, j))))
+
+    def begin(chunk):
+        send_near(chunk, me, (1, 0), (part, chan_at((1, 0))))
+        if line:
+            pass_on(chunk, me, (0, 2), flip(z, 3) * ny + y)
+        else:
+            for i in range(2, nz):
+                send_near(chunk, me, (i, 0), (part, chan_at((i, 0))))
 
     def near_in(chunk, o):
         i = index(chunk)
         src = chan_at(o)
         ref = near_ref(chunk, src, core)
         remote(ref, ref, r.near_send.at[i, place[o]], r.near_recv.at[i, place[o]], (part, src)).wait_recv()
+        if line and o[1] == 0:
+            if o[0] == 1:
+                pass_on(chunk, src, (1, 3), flip(z, 3) * ny + y)
+            else:
+                pass_on(chunk, src, o[:1] * 2, flip(z, 1) * ny + y)
         if o[1] == 0:
             for j in range(1, ny):
                 send_near(chunk, src, (o[0], j), (part, chan_at((0, j))))
@@ -265,39 +316,38 @@
         for piece, ref in enumerate(pieces):
             remote(ref, ref, r.core_send.at[piece, i, place[o]], r.core_recv.at[piece, i, place[o]], sibling).wait_recv()
 
-    def stage_one(chunk):
+    events = []
+    for c, chunk in enumerate(chunks):
+        if c >= 1:
+            events.append((c - LEAD, -1, begin, (chunk,)))
         for i in range(1, nz):
-            near_in(chunk, (i, 0))
-
-    def stage_two(chunk):
+            seen = c + LAG_B + i / (nz - 1) - 0.3
+            events.append((seen, c, near_in, (chunk, (i, 0))))
+            events.append((seen + LAG_X, c, x_in, (chunk, (i, 0))))
+            for j in range(1, ny):
+                events.append((seen + LAG_Y, c, near_in, (chunk, (i, j))))
+                events.append((seen + LAG_Y + LAG_X, c, x_in, (chunk, (i, j))))
         for j in range(1, ny):
-            near_in(chunk, (0, j))
-        for i in range(1, nz):
-            for j in range(1, ny):
-                near_in(chunk, (i, j))
-
-    def stage_three(chunk):
-        for o in offsets:
-            x_in(chunk, o)
-
-    def stage_four(chunk):
-        for o in offsets:
-            core_in(chunk, o)
-
-    turn = [0]
-
-    def gather_turn():
-        i = turn[0]
-        turn[0] += 1
-        for stage, delay in ((stage_one, 0), (stage_two, 1), (stage_three, 2), (stage_four, 3)):
-            if 0 <= i - delay < len(chunks):
-                stage(chunks[i - delay])
-            if delay == 0 and 2 <= i + 2 < len(chunks):
-                begin(chunks[i + 2])
-
-    def arrived(chunk):
-        while turn[0] < chunks.index(chunk) + 4:
-            gather_turn()
+            events.append((LAG_B + c * 0.7, c, near_in, (chunk, (0, j))))
+            events.append((LAG_B + c * 0.7 + LAG_X, c, x_in, (chunk, (0, j))))
+    events.sort(key=lambda event: event[0])
+    here = set()
+
+    def until(time):
+        while events and events[0][0] <= time:
+            event = events.pop(0)
+            event[2](*event[3])
+
+    def arrived(*wanted):
+        for chunk in wanted:
+            if chunk not in here:
+                here.add(chunk)
+                until(max([event[0] for event in events if event[1] == chunks.index(chunk)], default=0))
+                for o in offsets:
+                    core_in(chunk, o)
+
+    def conv_here(k):
+        arrived(*range(k * lr // gather_rows, ((k + 1) * lr - 1) // gather_rows + 1))
 
     order = tap_order()
     r.order[...] = order
@@ -329,11 +379,12 @@
         wave = jnp.where(steps_row < images, wave / (1.0 + jnp.exp(-wave)), 0.0)
         r.temb_act[:, i * C:(i + 1) * C] = wave.astype(BF16)
 
+    prepare((0, 1))
     pl.semaphore_wait(barrier, n + dp - 2)
-    prepare((0, 1))
     begin(chunks[0])
-    if conv_chunks > 2:
-        begin(chunks[1])
+    half = [chunk for chunk in chunks[:len(chunks) // 2] if chunk is not None]
+    for chunk in half:
+        begin_y(chunk)
 
     loads["vectors"].wait()
     loads[W_IN].wait()
@@ -363,7 +414,7 @@
     r.counts[part] = jnp.full((8, 128), total, jnp.int32).astype(F32)
     for o in offsets:
         i = place[o]
-        send(r.smalls.at[me], r.smalls.at[me], r.small_send.at[i], r.small_recv.at[i], (part, chan_at(o)))
+        send(r.smalls.at[me], r.smalls.at[me], r.small_send.at[i], r.small_recv.at[i], (part, pair_at(o)))
     for i in range(1, dp):
         send(r.counts.at[part], r.counts.at[part], r.count_send.at[i - 1], r.count_recv.at[i - 1], (next_part(i), me))
 
@@ -380,8 +431,10 @@
             r.out_taps[tap * 8:tap * 8 + 8, h * 128:(h + 1) * 128] = out_mixed[
                 h * 8:h * 8 + 8, tap * 128:(tap + 1) * 128
             ]
-    if conv_chunks <= 2:
-        begin(chunks[1])
+    for chunk in chunks:
+        if chunk not in half:
+            begin_y(chunk)
+    until(EARLY)
 
     lane = iota((1, PIX), 1)
     pix_x, pix_y = lane & (HW - 1), lane >> 4
@@ -425,10 +478,10 @@
             r.rows_scr[colour * TAPS + tap:colour * TAPS + tap + 1, :] = moved[colour:colour + 1]
     r.taps0[...] = r.rows_scr[...].astype(BF16)
 
-    gather_turn()
+    until(IMAGE)
 
     for o in offsets:
-        src = chan_at(o)
+        src = pair_at(o)
         remote(r.smalls.at[src], r.smalls.at[src], r.small_send.at[place[o]], r.small_recv.at[place[o]],
                (part, src)).wait_recv()
     for i in range(1, dp):
@@ -501,17 +554,17 @@
         return jnp.concatenate([value[span(b)] + vrow(first + b) for b in range(images)], axis=0)
 
     def chunk_of(k):
-        return k * lr // chunk_rows
+        return k * lr // sum_rows
 
     def block_fwd(block, source, target):
         norm_fwd(3 * block, hidden[source], vrow(3 * block), vrow(6 + 3 * block),
                  functools.partial(store_cols, cols[2 * block]))
-        arrived(chunk_of(2 * block))
+        conv_here(2 * block)
         middle = dot(cols[2 * block][...], conv_weight(2 * block), NT)
         middle = add_rows(middle, VEC_ROWS + block * images)
         norm_fwd(3 * block + 1, middle, vrow(3 * block + 1), vrow(7 + 3 * block),
                  functools.partial(store_cols, cols[2 * block + 1]))
-        arrived(chunk_of(2 * block + 1))
+        conv_here(2 * block + 1)
         branch = dot(cols[2 * block + 1][...], conv_weight(2 * block + 1), NT)
         hidden[target] = hidden[source] + (branch + vrow(14 + 2 * block))
 
@@ -561,12 +614,12 @@
             return slice(0, 4 * lr), lanes_attn
         if chunk == TMB:
             return slice(0, 4 * lr), lanes_temb
-        return slice(chunk * chunk_rows, (chunk + 1) * chunk_rows), slice(0, HALF)
+        return slice(chunk * sum_rows, (chunk + 1) * sum_rows), slice(0, HALF)
 
     def family(chunk):
         if chunk == "out":
-            return (r.out_local, r.out_one, r.out_two, r.out_last), (slice(None), slice(None)), conv_chunks + 2
-        i = conv_chunks + (ATTN, TMB).index(chunk) if isinstance(chunk, str) else chunk
+            return (r.out_local, r.out_one, r.out_two, r.out_last), (slice(None), slice(None)), sum_chunks + 2
+        i = sum_chunks + (ATTN, TMB).index(chunk) if isinstance(chunk, str) else chunk
         return (r.local, r.one, r.two, r.last), region(chunk), i
 
     def view(ref, i, where):
@@ -672,7 +725,7 @@
                 r.local[h, k * lr:(k + 1) * lr, tap * 128:(tap + 1) * 128] = own[
                     :, tap * C + h * 128:tap * C + h * 128 + 128
                 ].astype(BF16)
-        if k * lr % chunk_rows == 0:
+        if k * lr % sum_rows == 0:
             ready(chunk_of(k))
         tick()
         parts = dot(low, conv_weight(k), NN)
@@ -821,32 +874,49 @@
     def conv_steps(which, natural):
         for number, name, k, lanes, h, rows, held in matrix_parts(lr):
             if name == CONV and chunk_of(k) in which:
-                top = h * len(which) * chunk_rows + k * lr - min(which) * chunk_rows
+                top = h * len(which) * sum_rows + k * lr - min(which) * sum_rows
                 lamb(number, name, (k, every, lanes), natural[top:top + lr])
                 if h == 1:
                     put_all(CONV, k)
 
-    early = list(range(1, conv_chunks))
-    for chunk in early + [ATTN, TMB, "out"]:
+    def push(chunk, stage):
+        for item in [item for item in due if item[1][1] == chunk]:
+            while item is not None and item[1][0] <= stage:
+                due.remove(item)
+                run_due(item[1])
+                item = next((left for left in due if left[1][1] == chunk), None)
+
+    def whole_parts(which):
+        for number, name, k, lanes, h, rows, held in matrix_parts(lr):
+            if name == which:
+                value = r.last[h, rows, held].astype(F32)
+                if name == ATTN:
+                    r.attn_grad[k, :, lanes] = value
+                lamb(number, name, (k, every, lanes), value)
+        put_all(which)
+
+    early = list(range(1, sum_chunks))
+    for chunk in early + ["out"]:
         finish(chunk)
-    stack = [r.last[h, chunk_rows:4 * lr, 0:HALF] for h in range(2)]
+    push(0, 2)
+    push(TMB, 2)
+    stack = [r.last[h, sum_rows:4 * lr, 0:HALF] for h in range(2)]
     stack += [jnp.concatenate([r.out_last[h], jnp.zeros((8, HALF), F32)], axis=0).astype(BF16) for h in range(2)]
     natural = dot(jnp.concatenate(stack, axis=0), r.order[...], NT)
+    finish(ATTN)
+    whole_parts(ATTN)
+    put("attn_grad")
+    push(TMB, 3)
+    push(0, 3)
     conv_steps(early, natural)
-    top = 2 * (4 * lr - chunk_rows)
+    top = 2 * (4 * lr - sum_rows)
     for h in range(2):
         lamb(11, "out", (every, slice(h * HALF, (h + 1) * HALF)), natural[top + h * 16:top + h * 16 + 3])
-    for number, name, k, lanes, h, rows, held in matrix_parts(lr):
-        if name != CONV:
-            value = r.last[h, rows, held].astype(F32)
-            if name == ATTN:
-                r.attn_grad[k, :, lanes] = value
-            lamb(number, name, (k, every, lanes), value)
-    for name in ("out", TMB, ATTN):
-        put_all(name)
-    put("attn_grad")
+    put_all("out")
+    finish(TMB)
+    whole_parts(TMB)
     finish()
-    natural = dot(jnp.concatenate([r.last[h, 0:chunk_rows, 0:HALF] for h in range(2)], axis=0), r.order[...], NT)
+    natural = dot(jnp.concatenate([r.last[h, 0:sum_rows, 0:HALF] for h in range(2)], axis=0), r.order[...], NT)
     conv_steps([0], natural)
 
     for i in range(1, dp):
@@ -873,7 +943,7 @@
     r.tables[me] = table
     for o in offsets:
         i = place[o]
-        send(r.tables.at[me], r.tables.at[me], r.sum_send.at[i], r.sum_recv.at[i], (part, chan_at(o)))
+        send(r.tables.at[me], r.tables.at[me], r.sum_send.at[i], r.sum_recv.at[i], (part, pair_at(o)))
     first, second, direction = adapt(r.own_rows[0:VEC_ROWS, 0:lr], r.vec_m[...], r.vec_v[...])
     r.vec_new[...] = r.vectors[...] - RATE * direction
     r.vec_first[...] = first
@@ -881,7 +951,7 @@
     for name in ("vec_new", "vec_first", "vec_second"):
         put(name)
     for o in offsets:
-        src = chan_at(o)
+        src = pair_at(o)
         remote(r.tables.at[src], r.tables.at[src], r.sum_send.at[place[o]], r.sum_recv.at[place[o]],
                (part, src)).wait_recv()
     total = r.tables[0]
@@ -892,6 +962,9 @@
     total = jnp.where((row == 12) & (lane == 0), r.own_rows[LOSS_ROW:LOSS_ROW + 1, 0:1], total)
     r.norms[...] = total
     put("norms")
+    if line:
+        for chunk in chunks:
+            passed(chunk)
     for copy in sends:
         copy.wait_send()
     for copy in outward:
@@ -982,8 +1055,7 @@
     ny = 1 << ((n.bit_length() - 2) // 2)
     nz = n // ny
     dma = pltpu.SemaphoreType.DMA
-    chunk_rows = max(lr, 16)
-    chunks = 4 * lr // chunk_rows + 1
+    chunks = 4 * lr // min(GROWS, max(lr, 16)) + 1
 
     made = {}
     for key, name in (("in", W_IN), (CONV, "conv_w"), (TMB, "temb_w"), (ATTN, "attn_w"), ("out", "out_w")):
@@ -1002,7 +1074,7 @@
         load_sem=dma((len(STATE) + 2,)), conv_sem=dma((4,)),
         whole=pltpu.VMEM((n, 4 * lr, KW), BF16), attn_all=pltpu.VMEM((n, 4 * lr, C), BF16),
         smalls=pltpu.VMEM((n, 16, 128), F32), counts=pltpu.VMEM((dp, 8, 128), F32),
-        near_send=dma((chunks, n - 1)), near_recv=dma((chunks, n - 1)),
+        near_send=dma((chunks, n - 1)), pass_send=dma((chunks, 4)), near_recv=dma((chunks, n - 1)),
         x_send=dma((chunks, n - 1)), x_recv=dma((chunks, n - 1)),
         core_send=dma((2, chunks, n - 1)), core_recv=dma((2, chunks, n - 1)),
         small_send=dma((n - 1,)), small_recv=dma((n - 1,)), count_send=dma((dp - 1,)), count_recv=dma((dp - 1,)),

time: 81 us -> 77.4 us (0.956)
  Pallas kernels: 79.3 us -> 75.7 us
    pallas_call x1, Pallas kernels: 73.7 us -> 70 us  [per_device(): pl.pallas_call(functools.partial(step_kernel, n, ny, nz, nx, dp, lr, imag...]
where the time goes in v4:
time: 77.4 us; the launch traced here: 77.1 us
  Pallas kernels  75.7 us (98%)
  between operations  1.48 us (2%)
    pallas_call x1, Pallas kernels, per_device(): pl.pallas_call(functools.partial(step_kernel, n, ny, nz, nx, dp, lr, imag...  70 us
    pallas_call x1, Pallas kernels, per_device(): pl.pallas_call(functools.partial(update_kernel, names), out_shape=tuple(o...  5.62 us

profile of v4, /device:TPU:0, one launch (start us, length us, event | category | flops | bytes accessed | tf_op | source)
XLA Modules:
  0.0 77.1 jit_solution(1223400340450028023)
XLA Ops:
  1.3 70.0 %step.1 = (f32[32,27]{1,0:T(8,128)}, f32[32,27]{1,0:T(8,128)}, f32[32,27]{1,0:T(8,128)}, f32[4,32,2304]{2,1,0:T(8,128)}, f32[4,32,2304]{2,1,0:T(8,128)}, /*index...) custom-call(s32[2,3]{1,0:T(2,128)} %refs_0_.1, ...), custom_call_target="tpu_custom_call" | custom-call | tf_op jit(solution)/shard_map/step/pallas_call | solution.py:1107
  71.4 5.6 %update.1 = (f32[2,12]{1,0:T(2,128)}, f32[1,1]{1,0:T(1,128)}, f32[32,27]{1,0:T(8,128)}, f32[32,27]{1,0:T(8,128)}, f32[4,32,2304]{2,1,0:T(8,128)}, /*index=5*/f32...) custom-call(f32[16,128]{1,0:T(8,128)} %get-tuple-element.68.refs_0_,, ...), custom_call_target="tpu_custom_call" | custom-call | tf_op jit(solution)/shard_map/update/pallas_call | solution.py:1138

commit v5 on v4

--- a/solution.py
+++ b/solution.py
@@ -34,7 +34,7 @@
 
 GROWS = 32
 XBIG = 4
-XLAST = 2
+XLAST = 3
 XTAIL = 1
 LEAD = 1
 EARLY = 2
@@ -950,6 +950,12 @@
     r.vec_second[...] = second
     for name in ("vec_new", "vec_first", "vec_second"):
         put(name)
+    for copy in sends[:-len(offsets)]:
+        copy.wait_send()
+    del sends[:-len(offsets)]
+    if line:
+        for chunk in chunks:
+            passed(chunk)
     for o in offsets:
         src = pair_at(o)
         remote(r.tables.at[src], r.tables.at[src], r.sum_send.at[place[o]], r.sum_recv.at[place[o]],
@@ -962,9 +968,6 @@
     total = jnp.where((row == 12) & (lane == 0), r.own_rows[LOSS_ROW:LOSS_ROW + 1, 0:1], total)
     r.norms[...] = total
     put("norms")
-    if line:
-        for chunk in chunks:
-            passed(chunk)
     for copy in sends:
         copy.wait_send()
     for copy in outward:

time: 77.4 us -> 77 us (level)
  no operation moved by 1% of the time
where the time goes in v5:
time: 77 us; the launch traced here: 76.8 us
  Pallas kernels  75.3 us (98%)
  between operations  1.48 us (2%)
    pallas_call x1, Pallas kernels, per_device(): pl.pallas_call(functools.partial(step_kernel, n, ny, nz, nx, dp, lr, imag...  69.7 us
    pallas_call x1, Pallas kernels, per_device(): pl.pallas_call(functools.partial(update_kernel, names), out_shape=tuple(o...  5.62 us

profile of v5, /device:TPU:0, one launch (start us, length us, event | category | flops | bytes accessed | tf_op | source)
XLA Modules:
  0.0 76.8 jit_solution(15414752645796428792)
XLA Ops:
  1.3 69.7 %step.1 = (f32[32,27]{1,0:T(8,128)}, f32[32,27]{1,0:T(8,128)}, f32[32,27]{1,0:T(8,128)}, f32[4,32,2304]{2,1,0:T(8,128)}, f32[4,32,2304]{2,1,0:T(8,128)}, /*index...) custom-call(s32[2,3]{1,0:T(2,128)} %refs_0_.1, ...), custom_call_target="tpu_custom_call" | custom-call | tf_op jit(solution)/shard_map/step/pallas_call | solution.py:1110
  71.0 5.6 %update.1 = (f32[2,12]{1,0:T(2,128)}, f32[1,1]{1,0:T(1,128)}, f32[32,27]{1,0:T(8,128)}, f32[32,27]{1,0:T(8,128)}, f32[4,32,2304]{2,1,0:T(8,128)}, /*index=5*/f32...) custom-call(f32[16,128]{1,0:T(8,128)} %get-tuple-element.68.refs_0_,, ...), custom_call_target="tpu_custom_call" | custom-call | tf_op jit(solution)/shard_map/update/pallas_call | solution.py:1141
